TPU v7x, 32 devices: a whole 2x2x4 slice. The times are simulated.
32 devices in a mesh: group: 2 (over y), ctx: 4 (over z), chan: 2 (over x), sub: 2 (over core).
Axes of the slice: x: 2, y: 2, z: 4, core: 2. Of those that a mesh axis runs over, the one named last changes fastest.
Arguments:
- q_proj: bfloat16 [2048, 4096], P(('group', 'ctx'), ('chan', 'sub')), parts along dimension 0, may hold values from -6 to 6
- k_proj: bfloat16 [2048, 4096], P(('group', 'ctx'), ('chan', 'sub')), parts along dimension 0, may hold values from -6 to 6
- v_proj: bfloat16 [2048, 4096], P(('group', 'ctx'), ('chan', 'sub')), parts along dimension 0, may hold values from -6 to 6
- filters: float32 [32, 512], P(('chan', 'sub')), may hold values from -0.375 to 0.375
- filter_blocks: int32 [32], P(('chan', 'sub')), may hold values from 1 to 2, as said below
- out_weight: bfloat16 [4096, 4096], P('ctx', ('chan', 'sub')), may hold values from -0.09375 to 0.09375
Outputs:
- mixed: bfloat16 [2048, 4096], P(('group', 'ctx'), ('chan', 'sub')), parts along dimension 0
There are 2 independent parts, one for each index of `group`. A program takes and returns all parts, laid end to end along the dimension named above; an argument that names none is the same for every part. Nothing has to cross between parts.
Inputs may be any that keep to these rules, and one draw needn't show every extreme that they name: `filter_blocks`: some group has exactly the largest length.
All inputs are finite; a program needn't handle non-finite values.
Results may differ from a plain program's by a relative error of at most 0.0095.
Values may be sent and summed in bfloat16 or wider, within the bound.
No kernel may reach another device: no remote copies, remote signals or barrier semaphores. Data moves between devices by JAX's collectives and lax.ppermute only.
A program may use at most 64 MiB of HBM per device.

v0:
```python
import math

import jax
import jax.numpy as jnp
from jax import lax
from jax.sharding import PartitionSpec as P


def shifted(value, axis, steps):
    count = lax.axis_size(axis)
    leading, last = (max(0, -steps), min(count, count - steps))
    return lax.ppermute(value, axis, [(source, source + steps) for source in range(leading, last)])


def forward_table(block_len, columns):
    length = 2 * block_len
    frequency = jnp.arange(block_len, dtype=jnp.int32)[:, None]
    positions = jnp.arange(columns, dtype=jnp.int32)[None, :]
    angles = (frequency * positions % length).astype(jnp.float32) * (2.0 * math.pi / length)
    alternating = (1 - 2 * (positions % 2)).astype(jnp.float32)
    upper = jnp.cos(angles)
    bottom = jnp.where(frequency == 0, alternating, -jnp.sin(angles))
    return jnp.concatenate([upper, bottom], axis=0)


def inverse_table(block_len):
    length = 2 * block_len
    samples = jnp.arange(block_len, dtype=jnp.int32)[:, None]
    frequency = jnp.arange(block_len, dtype=jnp.int32)[None, :]
    angles = (frequency * samples % length).astype(jnp.float32) * (2.0 * math.pi / length)
    alternating = (1 - 2 * (samples % 2)).astype(jnp.float32)
    left_half = jnp.where(frequency == 0, 1.0, 2.0 * jnp.cos(angles)) / length
    right_half = jnp.where(frequency == 0, alternating, -2.0 * jnp.sin(angles)) / length
    return jnp.concatenate([left_half, right_half], axis=1)


def packed_product(filter_spec, data_spec, first_row, block_len):
    filt_re = filter_spec[:block_len]
    filt_im = filter_spec[block_len:]
    data_re = data_spec[:block_len]
    data_im = data_spec[block_len:]
    other_rows = 1.0 - first_row
    upper = filt_re * data_re - filt_im * data_im * other_rows
    bottom = (filt_re * data_im + filt_im * data_re) * other_rows + filt_im * data_im * first_row
    return jnp.concatenate([upper, bottom], axis=0)


def per_device(q_proj, k_proj, v_proj, filters, filter_blocks, out_weight):
    block_len, channels = q_proj.shape
    groups = filters.shape[0]
    per_group = channels // groups
    reach = lax.axis_size("ctx") // 2
    highest = lax.Precision.HIGHEST
    product = (k_proj.astype(jnp.float32) * v_proj.astype(jnp.float32)).astype(jnp.bfloat16)
    tap_index = jnp.arange(filters.shape[1], dtype=jnp.int32)
    masked = jnp.where(tap_index[None, :] < filter_blocks[:, None] * block_len, filters, 0.0)
    tap_blocks = masked.reshape(groups, reach, block_len)
    empty_block = jnp.zeros((groups, 1, block_len), jnp.float32)
    extended = jnp.concatenate([empty_block, tap_blocks, empty_block], axis=1)
    segments = jnp.concatenate([extended[:, 1:], extended[:, :-1]], axis=2)
    full_table = forward_table(block_len, 2 * block_len)
    filter_spectra = jnp.einsum("gdm,fm->dfg", segments, full_table, precision=highest)
    half_table = forward_table(block_len, block_len)
    table_high = half_table.astype(jnp.bfloat16)
    table_low = (half_table - table_high.astype(jnp.float32)).astype(jnp.bfloat16)
    first_row = (jnp.arange(block_len) == 0).astype(jnp.float32)[:, None, None]
    longest = jnp.max(filter_blocks)
    position = lax.axis_index("ctx")

    def transform(block):
        spectrum = jnp.dot(table_high, block, preferred_element_type=jnp.float32)
        spectrum = spectrum + jnp.dot(table_low, block, preferred_element_type=jnp.float32)
        return spectrum.reshape(2 * block_len, groups, per_group)

    def contribution(running, block, distance):
        filter_spec = lax.dynamic_index_in_dim(filter_spectra, distance, 0, keepdims=False)[
            :, :, None
        ]

        def add_term(partial_sum):
            return partial_sum + packed_product(filter_spec, transform(block), first_row, block_len)

        needed = (distance <= longest) & (position >= distance)
        return lax.cond(needed, add_term, lambda partial_sum: partial_sum, running)

    running = packed_product(
        filter_spectra[0][:, :, None], transform(product), first_row, block_len
    )

    def relay_step(distance, carry):
        carried, partial_sum = carry
        carried = shifted(carried, "ctx", 1)
        return (carried, contribution(partial_sum, carried, distance))

    carried, running = lax.fori_loop(1, reach + 1, relay_step, (product, running))
    spectrum_sum = running.reshape(2 * block_len, channels)
    conv = jnp.dot(inverse_table(block_len), spectrum_sum, precision=highest)
    gated = (q_proj.astype(jnp.float32) * conv).astype(jnp.bfloat16)
    all_gated = lax.all_gather(gated, ("chan", "sub"), axis=1, tiled=True)
    mixed = jnp.dot(
        all_gated,
        lax.all_gather(out_weight, "ctx", axis=0, tiled=True),
        preferred_element_type=jnp.float32,
    )
    return mixed.astype(jnp.bfloat16)


def solution(mesh):
    in_specs = (
        P(("group", "ctx"), ("chan", "sub")),
        P(("group", "ctx"), ("chan", "sub")),
        P(("group", "ctx"), ("chan", "sub")),
        P(("chan", "sub"), None),
        P(("chan", "sub")),
        P("ctx", ("chan", "sub")),
    )
    out_specs = P(("group", "ctx"), ("chan", "sub"))
    return jax.shard_map(
        per_device, mesh=mesh, in_specs=in_specs, out_specs=out_specs, check_vma=False
    )
```

profile of v0, /device:TPU:0, one launch (start us, length us, event | category | flops | bytes accessed | tf_op | source)
XLA Modules:
  0.0 255.5 jit_solution(7464042446267970455)
XLA Ops:
  6.6 1.0 fusion.39
  7.6 1.9 select_multiply_fusion
  9.6 2.1 negate_select_fusion.2
  11.7 0.7 fusion.62
  12.5 1.0 convolution_bitcast_fusion
  13.5 1.2 copy.9
  14.9 0.4 fusion.60
  15.3 0.3 copy-done
  15.7 0.4 convolution_add_fusion.1
  16.1 0.2 slice_bitcast_fusion.3
  16.4 0.2 copy.12
  17.0 1.5 fusion.18
  18.6 37.8 %while.20 = (s32[]{:T(128)}, bf16[256,1024]{1,0:T(8,128)(2,1)}, f32[512,8,128]{2,1,0:T(8,128)S(1)}, s32[]{:T(128)}, s32[]{:T(128)}, /*index=5*/f32[3,512,8]{2,1,...) while((s32[]{:T(128)}, bf16[256,1024]{1,0:T(8,128)(2,1)}, ...), condition=%wide.region_4.5_spmd.clone.clone, body=%wide.region_1.4_spmd.clone.clone.sunk | while | flops 541066240 | bytes 29942052 | solution.py:95
  18.7 5.0 %collective-permute-start = (bf16[256,1024]{1,0:T(8,128)(2,1)}, bf16[256,1024]{1,0:T(8,128)(2,1)S(1)}, u32[]{:S(2)}, u32[]{:S(2)}) collective-permute-start(bf16[256,1024]{1,0:T(8,128)(2,1)} %get-tuple-element.393), channel_id=1, source_target_pairs={{0,4},{4,8},{8,12},{1,5},{5,9},{9,13},{2,6},{6,10},{10,14},{3,7},{... | collective-permute-start | bytes 1572872 | tf_op jit(solution)/shard_map/while/body/eval_jaxpr/ppermute | solution.py:12
  24.3 10.8 %collective-permute-done = bf16[256,1024]{1,0:T(8,128)(2,1)S(1)} collective-permute-done((bf16[256,1024]{1,0:T(8,128)(2,1)}, bf16[256,1024]{1,0:T(8,128)(2,1)S(1)}, u32[]{:S(2)}, u32[]{:S(2)}) %collective-permute-start) | collective-permute-done | bytes 524320 | tf_op jit(solution)/shard_map/while/body/eval_jaxpr/ppermute | solution.py:12
  35.1 0.8 copy.32
  35.9 9.2 %collective-permute-start = (bf16[256,1024]{1,0:T(8,128)(2,1)}, bf16[256,1024]{1,0:T(8,128)(2,1)S(1)}, u32[]{:S(2)}, u32[]{:S(2)}) collective-permute-start(bf16[256,1024]{1,0:T(8,128)(2,1)} %get-tuple-element.393), channel_id=1, source_target_pairs={{0,4},{4,8},{8,12},{1,5},{5,9},{9,13},{2,6},{6,10},{10,14},{3,7},{... | collective-permute-start | bytes 1572872 | tf_op jit(solution)/shard_map/while/body/eval_jaxpr/ppermute | solution.py:12
  45.8 9.9 %collective-permute-done = bf16[256,1024]{1,0:T(8,128)(2,1)S(1)} collective-permute-done((bf16[256,1024]{1,0:T(8,128)(2,1)}, bf16[256,1024]{1,0:T(8,128)(2,1)S(1)}, u32[]{:S(2)}, u32[]{:S(2)}) %collective-permute-start) | collective-permute-done | bytes 524320 | tf_op jit(solution)/shard_map/while/body/eval_jaxpr/ppermute | solution.py:12
  55.7 0.8 copy.32
  56.5 4.1 %fusion.12 = bf16[256,1024]{1,0:T(8,128)(2,1)} fusion(f32[64,8,8,128]{3,2,1,0:T(8,128)S(1)} %bitcast.82, bf16[256,1024]{1,0:T(8,128)(2,1)} %param.10, f32[256,256]{1,0:T(8,128)S(1)} %get-tuple-element.327, f32[256,256]{1,0:T(8,128)} %get-tuple-element.329), kind=kOutput, calls=%fused_computation.25 | convolution fusion | flops 1611530240 | bytes 3670016 | tf_op jit(solution)/shard_map/dot_general | solution.py:97
  60.6 0.7 all-gather.5.cloned.1.call-update
  61.3 28.9 %all-gather.3.cloned.1.call-done = bf16[256,4096]{1,0:T(8,128)(2,1)} async-done(((bf16[256,1024]{1,0:T(8,128)(2,1)}), bf16[256,4096]{1,0:T(8,128)(2,1)}) %all-gather.3.cloned.1.call-update) | async-done | bytes 2097168 | tf_op jit(solution)/shard_map/all_gather | solution.py:99
  90.2 151.2 %all-gather.5.cloned.1.call-done = bf16[4096,1024]{1,0:T(8,128)(2,1)} async-done(((bf16[1024,1024]{1,0:T(8,128)(2,1)}), bf16[4096,1024]{1,0:T(8,128)(2,1)}) %all-gather.5.cloned.1.call-update) | async-done | bytes 8388624 | tf_op jit(solution)/shard_map/all_gather | solution.py:102
  241.5 7.1 %convolution_convert_fusion = bf16[256,1024]{1,0:T(8,128)(2,1)} fusion(bf16[256,4096]{1,0:T(8,128)(2,1)} %all-gather.3.cloned.1.call-done, bf16[4096,1024]{1,0:T(8,128)(2,1)} %all-gather.5.cloned.1.call-done), kind=kOutput, calls=%fused_computation.24 | convolution fusion | flops 2147745792 | bytes 11010048 | tf_op jit(solution)/shard_map/dot_general | solution.py:100
  (30 shorter events, 1.1 us)
Async XLA Ops:
  6.5 5.2 %copy-start.4 = (s32[8]{0:T(128)S(1)}, s32[8]{0:T(128)}, u32[]{:S(2)}) copy-start(s32[8]{0:T(128)} %param.14) | copy-start | bytes 100
  6.5 5.9 %copy-start.3 = (f32[8,512]{1,0:T(8,128)S(1)}, f32[8,512]{1,0:T(8,128)}, u32[]{:S(2)}) copy-start(f32[8,512]{1,0:T(8,128)} %param.13) | copy-start | bytes 49156
  6.5 83.7 %all-gather.3.cloned.1.call-start = ((), (), s32[]{:S(2)}) async-start(), calls=%async_computation | async-start | bytes 2621440 | tf_op jit(solution)/shard_map/all_gather | solution.py:99
  9.5 5.2 %copy-start.1 = (bf16[256,1024]{1,0:T(8,128)(2,1)S(1)}, bf16[256,1024]{1,0:T(8,128)(2,1)}, u32[]{:S(2)}) copy-start(bf16[256,1024]{1,0:T(8,128)(2,1)} %param.12) | copy-start | bytes 1572868
  9.5 5.1 %copy-start.2 = (bf16[256,1024]{1,0:T(8,128)(2,1)S(1)}, bf16[256,1024]{1,0:T(8,128)(2,1)}, u32[]{:S(2)}) copy-start(bf16[256,1024]{1,0:T(8,128)(2,1)} %param.11) | copy-start | bytes 1572868
  14.9 0.8 copy-start
  18.7 16.4 %collective-permute-start = (bf16[256,1024]{1,0:T(8,128)(2,1)}, bf16[256,1024]{1,0:T(8,128)(2,1)S(1)}, u32[]{:S(2)}, u32[]{:S(2)}) collective-permute-start(bf16[256,1024]{1,0:T(8,128)(2,1)} %get-tuple-element.393), channel_id=1, source_target_pairs={{0,4},{4,8},{8,12},{1,5},{5,9},{9,13},{2,6},{6,10},{10,14},{3,7},{... | collective-permute-start | bytes 1572872 | tf_op jit(solution)/shard_map/while/body/eval_jaxpr/ppermute | solution.py:12
  35.9 19.8 %collective-permute-start = (bf16[256,1024]{1,0:T(8,128)(2,1)}, bf16[256,1024]{1,0:T(8,128)(2,1)S(1)}, u32[]{:S(2)}, u32[]{:S(2)}) collective-permute-start(bf16[256,1024]{1,0:T(8,128)(2,1)} %get-tuple-element.393), channel_id=1, source_target_pairs={{0,4},{4,8},{8,12},{1,5},{5,9},{9,13},{2,6},{6,10},{10,14},{3,7},{... | collective-permute-start | bytes 1572872 | tf_op jit(solution)/shard_map/while/body/eval_jaxpr/ppermute | solution.py:12
  60.5 180.9 %all-gather.5.cloned.1.call-start = ((), (), s32[]{:S(2)}) async-start(), calls=%async_computation.1 | async-start | bytes 10485760 | tf_op jit(solution)/shard_map/all_gather | solution.py:102
Sparse Core Ops, SparseCore 0:
  60.7 29.5 all-gather.2
  91.8 149.6 all-gather.4
where the time goes:
time: 256 us; the launch traced here: 255 us
  waiting for transfers between devices  202 us (79%)
  starting transfers between devices  14.2 us (6%)
  between operations  13.6 us (5%)
  matrix products  13.1 us (5%)
  other arithmetic  7.65 us (3%)
  local copies, waits for them, and re-layouts  4.01 us (2%)
    all_gather x1, waiting for transfers between devices, per_device(): lax.all_gather(out_weight, 'ctx', axis=0, tiled=True)  151 us
    all_gather x1, waiting for transfers between devices, per_device(): all_gated = lax.all_gather(gated, ('chan', 'sub'), axis=1, tiled=True)  28.9 us
    ppermute x2, waiting for transfers between devices, shifted(): lax.ppermute(value, axis, [(source, source + steps) for source in range(l...  20.6 us
    ppermute x2, starting transfers between devices, shifted(): lax.ppermute(value, axis, [(source, source + steps) for source in range(l...  14.2 us
    dot_general x1, matrix products, per_device(): jnp.dot(all_gated, lax.all_gather(out_weight, 'ctx', axis=0, tiled=True),...  7.14 us
  transfers between devices with their start and end apart: 4, of which 4 were waited for; matrix products, arithmetic and copies ran while one was open for 0% of the time, Pallas kernels for 0%

commit v1 on v0

--- a/solution.py
+++ b/solution.py
@@ -3,6 +3,8 @@
 import jax
 import jax.numpy as jnp
 from jax import lax
+from jax.experimental import pallas as pl
+from jax.experimental.pallas import tpu as pltpu
 from jax.sharding import PartitionSpec as P
 
 
@@ -45,7 +47,7 @@
     return jnp.concatenate([upper, bottom], axis=0)
 
 
-def per_device(q_proj, k_proj, v_proj, filters, filter_blocks, out_weight):
+def gathered_plan(q_proj, k_proj, v_proj, filters, filter_blocks, out_weight):
     block_len, channels = q_proj.shape
     groups = filters.shape[0]
     per_group = channels // groups
@@ -105,7 +107,184 @@
     return mixed.astype(jnp.bfloat16)
 
 
+def swap(value, *axes):
+    sizes = [lax.axis_size(axis) for axis in axes]
+    total = math.prod(sizes)
+    flip, stride = 0, 1
+    for size in reversed(sizes):
+        flip += stride
+        stride *= size
+    return lax.ppermute(value, axes, [(i, i ^ flip) for i in range(total)])
+
+
+def across(value, distance):
+    count = lax.axis_size("ctx")
+    return lax.ppermute(value, "ctx", [(i, i ^ distance) for i in range(count)])
+
+
+def conv_kernel(place, row_ref, *refs):
+    pieces, conv_ref, padded = refs[:4], refs[4], refs[5]
+    block, width = pieces[0].shape
+    groups, span = row_ref.shape
+    per_group = width // groups
+    padded[0] = jnp.zeros((block, width), padded.dtype)
+    padded[1] = jnp.zeros((block, width), padded.dtype)
+    for distance in range(4):
+        padded[2 + (place[0] ^ distance)] = pieces[distance][...]
+    for group in range(groups):
+        columns = pl.ds(group * per_group, per_group)
+        rows = jnp.broadcast_to(row_ref[group : group + 1, :], (block, span))
+        toeplitz = pltpu.roll(rows, 0, 1, stride=1, stride_axis=0).astype(jnp.bfloat16)
+        for token in range(4):
+            source = jnp.concatenate([padded[token + step, :, columns] for step in range(3)], axis=0)
+            conv_ref[token, :, columns] = jnp.dot(
+                toeplitz, source, preferred_element_type=jnp.float32
+            )
+
+
+def causal_conv(place, first_rows, pieces):
+    block, width = pieces[0].shape
+    return pl.pallas_call(
+        conv_kernel,
+        out_shape=jax.ShapeDtypeStruct((4, block, width), jnp.float32),
+        grid_spec=pltpu.PrefetchScalarGridSpec(
+            num_scalar_prefetch=1,
+            grid=(1,),
+            in_specs=[pl.BlockSpec(first_rows.shape, lambda i, s: (0, 0))]
+            + [pl.BlockSpec((block, width), lambda i, s: (0, 0))] * 4,
+            out_specs=pl.BlockSpec((4, block, width), lambda i, s: (0, 0, 0)),
+            scratch_shapes=[pltpu.VMEM((6, block, width), jnp.bfloat16)],
+        ),
+        compiler_params=pltpu.CompilerParams(vmem_limit_bytes=32 * 2**20),
+        cost_estimate=pl.CostEstimate(
+            flops=2 * 4 * block * 3 * block * width, bytes_accessed=2**21, transcendentals=0
+        ),
+    )(place, first_rows, *pieces)
+
+
+def project_kernel(place, *refs):
+    mine, other, own_w, got_w, out_ref = refs[:4], refs[4], refs[5], refs[6], refs[7]
+    bit, quarter, same = place[1], place[2], place[3]
+    tokens, width = mine[0].shape
+    half = tokens // 2
+    for part in range(2):
+        rows = pl.ds(part * half, half)
+        total = jnp.zeros((half, out_ref.shape[2]), jnp.float32)
+        for flip in range(4):
+            here, there = mine[flip][rows, :], other[flip, rows, :]
+            first = jnp.where(same == 1, here, there)
+            second = jnp.where(same == 1, there, here)
+            block = pl.ds(pl.multiple_of((quarter ^ flip) * width, width), width)
+            total += jnp.dot(first, own_w[block, :], preferred_element_type=jnp.float32)
+            total += jnp.dot(second, got_w[block, :], preferred_element_type=jnp.float32)
+        out_ref[part ^ bit] = total.astype(out_ref.dtype)
+
+
+def project(place, mine, other, out_weight, got_w):
+    tokens, width = mine[0].shape
+    depth, columns = got_w.shape
+    return pl.pallas_call(
+        project_kernel,
+        out_shape=jax.ShapeDtypeStruct((2, tokens // 2, columns), jnp.bfloat16),
+        grid_spec=pltpu.PrefetchScalarGridSpec(
+            num_scalar_prefetch=1,
+            grid=(1,),
+            in_specs=[pl.BlockSpec((tokens, width), lambda i, s: (0, 0))] * 4
+            + [
+                pl.BlockSpec((4, tokens, width), lambda i, s: (0, 0, 0)),
+                pl.BlockSpec((depth, columns), lambda i, s: (0, s[1])),
+                pl.BlockSpec((depth, columns), lambda i, s: (0, 0)),
+            ],
+            out_specs=pl.BlockSpec((2, tokens // 2, columns), lambda i, s: (0, 0, 0)),
+        ),
+        compiler_params=pltpu.CompilerParams(vmem_limit_bytes=32 * 2**20),
+        cost_estimate=pl.CostEstimate(
+            flops=2 * tokens * 8 * width * columns, bytes_accessed=2**22, transcendentals=0
+        ),
+    )(place, *mine, other, out_weight, got_w)
+
+
+def paired_plan(q_proj, k_proj, v_proj, filters, filter_blocks, out_weight):
+    block, channels = q_proj.shape
+    groups = filters.shape[0]
+    z, x, c = lax.axis_index("ctx"), lax.axis_index("chan"), lax.axis_index("sub")
+    pair, bit = z // 2, z % 2
+    quarter = 2 * x + bit
+    half, fourth = channels // 2, channels // 4
+    place = jnp.stack([z, bit, quarter, (c == bit).astype(jnp.int32)]).astype(jnp.int32)
+
+    tap_index = jnp.arange(filters.shape[1], dtype=jnp.int32)
+    masked = jnp.where(tap_index[None, :] < filter_blocks[:, None] * block, filters, 0.0)
+    taken = groups // 4
+    for_other = lax.dynamic_slice_in_dim(masked, (2 * (1 - x) + bit) * taken, taken, 0)
+    taps = jnp.where(
+        pair == x, lax.dynamic_slice_in_dim(masked, quarter * taken, taken, 0), swap(for_other, "chan")
+    )
+    first_rows = jnp.concatenate(
+        [jnp.zeros((taken, 1), jnp.float32), taps[:, ::-1], jnp.zeros((taken, block - 1), jnp.float32)],
+        axis=1,
+    )
+
+    product = (k_proj.astype(jnp.float32) * v_proj.astype(jnp.float32)).astype(jnp.bfloat16)
+
+    def spread(array):
+        kept = lax.dynamic_slice_in_dim(array, x * half, half, 1)
+        came = swap(lax.dynamic_slice_in_dim(array, (1 - x) * half, half, 1), "chan")
+        pieces = []
+        for distance in range(4):
+            target = z ^ distance
+            start = (target % 2) * fourth
+            pieces.append(
+                jnp.where(
+                    target // 2 == x,
+                    lax.dynamic_slice_in_dim(kept, start, fourth, 1),
+                    lax.dynamic_slice_in_dim(came, start, fourth, 1),
+                )
+            )
+        return [pieces[0]] + [across(pieces[distance], distance) for distance in (1, 2, 3)]
+
+    product_pieces = spread(product)
+    q_pieces = spread(q_proj)
+    got_w = across(lax.dynamic_slice_in_dim(out_weight, (1 - bit) * half, half, 1), 1)
+    conv = causal_conv(place, first_rows, product_pieces)
+
+    def mixed_partials(own, near, which):
+        low = jnp.where(bit == 0, own, near)
+        high = jnp.where(bit == 0, near, own)
+        gate = jnp.stack([low, high])
+        signal = lax.dynamic_slice_in_dim(conv, 2 * which, 2, 0)
+        gated = (gate.astype(jnp.float32) * signal).astype(jnp.bfloat16).reshape(2 * block, fourth)
+        mine = [gated, swap(gated, "ctx"), swap(gated, "chan"), swap(gated, "ctx", "chan")]
+        other = swap(jnp.stack(mine), "sub")
+        return project(place, mine, other, out_weight, got_w)
+
+    far = mixed_partials(q_pieces[2], q_pieces[3], 1 - pair)
+    far_own, far_near = across(far[0], 2), across(far[1], 3)
+    close = mixed_partials(q_pieces[0], q_pieces[1], pair)
+    near = across(close[1], 1)
+    this_half = close[0].astype(jnp.float32) + far_own.astype(jnp.float32)
+    that_half = near.astype(jnp.float32) + far_near.astype(jnp.float32)
+    left = jnp.where(bit == 0, this_half, that_half)
+    right = jnp.where(bit == 0, that_half, this_half)
+    return jnp.concatenate([left, right], axis=1).astype(jnp.bfloat16)
+
+
 def solution(mesh):
+    sizes = dict(mesh.shape)
+
+    def per_device(q_proj, k_proj, v_proj, filters, filter_blocks, out_weight):
+        block, channels = q_proj.shape
+        groups, taps = filters.shape
+        paired = (
+            (sizes["ctx"], sizes["chan"], sizes["sub"]) == (4, 2, 2)
+            and taps == 2 * block
+            and groups % 4 == 0
+            and (channels // groups) % 128 == 0
+            and out_weight.shape == (channels, channels)
+        )
+        plan = paired_plan if paired else gathered_plan
+        return plan(q_proj, k_proj, v_proj, filters, filter_blocks, out_weight)
+
     in_specs = (
         P(("group", "ctx"), ("chan", "sub")),
         P(("group", "ctx"), ("chan", "sub")),

time: 256 us -> 120 us (0.47)
  waiting for transfers between devices: 202 us -> 81.9 us
  between operations: 13.6 us -> 0.23 us
  matrix products: 13.1 us -> 0 us
  starting transfers between devices: 14.2 us -> 25.9 us
  Pallas kernels: 0 us -> 5.31 us
    all_gather x2 -> x0, waiting for transfers between devices: 180 us -> none  [the longest x1 151 us: per_device(): lax.all_gather(out_weight, 'ctx', axis=0, tiled=True)]
    ppermute x2 -> x21, waiting for transfers between devices: 20.6 us -> 81.9 us  [the longest x11 47.1 us: swap(): return lax.ppermute(value, axes, [(i, i ^ flip) for i in range(total)])]
    dot_general x5 -> x0, matrix products: 13.1 us -> none  [the longest x1 7.14 us: per_device(): jnp.dot(all_gated, lax.all_gather(out_weight, 'ctx', axis=0, tiled=True),...]
    ppermute x2 -> x21, starting transfers between devices: 14.2 us -> 25.9 us  [the longest x10 16.4 us: across(): return lax.ppermute(value, 'ctx', [(i, i ^ distance) for i in range(count)])]
    pallas_call x0 -> x3, Pallas kernels: none -> 5.31 us  [the longest x2 3.73 us: project(): pl.pallas_call(project_kernel, out_shape=jax.ShapeDtypeStruct((2, tokens...]
  transfers between devices with their start and end apart: 4 -> 21, of which waited for: 4 -> 11; matrix products, arithmetic and copies ran while one was open for 0% -> 3% of each run, Pallas kernels for 0% -> 4%
where the time goes in v1:
time: 120 us
  waiting for transfers between devices  81.9 us (68%)
  starting transfers between devices  25.9 us (22%)
  Pallas kernels  5.31 us (4%)
  other arithmetic  5.19 us (4%)
  local copies, waits for them, and re-layouts  1.62 us (1%)
    ppermute x11, waiting for transfers between devices, swap(): return lax.ppermute(value, axes, [(i, i ^ flip) for i in range(total)])  47.1 us
    ppermute x10, waiting for transfers between devices, across(): return lax.ppermute(value, 'ctx', [(i, i ^ distance) for i in range(count)])  34.8 us
    ppermute x10, starting transfers between devices, across(): return lax.ppermute(value, 'ctx', [(i, i ^ distance) for i in range(count)])  16.4 us
    ppermute x11, starting transfers between devices, swap(): return lax.ppermute(value, axes, [(i, i ^ flip) for i in range(total)])  9.51 us
    pallas_call x2, Pallas kernels, project(): pl.pallas_call(project_kernel, out_shape=jax.ShapeDtypeStruct((2, tokens...  3.73 us
  transfers between devices with their start and end apart: 21, of which 11 were waited for; matrix products, arithmetic and copies ran while one was open for 3% of the time, Pallas kernels for 4%

profile of v1, /device:TPU:0, one launch (start us, length us, event | category | flops | bytes accessed | tf_op | source)
XLA Modules:
  0.0 120.1 jit_solution(12092794292665609319)
XLA Ops:
  1.5 3.0 %collective-permute-start.2 = (f32[2,512]{1,0:T(2,128)S(1)}, f32[2,512]{1,0:T(2,128)S(1)}, u32[]{:S(2)}, u32[]{:S(2)}) collective-permute-start(f32[2,512]{1,0:T(2,128)S(1)} %constant_dynamic-slice_fusion.2), channel_id=1, source_target_pairs={{0,2},{2,0},{1,3},{3,1},{4,6},{6,4},{5,7},{7,5},{8,10},{10,8},{9,1... | collective-permute-start | bytes 12296 | tf_op jit(solution)/shard_map/ppermute | solution.py:117
  7.0 2.1 %collective-permute-start.3 = (bf16[256,512]{1,0:T(8,128)(2,1)S(1)}, bf16[256,512]{1,0:T(8,128)(2,1)S(1)}, u32[]{:S(2)}, u32[]{:S(2)}) collective-permute-start(bf16[256,512]{1,0:T(8,128)(2,1)S(1)} %constant_dynamic-slice_fusion.1), channel_id=1, source_target_pairs={{0,2},{2,0},{1,3},{3,1},{4,6},{6,4},{5,7},{7,5},{8,10},{10,8},{9,1... | collective-permute-start | bytes 786440 | tf_op jit(solution)/shard_map/ppermute | solution.py:117
  9.3 5.5 %collective-permute-done = bf16[256,512]{1,0:T(8,128)(2,1)S(1)} collective-permute-done((bf16[256,512]{1,0:T(8,128)(2,1)S(1)}, bf16[256,512]{1,0:T(8,128)(2,1)S(1)}, u32[]{:S(2)}, u32[]{:S(2)}) %collective-permute-start) | collective-permute-done | bytes 262176 | tf_op jit(solution)/shard_map/ppermute | solution.py:117
  14.9 1.6 %collective-permute-start.1 = (bf16[256,256]{1,0:T(8,128)(2,1)S(1)}, bf16[256,256]{1,0:T(8,128)(2,1)S(1)}, u32[]{:S(2)}, u32[]{:S(2)}) collective-permute-start(bf16[256,256]{1,0:T(8,128)(2,1)S(1)} %dynamic-slice_select_fusion.6), channel_id=1, source_target_pairs={{0,4},{4,0},{8,12},{12,8},{1,5},{5,1},{9,13},{13,9},{2,6},{6,2},{1... | collective-permute-start | bytes 393224 | tf_op jit(solution)/shard_map/ppermute | solution.py:122
  16.9 2.0 %collective-permute-done.3 = bf16[256,512]{1,0:T(8,128)(2,1)S(1)} collective-permute-done((bf16[256,512]{1,0:T(8,128)(2,1)S(1)}, bf16[256,512]{1,0:T(8,128)(2,1)S(1)}, u32[]{:S(2)}, u32[]{:S(2)}) %collective-permute-start.3) | collective-permute-done | bytes 262176 | tf_op jit(solution)/shard_map/ppermute | solution.py:117
  19.2 1.6 %collective-permute-start.4 = (bf16[256,256]{1,0:T(8,128)(2,1)S(1)}, bf16[256,256]{1,0:T(8,128)(2,1)S(1)}, u32[]{:S(2)}, u32[]{:S(2)}) collective-permute-start(bf16[256,256]{1,0:T(8,128)(2,1)S(1)} %get-tuple-element.15), channel_id=1, source_target_pairs={{0,4},{4,0},{8,12},{12,8},{1,5},{5,1},{9,13},{13,9},{2,6},{6,2},{1... | collective-permute-start | bytes 393224 | tf_op jit(solution)/shard_map/ppermute | solution.py:122
  20.9 2.6 %collective-permute-start.5 = (bf16[256,256]{1,0:T(8,128)(2,1)S(1)}, bf16[256,256]{1,0:T(8,128)(2,1)S(1)}, u32[]{:S(2)}, u32[]{:S(2)}) collective-permute-start(bf16[256,256]{1,0:T(8,128)(2,1)S(1)} %get-tuple-element.14), channel_id=1, source_target_pairs={{0,8},{4,12},{8,0},{12,4},{1,9},{5,13},{9,1},{13,5},{2,10},{6,14},... | collective-permute-start | bytes 393224 | tf_op jit(solution)/shard_map/ppermute | solution.py:122
  23.9 1.8 %collective-permute-start.12 = (bf16[256,256]{1,0:T(8,128)(2,1)S(1)}, bf16[256,256]{1,0:T(8,128)(2,1)S(1)}, u32[]{:S(2)}, u32[]{:S(2)}) collective-permute-start(bf16[256,256]{1,0:T(8,128)(2,1)S(1)} %get-tuple-element.12), channel_id=1, source_target_pairs={{0,8},{4,12},{8,0},{12,4},{1,9},{5,13},{9,1},{13,5},{2,10},{6,14},... | collective-permute-start | bytes 393224 | tf_op jit(solution)/shard_map/ppermute | solution.py:122
  25.7 2.0 %collective-permute-start.13 = (bf16[256,256]{1,0:T(8,128)(2,1)S(1)}, bf16[256,256]{1,0:T(8,128)(2,1)S(1)}, u32[]{:S(2)}, u32[]{:S(2)}) collective-permute-start(bf16[256,256]{1,0:T(8,128)(2,1)S(1)} %get-tuple-element.11), channel_id=1, source_target_pairs={{0,12},{4,8},{8,4},{12,0},{1,13},{5,9},{9,5},{13,1},{2,14},{6,10},... | collective-permute-start | bytes 393224 | tf_op jit(solution)/shard_map/ppermute | solution.py:122
  27.8 10.5 %collective-permute-done.5.refs_2_ = bf16[256,256]{1,0:T(8,128)(2,1)S(1)} collective-permute-done((bf16[256,256]{1,0:T(8,128)(2,1)S(1)}, bf16[256,256]{1,0:T(8,128)(2,1)S(1)}, u32[]{:S(2)}, u32[]{:S(2)}) %collective-permute-start.5) | collective-permute-done | bytes 131104 | tf_op jit(solution)/shard_map/ppermute | solution.py:122
  38.3 1.6 %shard_map.64 = f32[4,256,256]{2,1,0:T(8,128)S(1)} custom-call(s32[4]{0:T(128)S(1)} %pad_add_fusion.place, f32[2,768]{1,0:T(2,128)S(1)} %maximum_maximum_fusion.row_ref, bf16[256,256]{1,0:T(8,128)(2,1)S(1)} %get-tuple-element.16.refs_0_, bf16[256,256]{1,0:T(8,128)(2,1)S(1)} %collective-permute-done.4.refs_1_, ...), custom_call_target="tpu_custom_call" | custom-call | flops 402653184 | bytes 2097152 | tf_op jit(solution)/shard_map/pallas_call | solution.py:147
  39.9 3.9 %collective-permute-done.12 = bf16[256,256]{1,0:T(8,128)(2,1)S(1)} collective-permute-done((bf16[256,256]{1,0:T(8,128)(2,1)S(1)}, bf16[256,256]{1,0:T(8,128)(2,1)S(1)}, u32[]{:S(2)}, u32[]{:S(2)}) %collective-permute-start.12) | collective-permute-done | bytes 131104 | tf_op jit(solution)/shard_map/ppermute | solution.py:122
  44.0 2.0 %collective-permute-start.14 = (bf16[512,256]{1,0:T(8,128)(2,1)S(1)}, bf16[512,256]{1,0:T(8,128)(2,1)S(1)}, u32[]{:S(2)}, u32[]{:S(2)}) collective-permute-start(bf16[512,256]{1,0:T(8,128)(2,1)S(1)} %bitcast.41), channel_id=1, source_target_pairs={{0,4},{4,0},{8,12},{12,8},{1,5},{5,1},{9,13},{13,9},{2,6},{6,2},{1... | collective-permute-start | bytes 786440 | tf_op jit(solution)/shard_map/ppermute | solution.py:117
  47.7 2.0 %collective-permute-start.11 = (bf16[1024,512]{1,0:T(8,128)(2,1)S(1)}, bf16[1024,512]{1,0:T(8,128)(2,1)S(1)}, u32[]{:S(2)}, u32[]{:S(2)}) collective-permute-start(bf16[1024,512]{1,0:T(8,128)(2,1)S(1)} %constant_dynamic-slice_fusion), channel_id=1, source_target_pairs={{0,4},{4,0},{8,12},{12,8},{1,5},{5,1},{9,13},{13,9},{2,6},{6,2},{1... | collective-permute-start | bytes 3145736 | tf_op jit(solution)/shard_map/ppermute | solution.py:122
  49.7 3.5 %collective-permute-done.14.refs_1_ = bf16[512,256]{1,0:T(8,128)(2,1)S(1)} collective-permute-done((bf16[512,256]{1,0:T(8,128)(2,1)S(1)}, bf16[512,256]{1,0:T(8,128)(2,1)S(1)}, u32[]{:S(2)}, u32[]{:S(2)}) %collective-permute-start.14) | collective-permute-done | bytes 262176 | tf_op jit(solution)/shard_map/ppermute | solution.py:117
  53.9 6.4 %collective-permute-done.15.refs_2_ = bf16[512,256]{1,0:T(8,128)(2,1)S(1)} collective-permute-done((bf16[512,256]{1,0:T(8,128)(2,1)S(1)}, bf16[512,256]{1,0:T(8,128)(2,1)S(1)}, u32[]{:S(2)}, u32[]{:S(2)}) %collective-permute-start.15) | collective-permute-done | bytes 262176 | tf_op jit(solution)/shard_map/ppermute | solution.py:117
  60.5 26.5 %collective-permute-done.7.refs_1_ = bf16[512,256]{1,0:T(8,128)(2,1)S(1)} collective-permute-done((bf16[512,256]{1,0:T(8,128)(2,1)S(1)}, bf16[512,256]{1,0:T(8,128)(2,1)S(1)}, u32[]{:S(2)}, u32[]{:S(2)}) %collective-permute-start.7) | collective-permute-done | bytes 262176 | tf_op jit(solution)/shard_map/ppermute | solution.py:117
  87.0 3.2 %collective-permute-done.9.refs_3_ = bf16[512,256]{1,0:T(8,128)(2,1)S(1)} collective-permute-done((bf16[512,256]{1,0:T(8,128)(2,1)S(1)}, bf16[512,256]{1,0:T(8,128)(2,1)S(1)}, u32[]{:S(2)}, u32[]{:S(2)}) %collective-permute-start.9) | collective-permute-done | bytes 262176 | tf_op jit(solution)/shard_map/ppermute | solution.py:117
  90.4 1.9 %shard_map.66 = bf16[2,256,512]{2,1,0:T(8,128)(2,1)S(1)} custom-call(s32[4]{0:T(128)S(1)} %pad_add_fusion.place, bf16[512,256]{1,0:T(8,128)(2,1)S(1)} %bitcast.45, bf16[512,256]{1,0:T(8,128)(2,1)S(1)} %collective-permute-done.14.refs_1_, bf16[512,256]{1,0:T(8,128)(2,1)S(1)} %collective-permute-done.15.refs_2_, ...), custom_call_target="tpu_custom_call" | custom-call | flops 1073741824 | bytes 4194304 | tf_op jit(solution)/shard_map/pallas_call | solution.py:186
  92.3 2.2 %collective-permute-start.20 = (bf16[256,512]{1,0:T(8,128)(2,1)S(1)}, bf16[256,512]{1,0:T(8,128)(2,1)S(1)}, u32[]{:S(2)}, u32[]{:S(2)}) collective-permute-start(bf16[256,512]{1,0:T(8,128)(2,1)S(1)} %get-tuple-element.18), channel_id=1, source_target_pairs={{0,12},{4,8},{8,4},{12,0},{1,13},{5,9},{9,5},{13,1},{2,14},{6,10},... | collective-permute-start | bytes 786440 | tf_op jit(solution)/shard_map/ppermute | solution.py:122
  94.5 1.9 %shard_map.65 = bf16[2,256,512]{2,1,0:T(8,128)(2,1)S(1)} custom-call(s32[4]{0:T(128)S(1)} %pad_add_fusion.place, bf16[512,256]{1,0:T(8,128)(2,1)S(1)} %bitcast.40, bf16[512,256]{1,0:T(8,128)(2,1)S(1)} %collective-permute-done.7.refs_1_, bf16[512,256]{1,0:T(8,128)(2,1)S(1)} %collective-permute-done.8.refs_2_, ...), custom_call_target="tpu_custom_call" | custom-call | flops 1073741824 | bytes 4194304 | tf_op jit(solution)/shard_map/pallas_call | solution.py:186
  98.7 4.7 %collective-permute-done.20 = bf16[256,512]{1,0:T(8,128)(2,1)S(1)} collective-permute-done((bf16[256,512]{1,0:T(8,128)(2,1)S(1)}, bf16[256,512]{1,0:T(8,128)(2,1)S(1)}, u32[]{:S(2)}, u32[]{:S(2)}) %collective-permute-start.20) | collective-permute-done | bytes 262176 | tf_op jit(solution)/shard_map/ppermute | solution.py:122
  103.4 6.0 %collective-permute-done.19 = bf16[256,512]{1,0:T(8,128)(2,1)S(1)} collective-permute-done((bf16[256,512]{1,0:T(8,128)(2,1)S(1)}, bf16[256,512]{1,0:T(8,128)(2,1)S(1)}, u32[]{:S(2)}, u32[]{:S(2)}) %collective-permute-start.19) | collective-permute-done | bytes 262176 | tf_op jit(solution)/shard_map/ppermute | solution.py:122
  109.4 9.7 %collective-permute-done.18 = bf16[256,512]{1,0:T(8,128)(2,1)S(1)} collective-permute-done((bf16[256,512]{1,0:T(8,128)(2,1)S(1)}, bf16[256,512]{1,0:T(8,128)(2,1)S(1)}, u32[]{:S(2)}, u32[]{:S(2)}) %collective-permute-start.18) | collective-permute-done | bytes 262176 | tf_op jit(solution)/shard_map/ppermute | solution.py:122
  (50 shorter events, 11.8 us)
Async XLA Ops:
  0.0 14.8 %copy-start.1 = (bf16[256,1024]{1,0:T(8,128)(2,1)S(1)}, bf16[256,1024]{1,0:T(8,128)(2,1)}, u32[]{:S(2)}) copy-start(bf16[256,1024]{1,0:T(8,128)(2,1)} %param.6) | copy-start | bytes 1572868
  1.5 15.0 %collective-permute-start.2 = (f32[2,512]{1,0:T(2,128)S(1)}, f32[2,512]{1,0:T(2,128)S(1)}, u32[]{:S(2)}, u32[]{:S(2)}) collective-permute-start(f32[2,512]{1,0:T(2,128)S(1)} %constant_dynamic-slice_fusion.2), channel_id=1, source_target_pairs={{0,2},{2,0},{1,3},{3,1},{4,6},{6,4},{5,7},{7,5},{8,10},{10,8},{9,1... | collective-permute-start | bytes 12296 | tf_op jit(solution)/shard_map/ppermute | solution.py:117
  5.5 9.3 %collective-permute-start = (bf16[256,512]{1,0:T(8,128)(2,1)S(1)}, bf16[256,512]{1,0:T(8,128)(2,1)S(1)}, u32[]{:S(2)}, u32[]{:S(2)}) collective-permute-start(bf16[256,512]{1,0:T(8,128)(2,1)S(1)} %constant_dynamic-slice_fusion.4), channel_id=1, source_target_pairs={{0,2},{2,0},{1,3},{3,1},{4,6},{6,4},{5,7},{7,5},{8,10},{10,8},{9,1... | collective-permute-start | bytes 786440 | tf_op jit(solution)/shard_map/ppermute | solution.py:117
  7.0 11.9 %collective-permute-start.3 = (bf16[256,512]{1,0:T(8,128)(2,1)S(1)}, bf16[256,512]{1,0:T(8,128)(2,1)S(1)}, u32[]{:S(2)}, u32[]{:S(2)}) collective-permute-start(bf16[256,512]{1,0:T(8,128)(2,1)S(1)} %constant_dynamic-slice_fusion.1), channel_id=1, source_target_pairs={{0,2},{2,0},{1,3},{3,1},{4,6},{6,4},{5,7},{7,5},{8,10},{10,8},{9,1... | collective-permute-start | bytes 786440 | tf_op jit(solution)/shard_map/ppermute | solution.py:117
  14.9 8.8 %collective-permute-start.1 = (bf16[256,256]{1,0:T(8,128)(2,1)S(1)}, bf16[256,256]{1,0:T(8,128)(2,1)S(1)}, u32[]{:S(2)}, u32[]{:S(2)}) collective-permute-start(bf16[256,256]{1,0:T(8,128)(2,1)S(1)} %dynamic-slice_select_fusion.6), channel_id=1, source_target_pairs={{0,4},{4,0},{8,12},{12,8},{1,5},{5,1},{9,13},{13,9},{2,6},{6,2},{1... | collective-permute-start | bytes 393224 | tf_op jit(solution)/shard_map/ppermute | solution.py:122
  19.2 8.6 %collective-permute-start.4 = (bf16[256,256]{1,0:T(8,128)(2,1)S(1)}, bf16[256,256]{1,0:T(8,128)(2,1)S(1)}, u32[]{:S(2)}, u32[]{:S(2)}) collective-permute-start(bf16[256,256]{1,0:T(8,128)(2,1)S(1)} %get-tuple-element.15), channel_id=1, source_target_pairs={{0,4},{4,0},{8,12},{12,8},{1,5},{5,1},{9,13},{13,9},{2,6},{6,2},{1... | collective-permute-start | bytes 393224 | tf_op jit(solution)/shard_map/ppermute | solution.py:122
  20.9 17.4 %collective-permute-start.5 = (bf16[256,256]{1,0:T(8,128)(2,1)S(1)}, bf16[256,256]{1,0:T(8,128)(2,1)S(1)}, u32[]{:S(2)}, u32[]{:S(2)}) collective-permute-start(bf16[256,256]{1,0:T(8,128)(2,1)S(1)} %get-tuple-element.14), channel_id=1, source_target_pairs={{0,8},{4,12},{8,0},{12,4},{1,9},{5,13},{9,1},{13,5},{2,10},{6,14},... | collective-permute-start | bytes 393224 | tf_op jit(solution)/shard_map/ppermute | solution.py:122
  23.4 14.8 %collective-permute-start.6 = (bf16[256,256]{1,0:T(8,128)(2,1)S(1)}, bf16[256,256]{1,0:T(8,128)(2,1)S(1)}, u32[]{:S(2)}, u32[]{:S(2)}) collective-permute-start(bf16[256,256]{1,0:T(8,128)(2,1)S(1)} %get-tuple-element.13), channel_id=1, source_target_pairs={{0,12},{4,8},{8,4},{12,0},{1,13},{5,9},{9,5},{13,1},{2,14},{6,10},... | collective-permute-start | bytes 393224 | tf_op jit(solution)/shard_map/ppermute | solution.py:122
  23.9 19.8 %collective-permute-start.12 = (bf16[256,256]{1,0:T(8,128)(2,1)S(1)}, bf16[256,256]{1,0:T(8,128)(2,1)S(1)}, u32[]{:S(2)}, u32[]{:S(2)}) collective-permute-start(bf16[256,256]{1,0:T(8,128)(2,1)S(1)} %get-tuple-element.12), channel_id=1, source_target_pairs={{0,8},{4,12},{8,0},{12,4},{1,9},{5,13},{9,1},{13,5},{2,10},{6,14},... | collective-permute-start | bytes 393224 | tf_op jit(solution)/shard_map/ppermute | solution.py:122
  25.7 18.1 %collective-permute-start.13 = (bf16[256,256]{1,0:T(8,128)(2,1)S(1)}, bf16[256,256]{1,0:T(8,128)(2,1)S(1)}, u32[]{:S(2)}, u32[]{:S(2)}) collective-permute-start(bf16[256,256]{1,0:T(8,128)(2,1)S(1)} %get-tuple-element.11), channel_id=1, source_target_pairs={{0,12},{4,8},{8,4},{12,0},{1,13},{5,9},{9,5},{13,1},{2,14},{6,10},... | collective-permute-start | bytes 393224 | tf_op jit(solution)/shard_map/ppermute | solution.py:122
  38.3 9.3 %copy-start = (bf16[1024,1024]{1,0:T(8,128)(2,1)S(1)}, bf16[1024,1024]{1,0:T(8,128)(2,1)}, u32[]{:S(2)}) copy-start(bf16[1024,1024]{1,0:T(8,128)(2,1)} %refs_5_.3) | copy-start | bytes 6291460
  44.0 9.3 %collective-permute-start.14 = (bf16[512,256]{1,0:T(8,128)(2,1)S(1)}, bf16[512,256]{1,0:T(8,128)(2,1)S(1)}, u32[]{:S(2)}, u32[]{:S(2)}) collective-permute-start(bf16[512,256]{1,0:T(8,128)(2,1)S(1)} %bitcast.41), channel_id=1, source_target_pairs={{0,4},{4,0},{8,12},{12,8},{1,5},{5,1},{9,13},{13,9},{2,6},{6,2},{1... | collective-permute-start | bytes 786440 | tf_op jit(solution)/shard_map/ppermute | solution.py:117
  46.0 14.3 %collective-permute-start.15 = (bf16[512,256]{1,0:T(8,128)(2,1)S(1)}, bf16[512,256]{1,0:T(8,128)(2,1)S(1)}, u32[]{:S(2)}, u32[]{:S(2)}) collective-permute-start(bf16[512,256]{1,0:T(8,128)(2,1)S(1)} %bitcast.42), channel_id=1, source_target_pairs={{0,2},{2,0},{1,3},{3,1},{4,6},{6,4},{5,7},{7,5},{8,10},{10,8},{9,1... | collective-permute-start | bytes 786440 | tf_op jit(solution)/shard_map/ppermute | solution.py:117
  46.6 13.7 %collective-permute-start.16 = (bf16[512,256]{1,0:T(8,128)(2,1)S(1)}, bf16[512,256]{1,0:T(8,128)(2,1)S(1)}, u32[]{:S(2)}, u32[]{:S(2)}) collective-permute-start(bf16[512,256]{1,0:T(8,128)(2,1)S(1)} %bitcast.43), channel_id=1, source_target_pairs={{0,6},{2,4},{4,2},{6,0},{8,14},{10,12},{12,10},{14,8},{1,7},{3,5},... | collective-permute-start | bytes 786440 | tf_op jit(solution)/shard_map/ppermute | solution.py:117
  47.7 42.7 %collective-permute-start.11 = (bf16[1024,512]{1,0:T(8,128)(2,1)S(1)}, bf16[1024,512]{1,0:T(8,128)(2,1)S(1)}, u32[]{:S(2)}, u32[]{:S(2)}) collective-permute-start(bf16[1024,512]{1,0:T(8,128)(2,1)S(1)} %constant_dynamic-slice_fusion), channel_id=1, source_target_pairs={{0,4},{4,0},{8,12},{12,8},{1,5},{5,1},{9,13},{13,9},{2,6},{6,2},{1... | collective-permute-start | bytes 3145736 | tf_op jit(solution)/shard_map/ppermute | solution.py:122
  49.7 37.3 %collective-permute-start.7 = (bf16[512,256]{1,0:T(8,128)(2,1)S(1)}, bf16[512,256]{1,0:T(8,128)(2,1)S(1)}, u32[]{:S(2)}, u32[]{:S(2)}) collective-permute-start(bf16[512,256]{1,0:T(8,128)(2,1)S(1)} %bitcast.36), channel_id=1, source_target_pairs={{0,4},{4,0},{8,12},{12,8},{1,5},{5,1},{9,13},{13,9},{2,6},{6,2},{1... | collective-permute-start | bytes 786440 | tf_op jit(solution)/shard_map/ppermute | solution.py:117
  53.3 33.7 %collective-permute-start.8 = (bf16[512,256]{1,0:T(8,128)(2,1)S(1)}, bf16[512,256]{1,0:T(8,128)(2,1)S(1)}, u32[]{:S(2)}, u32[]{:S(2)}) collective-permute-start(bf16[512,256]{1,0:T(8,128)(2,1)S(1)} %bitcast.37), channel_id=1, source_target_pairs={{0,2},{2,0},{1,3},{3,1},{4,6},{6,4},{5,7},{7,5},{8,10},{10,8},{9,1... | collective-permute-start | bytes 786440 | tf_op jit(solution)/shard_map/ppermute | solution.py:117
  60.3 29.9 %collective-permute-start.9 = (bf16[512,256]{1,0:T(8,128)(2,1)S(1)}, bf16[512,256]{1,0:T(8,128)(2,1)S(1)}, u32[]{:S(2)}, u32[]{:S(2)}) collective-permute-start(bf16[512,256]{1,0:T(8,128)(2,1)S(1)} %bitcast.38), channel_id=1, source_target_pairs={{0,6},{2,4},{4,2},{6,0},{8,14},{10,12},{12,10},{14,8},{1,7},{3,5},... | collective-permute-start | bytes 786440 | tf_op jit(solution)/shard_map/ppermute | solution.py:117
  60.4 30.0 %collective-permute-start.17 = (bf16[4,512,256]{2,1,0:T(8,128)(2,1)S(1)}, bf16[4,512,256]{2,1,0:T(8,128)(2,1)S(1)}, u32[]{:S(2)}, u32[]{:S(2)}) collective-permute-start(bf16[4,512,256]{2,1,0:T(8,128)(2,1)S(1)} %pad_maximum_fusion.1), channel_id=1, source_target_pairs={{0,1},{1,0},{2,3},{3,2},{4,5},{5,4},{6,7},{7,6},{8,9},{9,8},{10,11... | collective-permute-start | bytes 3145736 | tf_op jit(solution)/shard_map/ppermute | solution.py:117
  90.3 4.2 %collective-permute-start.10 = (bf16[4,512,256]{2,1,0:T(8,128)(2,1)S(1)}, bf16[4,512,256]{2,1,0:T(8,128)(2,1)S(1)}, u32[]{:S(2)}, u32[]{:S(2)}) collective-permute-start(bf16[4,512,256]{2,1,0:T(8,128)(2,1)S(1)} %pad_maximum_fusion), channel_id=1, source_target_pairs={{0,1},{1,0},{2,3},{3,2},{4,5},{5,4},{6,7},{7,6},{8,9},{9,8},{10,11... | collective-permute-start | bytes 3145736 | tf_op jit(solution)/shard_map/ppermute | solution.py:117
  92.3 11.1 %collective-permute-start.20 = (bf16[256,512]{1,0:T(8,128)(2,1)S(1)}, bf16[256,512]{1,0:T(8,128)(2,1)S(1)}, u32[]{:S(2)}, u32[]{:S(2)}) collective-permute-start(bf16[256,512]{1,0:T(8,128)(2,1)S(1)} %get-tuple-element.18), channel_id=1, source_target_pairs={{0,12},{4,8},{8,4},{12,0},{1,13},{5,9},{9,5},{13,1},{2,14},{6,10},... | collective-permute-start | bytes 786440 | tf_op jit(solution)/shard_map/ppermute | solution.py:122
  96.4 13.0 %collective-permute-start.19 = (bf16[256,512]{1,0:T(8,128)(2,1)S(1)}, bf16[256,512]{1,0:T(8,128)(2,1)S(1)}, u32[]{:S(2)}, u32[]{:S(2)}) collective-permute-start(bf16[256,512]{1,0:T(8,128)(2,1)S(1)} %slice_bitcast_fusion.1), channel_id=1, source_target_pairs={{0,4},{4,0},{8,12},{12,8},{1,5},{5,1},{9,13},{13,9},{2,6},{6,2},{1... | collective-permute-start | bytes 786440 | tf_op jit(solution)/shard_map/ppermute | solution.py:122
  97.3 21.8 %collective-permute-start.18 = (bf16[256,512]{1,0:T(8,128)(2,1)S(1)}, bf16[256,512]{1,0:T(8,128)(2,1)S(1)}, u32[]{:S(2)}, u32[]{:S(2)}) collective-permute-start(bf16[256,512]{1,0:T(8,128)(2,1)S(1)} %get-tuple-element.17), channel_id=1, source_target_pairs={{0,8},{4,12},{8,0},{12,4},{1,9},{5,13},{9,1},{13,5},{2,10},{6,14},... | collective-permute-start | bytes 786440 | tf_op jit(solution)/shard_map/ppermute | solution.py:122

commit v2 on v1

--- a/solution.py
+++ b/solution.py
@@ -208,28 +208,39 @@
     block, channels = q_proj.shape
     groups = filters.shape[0]
     z, x, c = lax.axis_index("ctx"), lax.axis_index("chan"), lax.axis_index("sub")
+    g = lax.axis_index("group")
     pair, bit = z // 2, z % 2
     quarter = 2 * x + bit
     half, fourth = channels // 2, channels // 4
     place = jnp.stack([z, bit, quarter, (c == bit).astype(jnp.int32)]).astype(jnp.int32)
 
+    other_cols = (1 - bit) * half + g * fourth
+    w_near = across(lax.dynamic_slice_in_dim(out_weight, other_cols, fourth, 1), 1)
+    w_far = swap(w_near, "group")
+    got_w = jnp.where(
+        g == 0, jnp.concatenate([w_near, w_far], axis=1), jnp.concatenate([w_far, w_near], axis=1)
+    )
+
     tap_index = jnp.arange(filters.shape[1], dtype=jnp.int32)
     masked = jnp.where(tap_index[None, :] < filter_blocks[:, None] * block, filters, 0.0)
+    masked = masked.astype(jnp.bfloat16)
     taken = groups // 4
     for_other = lax.dynamic_slice_in_dim(masked, (2 * (1 - x) + bit) * taken, taken, 0)
+    for_other = jnp.concatenate([for_other, jnp.zeros((16 - taken, half), jnp.bfloat16)], axis=0)
+
+    product = (k_proj.astype(jnp.float32) * v_proj.astype(jnp.float32)).astype(jnp.bfloat16)
+    product_send = lax.dynamic_slice_in_dim(product, (1 - x) * half, half, 1)
+    came = swap(jnp.concatenate([product_send, for_other], axis=0), "chan")
     taps = jnp.where(
-        pair == x, lax.dynamic_slice_in_dim(masked, quarter * taken, taken, 0), swap(for_other, "chan")
-    )
+        pair == x, lax.dynamic_slice_in_dim(masked, quarter * taken, taken, 0), came[block : block + taken]
+    ).astype(jnp.float32)
     first_rows = jnp.concatenate(
         [jnp.zeros((taken, 1), jnp.float32), taps[:, ::-1], jnp.zeros((taken, block - 1), jnp.float32)],
         axis=1,
     )
 
-    product = (k_proj.astype(jnp.float32) * v_proj.astype(jnp.float32)).astype(jnp.bfloat16)
-
-    def spread(array):
+    def spread(array, came):
         kept = lax.dynamic_slice_in_dim(array, x * half, half, 1)
-        came = swap(lax.dynamic_slice_in_dim(array, (1 - x) * half, half, 1), "chan")
         pieces = []
         for distance in range(4):
             target = z ^ distance
@@ -238,14 +249,16 @@
                 jnp.where(
                     target // 2 == x,
                     lax.dynamic_slice_in_dim(kept, start, fourth, 1),
-                    lax.dynamic_slice_in_dim(came, start, fourth, 1),
+                    lax.dynamic_slice_in_dim(came[:block], start, fourth, 1),
                 )
             )
         return [pieces[0]] + [across(pieces[distance], distance) for distance in (1, 2, 3)]
 
-    product_pieces = spread(product)
-    q_pieces = spread(q_proj)
-    got_w = across(lax.dynamic_slice_in_dim(out_weight, (1 - bit) * half, half, 1), 1)
+    product_pieces = spread(product, came)
+    q_pieces = spread(
+        q_proj, swap(lax.dynamic_slice_in_dim(q_proj, (1 - x) * half, half, 1), "chan")
+    )
+    first_rows, got_w = lax.optimization_barrier((first_rows, got_w))
     conv = causal_conv(place, first_rows, product_pieces)
 
     def mixed_partials(own, near, which):
@@ -276,8 +289,9 @@
         block, channels = q_proj.shape
         groups, taps = filters.shape
         paired = (
-            (sizes["ctx"], sizes["chan"], sizes["sub"]) == (4, 2, 2)
+            (sizes["group"], sizes["ctx"], sizes["chan"], sizes["sub"]) == (2, 4, 2, 2)
             and taps == 2 * block
+            and taps == channels // 2
             and groups % 4 == 0
             and (channels // groups) % 128 == 0
             and out_weight.shape == (channels, channels)

time: 120 us -> 107 us (0.89)
  waiting for transfers between devices: 81.9 us -> 54.5 us
  starting transfers between devices: 25.9 us -> 33.6 us
  other arithmetic: 5.19 us -> 9.42 us
  local copies, waits for them, and re-layouts: 1.62 us -> 3.34 us
    ppermute x11, waiting for transfers between devices: 47.1 us -> 19.7 us  [swap(): return lax.ppermute(value, axes, [(i, i ^ flip) for i in range(total)])]
    ppermute x11, starting transfers between devices: 9.51 us -> 14.3 us  [swap(): return lax.ppermute(value, axes, [(i, i ^ flip) for i in range(total)])]
    ppermute x10, starting transfers between devices: 16.4 us -> 19.3 us  [across(): return lax.ppermute(value, 'ctx', [(i, i ^ distance) for i in range(count)])]
    dynamic_slice x3, local copies, waits for them, and re-layouts: 1.1 us -> 2.71 us  [the longest x1 1.83 us: paired_plan(): lax.dynamic_slice_in_dim(q_proj, (1 - x) * half, half, 1)]
    select_n x2, other arithmetic: 0.41 us -> 1.98 us  [spread(): jnp.where(target // 2 == x, lax.dynamic_slice_in_dim(kept, start, fourth,...]
  transfers between devices with their start and end apart: 21 -> 21, of which waited for: 11 -> 14; matrix products, arithmetic and copies ran while one was open for 3% -> 9% of each run, Pallas kernels for 4% -> 3%
where the time goes in v2:
time: 107 us; the launch traced here: 106 us
  waiting for transfers between devices  54.5 us (51%)
  starting transfers between devices  33.6 us (31%)
  other arithmetic  9.42 us (9%)
  Pallas kernels  5.25 us (5%)
  local copies, waits for them, and re-layouts  3.34 us (3%)
    ppermute x10, waiting for transfers between devices, across(): return lax.ppermute(value, 'ctx', [(i, i ^ distance) for i in range(count)])  34.9 us
    ppermute x11, waiting for transfers between devices, swap(): return lax.ppermute(value, axes, [(i, i ^ flip) for i in range(total)])  19.7 us
    ppermute x10, starting transfers between devices, across(): return lax.ppermute(value, 'ctx', [(i, i ^ distance) for i in range(count)])  19.3 us
    ppermute x11, starting transfers between devices, swap(): return lax.ppermute(value, axes, [(i, i ^ flip) for i in range(total)])  14.3 us
    pallas_call x2, Pallas kernels, project(): pl.pallas_call(project_kernel, out_shape=jax.ShapeDtypeStruct((2, tokens...  3.67 us
  transfers between devices with their start and end apart: 21, of which 14 were waited for; matrix products, arithmetic and copies ran while one was open for 9% of the time, Pallas kernels for 3%

profile of v2, /device:TPU:0, one launch (start us, length us, event | category | flops | bytes accessed | tf_op | source)
XLA Modules:
  0.0 106.4 jit_solution(17752924858395965278)
XLA Ops:
  0.0 1.8 %constant_dynamic-slice_fusion.4 = bf16[256,512]{1,0:T(8,128)(2,1)} fusion(bf16[256,1024]{1,0:T(8,128)(2,1)} %param.6, s32[]{:T(128)S(6)} %select_n.205), kind=kLoop, calls=%fused_computation.35 | loop fusion | bytes 524292 | tf_op jit(solution)/shard_map/dynamic_slice | solution.py:259
  1.8 2.9 %collective-permute-start = (bf16[256,512]{1,0:T(8,128)(2,1)}, bf16[256,512]{1,0:T(8,128)(2,1)}, u32[]{:S(2)}, u32[]{:S(2)}) collective-permute-start(bf16[256,512]{1,0:T(8,128)(2,1)} %constant_dynamic-slice_fusion.4), channel_id=1, source_target_pairs={{0,2},{2,0},{1,3},{3,1},{4,6},{6,4},{5,7},{7,5},{8,10},{10,8},{9,1... | collective-permute-start | bytes 786440 | tf_op jit(solution)/shard_map/ppermute | solution.py:117
  8.8 2.0 %collective-permute-start.3 = (bf16[1024,256]{1,0:T(8,128)(2,1)}, bf16[1024,256]{1,0:T(8,128)(2,1)}, u32[]{:S(2)}, u32[]{:S(2)}) collective-permute-start(bf16[1024,256]{1,0:T(8,128)(2,1)} %constant_dynamic-slice_fusion), channel_id=1, source_target_pairs={{0,4},{4,0},{8,12},{12,8},{1,5},{5,1},{9,13},{13,9},{2,6},{6,2},{1... | collective-permute-start | bytes 1572872 | tf_op jit(solution)/shard_map/ppermute | solution.py:122
  13.9 2.1 %collective-permute-start.1 = (bf16[256,256]{1,0:T(8,128)(2,1)}, bf16[256,256]{1,0:T(8,128)(2,1)}, u32[]{:S(2)}, u32[]{:S(2)}) collective-permute-start(bf16[256,256]{1,0:T(8,128)(2,1)} %dynamic-slice_select_fusion.6), channel_id=1, source_target_pairs={{0,4},{4,0},{8,12},{12,8},{1,5},{5,1},{9,13},{13,9},{2,6},{6,2},{1... | collective-permute-start | bytes 393224 | tf_op jit(solution)/shard_map/ppermute | solution.py:122
  18.0 1.9 %collective-permute-start.5 = (bf16[256,256]{1,0:T(8,128)(2,1)S(1)}, bf16[256,256]{1,0:T(8,128)(2,1)S(1)}, u32[]{:S(2)}, u32[]{:S(2)}) collective-permute-start(bf16[256,256]{1,0:T(8,128)(2,1)S(1)} %get-tuple-element.19), channel_id=1, source_target_pairs={{0,4},{4,0},{8,12},{12,8},{1,5},{5,1},{9,13},{13,9},{2,6},{6,2},{1... | collective-permute-start | bytes 393224 | tf_op jit(solution)/shard_map/ppermute | solution.py:122
  19.9 2.6 %collective-permute-start.6 = (bf16[256,256]{1,0:T(8,128)(2,1)S(1)}, bf16[256,256]{1,0:T(8,128)(2,1)S(1)}, u32[]{:S(2)}, u32[]{:S(2)}) collective-permute-start(bf16[256,256]{1,0:T(8,128)(2,1)S(1)} %get-tuple-element.18), channel_id=1, source_target_pairs={{0,8},{4,12},{8,0},{12,4},{1,9},{5,13},{9,1},{13,5},{2,10},{6,14},... | collective-permute-start | bytes 393224 | tf_op jit(solution)/shard_map/ppermute | solution.py:122
  22.4 4.4 %collective-permute-done.3 = bf16[1024,256]{1,0:T(8,128)(2,1)} collective-permute-done((bf16[1024,256]{1,0:T(8,128)(2,1)}, bf16[1024,256]{1,0:T(8,128)(2,1)}, u32[]{:S(2)}, u32[]{:S(2)}) %collective-permute-start.3) | collective-permute-done | bytes 524320 | tf_op jit(solution)/shard_map/ppermute | solution.py:122
  26.8 2.0 %collective-permute-start.4 = (bf16[1024,256]{1,0:T(8,128)(2,1)}, bf16[1024,256]{1,0:T(8,128)(2,1)S(1)}, u32[]{:S(2)}, u32[]{:S(2)}) collective-permute-start(bf16[1024,256]{1,0:T(8,128)(2,1)} %collective-permute-done.3), channel_id=1, source_target_pairs={{0,16},{16,0},{1,17},{17,1},{2,18},{18,2},{3,19},{19,3},{4,20},{20... | collective-permute-start | bytes 1572872 | tf_op jit(solution)/shard_map/ppermute | solution.py:117
  30.9 1.9 %collective-permute-start.12 = (bf16[256,256]{1,0:T(8,128)(2,1)S(1)}, bf16[256,256]{1,0:T(8,128)(2,1)S(1)}, u32[]{:S(2)}, u32[]{:S(2)}) collective-permute-start(bf16[256,256]{1,0:T(8,128)(2,1)S(1)} %get-tuple-element.16), channel_id=1, source_target_pairs={{0,8},{4,12},{8,0},{12,4},{1,9},{5,13},{9,1},{13,5},{2,10},{6,14},... | collective-permute-start | bytes 393224 | tf_op jit(solution)/shard_map/ppermute | solution.py:122
  32.8 2.0 %collective-permute-start.13 = (bf16[256,256]{1,0:T(8,128)(2,1)S(1)}, bf16[256,256]{1,0:T(8,128)(2,1)S(1)}, u32[]{:S(2)}, u32[]{:S(2)}) collective-permute-start(bf16[256,256]{1,0:T(8,128)(2,1)S(1)} %get-tuple-element.15), channel_id=1, source_target_pairs={{0,12},{4,8},{8,4},{12,0},{1,13},{5,9},{9,5},{13,1},{2,14},{6,10},... | collective-permute-start | bytes 393224 | tf_op jit(solution)/shard_map/ppermute | solution.py:122
  34.9 6.7 %collective-permute-done.12 = bf16[256,256]{1,0:T(8,128)(2,1)S(1)} collective-permute-done((bf16[256,256]{1,0:T(8,128)(2,1)S(1)}, bf16[256,256]{1,0:T(8,128)(2,1)S(1)}, u32[]{:S(2)}, u32[]{:S(2)}) %collective-permute-start.12) | collective-permute-done | bytes 131104 | tf_op jit(solution)/shard_map/ppermute | solution.py:122
  41.6 2.4 %collective-permute-start.7 = (bf16[256,256]{1,0:T(8,128)(2,1)S(1)}, bf16[256,256]{1,0:T(8,128)(2,1)S(1)}, u32[]{:S(2)}, u32[]{:S(2)}) collective-permute-start(bf16[256,256]{1,0:T(8,128)(2,1)S(1)} %get-tuple-element.17), channel_id=1, source_target_pairs={{0,12},{4,8},{8,4},{12,0},{1,13},{5,9},{9,5},{13,1},{2,14},{6,10},... | collective-permute-start | bytes 393224 | tf_op jit(solution)/shard_map/ppermute | solution.py:122
  45.5 3.3 %collective-permute-done.7.refs_3_ = bf16[256,256]{1,0:T(8,128)(2,1)S(1)} collective-permute-done((bf16[256,256]{1,0:T(8,128)(2,1)S(1)}, bf16[256,256]{1,0:T(8,128)(2,1)S(1)}, u32[]{:S(2)}, u32[]{:S(2)}) %collective-permute-start.7) | collective-permute-done | bytes 131104 | tf_op jit(solution)/shard_map/ppermute | solution.py:122
  57.2 2.6 %collective-permute-done.14.refs_1_ = bf16[512,256]{1,0:T(8,128)(2,1)S(1)} collective-permute-done((bf16[512,256]{1,0:T(8,128)(2,1)S(1)}, bf16[512,256]{1,0:T(8,128)(2,1)S(1)}, u32[]{:S(2)}, u32[]{:S(2)}) %collective-permute-start.14) | collective-permute-done | bytes 262176 | tf_op jit(solution)/shard_map/ppermute | solution.py:117
  59.8 2.5 %collective-permute-start.10 = (bf16[512,256]{1,0:T(8,128)(2,1)S(1)}, bf16[512,256]{1,0:T(8,128)(2,1)S(1)}, u32[]{:S(2)}, u32[]{:S(2)}) collective-permute-start(bf16[512,256]{1,0:T(8,128)(2,1)S(1)} %bitcast.38), channel_id=1, source_target_pairs={{0,6},{2,4},{4,2},{6,0},{8,14},{10,12},{12,10},{14,8},{1,7},{3,5},... | collective-permute-start | bytes 786440 | tf_op jit(solution)/shard_map/ppermute | solution.py:117
  62.3 4.8 %collective-permute-done.15.refs_2_ = bf16[512,256]{1,0:T(8,128)(2,1)S(1)} collective-permute-done((bf16[512,256]{1,0:T(8,128)(2,1)S(1)}, bf16[512,256]{1,0:T(8,128)(2,1)S(1)}, u32[]{:S(2)}, u32[]{:S(2)}) %collective-permute-start.15) | collective-permute-done | bytes 262176 | tf_op jit(solution)/shard_map/ppermute | solution.py:117
  67.3 3.7 %collective-permute-done.8.refs_1_ = bf16[512,256]{1,0:T(8,128)(2,1)S(1)} collective-permute-done((bf16[512,256]{1,0:T(8,128)(2,1)S(1)}, bf16[512,256]{1,0:T(8,128)(2,1)S(1)}, u32[]{:S(2)}, u32[]{:S(2)}) %collective-permute-start.8) | collective-permute-done | bytes 262176 | tf_op jit(solution)/shard_map/ppermute | solution.py:117
  71.1 6.0 %collective-permute-done.9.refs_2_ = bf16[512,256]{1,0:T(8,128)(2,1)S(1)} collective-permute-done((bf16[512,256]{1,0:T(8,128)(2,1)S(1)}, bf16[512,256]{1,0:T(8,128)(2,1)S(1)}, u32[]{:S(2)}, u32[]{:S(2)}) %collective-permute-start.9) | collective-permute-done | bytes 262176 | tf_op jit(solution)/shard_map/ppermute | solution.py:117
  77.3 1.8 %shard_map.66 = bf16[2,256,512]{2,1,0:T(8,128)(2,1)S(1)} custom-call(s32[4]{0:T(128)S(1)} %pad_add_fusion.place, bf16[512,256]{1,0:T(8,128)(2,1)S(1)} %bitcast.45, bf16[512,256]{1,0:T(8,128)(2,1)S(1)} %collective-permute-done.14.refs_1_, bf16[512,256]{1,0:T(8,128)(2,1)S(1)} %collective-permute-done.15.refs_2_, ...), custom_call_target="tpu_custom_call" | custom-call | flops 1073741824 | bytes 4194304 | tf_op jit(solution)/shard_map/pallas_call | solution.py:186
  79.9 1.8 %shard_map.65 = bf16[2,256,512]{2,1,0:T(8,128)(2,1)S(1)} custom-call(s32[4]{0:T(128)S(1)} %pad_add_fusion.place, bf16[512,256]{1,0:T(8,128)(2,1)S(1)} %bitcast.40, bf16[512,256]{1,0:T(8,128)(2,1)S(1)} %collective-permute-done.8.refs_1_, bf16[512,256]{1,0:T(8,128)(2,1)S(1)} %collective-permute-done.9.refs_2_, ...), custom_call_target="tpu_custom_call" | custom-call | flops 1073741824 | bytes 4194304 | tf_op jit(solution)/shard_map/pallas_call | solution.py:186
  83.0 2.6 %collective-permute-start.18 = (bf16[256,512]{1,0:T(8,128)(2,1)S(1)}, bf16[256,512]{1,0:T(8,128)(2,1)S(1)}, u32[]{:S(2)}, u32[]{:S(2)}) collective-permute-start(bf16[256,512]{1,0:T(8,128)(2,1)S(1)} %get-tuple-element.21), channel_id=1, source_target_pairs={{0,8},{4,12},{8,0},{12,4},{1,9},{5,13},{9,1},{13,5},{2,10},{6,14},... | collective-permute-start | bytes 786440 | tf_op jit(solution)/shard_map/ppermute | solution.py:122
  85.6 4.7 %collective-permute-done.20 = bf16[256,512]{1,0:T(8,128)(2,1)S(1)} collective-permute-done((bf16[256,512]{1,0:T(8,128)(2,1)S(1)}, bf16[256,512]{1,0:T(8,128)(2,1)S(1)}, u32[]{:S(2)}, u32[]{:S(2)}) %collective-permute-start.20) | collective-permute-done | bytes 262176 | tf_op jit(solution)/shard_map/ppermute | solution.py:122
  90.3 6.6 %collective-permute-done.19 = bf16[256,512]{1,0:T(8,128)(2,1)S(1)} collective-permute-done((bf16[256,512]{1,0:T(8,128)(2,1)S(1)}, bf16[256,512]{1,0:T(8,128)(2,1)S(1)}, u32[]{:S(2)}, u32[]{:S(2)}) %collective-permute-start.19) | collective-permute-done | bytes 262176 | tf_op jit(solution)/shard_map/ppermute | solution.py:122
  96.9 8.5 %collective-permute-done.18 = bf16[256,512]{1,0:T(8,128)(2,1)S(1)} collective-permute-done((bf16[256,512]{1,0:T(8,128)(2,1)S(1)}, bf16[256,512]{1,0:T(8,128)(2,1)S(1)}, u32[]{:S(2)}, u32[]{:S(2)}) %collective-permute-start.18) | collective-permute-done | bytes 262176 | tf_op jit(solution)/shard_map/ppermute | solution.py:122
  (57 shorter events, 24.4 us)
Async XLA Ops:
  0.0 6.9 %copy-start.2 = (f32[8,512]{1,0:T(8,128)S(1)}, f32[8,512]{1,0:T(8,128)}, u32[]{:S(2)}) copy-start(f32[8,512]{1,0:T(8,128)} %param.9) | copy-start | bytes 49156
  0.0 8.0 %copy-start = (bf16[1024,1024]{1,0:T(8,128)(2,1)S(1)}, bf16[1024,1024]{1,0:T(8,128)(2,1)}, u32[]{:S(2)}) copy-start(bf16[1024,1024]{1,0:T(8,128)(2,1)} %refs_5_.3) | copy-start | bytes 6291460
  1.8 10.4 %copy-start.1 = (bf16[256,1024]{1,0:T(8,128)(2,1)S(1)}, bf16[256,1024]{1,0:T(8,128)(2,1)}, u32[]{:S(2)}) copy-start(bf16[256,1024]{1,0:T(8,128)(2,1)} %param.6) | copy-start | bytes 1572868
  1.8 10.4 %collective-permute-start = (bf16[256,512]{1,0:T(8,128)(2,1)}, bf16[256,512]{1,0:T(8,128)(2,1)}, u32[]{:S(2)}, u32[]{:S(2)}) collective-permute-start(bf16[256,512]{1,0:T(8,128)(2,1)} %constant_dynamic-slice_fusion.4), channel_id=1, source_target_pairs={{0,2},{2,0},{1,3},{3,1},{4,6},{6,4},{5,7},{7,5},{8,10},{10,8},{9,1... | collective-permute-start | bytes 786440 | tf_op jit(solution)/shard_map/ppermute | solution.py:117
  7.9 9.4 %collective-permute-start.2 = (bf16[272,512]{1,0:T(8,128)(2,1)}, bf16[272,512]{1,0:T(8,128)(2,1)S(1)}, u32[]{:S(2)}, u32[]{:S(2)}) collective-permute-start(bf16[272,512]{1,0:T(8,128)(2,1)} %maximum_maximum_fusion), channel_id=1, source_target_pairs={{0,2},{2,0},{1,3},{3,1},{4,6},{6,4},{5,7},{7,5},{8,10},{10,8},{9,1... | collective-permute-start | bytes 835592 | tf_op jit(solution)/shard_map/ppermute | solution.py:117
  8.8 18.0 %collective-permute-start.3 = (bf16[1024,256]{1,0:T(8,128)(2,1)}, bf16[1024,256]{1,0:T(8,128)(2,1)}, u32[]{:S(2)}, u32[]{:S(2)}) collective-permute-start(bf16[1024,256]{1,0:T(8,128)(2,1)} %constant_dynamic-slice_fusion), channel_id=1, source_target_pairs={{0,4},{4,0},{8,12},{12,8},{1,5},{5,1},{9,13},{13,9},{2,6},{6,2},{1... | collective-permute-start | bytes 1572872 | tf_op jit(solution)/shard_map/ppermute | solution.py:122
  13.9 15.7 %collective-permute-start.1 = (bf16[256,256]{1,0:T(8,128)(2,1)}, bf16[256,256]{1,0:T(8,128)(2,1)}, u32[]{:S(2)}, u32[]{:S(2)}) collective-permute-start(bf16[256,256]{1,0:T(8,128)(2,1)} %dynamic-slice_select_fusion.6), channel_id=1, source_target_pairs={{0,4},{4,0},{8,12},{12,8},{1,5},{5,1},{9,13},{13,9},{2,6},{6,2},{1... | collective-permute-start | bytes 393224 | tf_op jit(solution)/shard_map/ppermute | solution.py:122
  18.0 27.6 %collective-permute-start.5 = (bf16[256,256]{1,0:T(8,128)(2,1)S(1)}, bf16[256,256]{1,0:T(8,128)(2,1)S(1)}, u32[]{:S(2)}, u32[]{:S(2)}) collective-permute-start(bf16[256,256]{1,0:T(8,128)(2,1)S(1)} %get-tuple-element.19), channel_id=1, source_target_pairs={{0,4},{4,0},{8,12},{12,8},{1,5},{5,1},{9,13},{13,9},{2,6},{6,2},{1... | collective-permute-start | bytes 393224 | tf_op jit(solution)/shard_map/ppermute | solution.py:122
  19.9 25.7 %collective-permute-start.6 = (bf16[256,256]{1,0:T(8,128)(2,1)S(1)}, bf16[256,256]{1,0:T(8,128)(2,1)S(1)}, u32[]{:S(2)}, u32[]{:S(2)}) collective-permute-start(bf16[256,256]{1,0:T(8,128)(2,1)S(1)} %get-tuple-element.18), channel_id=1, source_target_pairs={{0,8},{4,12},{8,0},{12,4},{1,9},{5,13},{9,1},{13,5},{2,10},{6,14},... | collective-permute-start | bytes 393224 | tf_op jit(solution)/shard_map/ppermute | solution.py:122
  26.8 17.2 %collective-permute-start.4 = (bf16[1024,256]{1,0:T(8,128)(2,1)}, bf16[1024,256]{1,0:T(8,128)(2,1)S(1)}, u32[]{:S(2)}, u32[]{:S(2)}) collective-permute-start(bf16[1024,256]{1,0:T(8,128)(2,1)} %collective-permute-done.3), channel_id=1, source_target_pairs={{0,16},{16,0},{1,17},{17,1},{2,18},{18,2},{3,19},{19,3},{4,20},{20... | collective-permute-start | bytes 1572872 | tf_op jit(solution)/shard_map/ppermute | solution.py:117
  30.9 10.7 %collective-permute-start.12 = (bf16[256,256]{1,0:T(8,128)(2,1)S(1)}, bf16[256,256]{1,0:T(8,128)(2,1)S(1)}, u32[]{:S(2)}, u32[]{:S(2)}) collective-permute-start(bf16[256,256]{1,0:T(8,128)(2,1)S(1)} %get-tuple-element.16), channel_id=1, source_target_pairs={{0,8},{4,12},{8,0},{12,4},{1,9},{5,13},{9,1},{13,5},{2,10},{6,14},... | collective-permute-start | bytes 393224 | tf_op jit(solution)/shard_map/ppermute | solution.py:122
  32.8 11.1 %collective-permute-start.13 = (bf16[256,256]{1,0:T(8,128)(2,1)S(1)}, bf16[256,256]{1,0:T(8,128)(2,1)S(1)}, u32[]{:S(2)}, u32[]{:S(2)}) collective-permute-start(bf16[256,256]{1,0:T(8,128)(2,1)S(1)} %get-tuple-element.15), channel_id=1, source_target_pairs={{0,12},{4,8},{8,4},{12,0},{1,13},{5,9},{9,5},{13,1},{2,14},{6,10},... | collective-permute-start | bytes 393224 | tf_op jit(solution)/shard_map/ppermute | solution.py:122
  41.6 7.2 %collective-permute-start.7 = (bf16[256,256]{1,0:T(8,128)(2,1)S(1)}, bf16[256,256]{1,0:T(8,128)(2,1)S(1)}, u32[]{:S(2)}, u32[]{:S(2)}) collective-permute-start(bf16[256,256]{1,0:T(8,128)(2,1)S(1)} %get-tuple-element.17), channel_id=1, source_target_pairs={{0,12},{4,8},{8,4},{12,0},{1,13},{5,9},{9,5},{13,1},{2,14},{6,10},... | collective-permute-start | bytes 393224 | tf_op jit(solution)/shard_map/ppermute | solution.py:122
  50.5 9.2 %collective-permute-start.14 = (bf16[512,256]{1,0:T(8,128)(2,1)S(1)}, bf16[512,256]{1,0:T(8,128)(2,1)S(1)}, u32[]{:S(2)}, u32[]{:S(2)}) collective-permute-start(bf16[512,256]{1,0:T(8,128)(2,1)S(1)} %bitcast.41), channel_id=1, source_target_pairs={{0,4},{4,0},{8,12},{12,8},{1,5},{5,1},{9,13},{13,9},{2,6},{6,2},{1... | collective-permute-start | bytes 786440 | tf_op jit(solution)/shard_map/ppermute | solution.py:117
  52.3 14.8 %collective-permute-start.15 = (bf16[512,256]{1,0:T(8,128)(2,1)S(1)}, bf16[512,256]{1,0:T(8,128)(2,1)S(1)}, u32[]{:S(2)}, u32[]{:S(2)}) collective-permute-start(bf16[512,256]{1,0:T(8,128)(2,1)S(1)} %bitcast.42), channel_id=1, source_target_pairs={{0,2},{2,0},{1,3},{3,1},{4,6},{6,4},{5,7},{7,5},{8,10},{10,8},{9,1... | collective-permute-start | bytes 786440 | tf_op jit(solution)/shard_map/ppermute | solution.py:117
  53.7 13.4 %collective-permute-start.16 = (bf16[512,256]{1,0:T(8,128)(2,1)S(1)}, bf16[512,256]{1,0:T(8,128)(2,1)S(1)}, u32[]{:S(2)}, u32[]{:S(2)}) collective-permute-start(bf16[512,256]{1,0:T(8,128)(2,1)S(1)} %bitcast.43), channel_id=1, source_target_pairs={{0,6},{2,4},{4,2},{6,0},{8,14},{10,12},{12,10},{14,8},{1,7},{3,5},... | collective-permute-start | bytes 786440 | tf_op jit(solution)/shard_map/ppermute | solution.py:117
  54.1 17.0 %collective-permute-start.8 = (bf16[512,256]{1,0:T(8,128)(2,1)S(1)}, bf16[512,256]{1,0:T(8,128)(2,1)S(1)}, u32[]{:S(2)}, u32[]{:S(2)}) collective-permute-start(bf16[512,256]{1,0:T(8,128)(2,1)S(1)} %bitcast.36), channel_id=1, source_target_pairs={{0,4},{4,0},{8,12},{12,8},{1,5},{5,1},{9,13},{13,9},{2,6},{6,2},{1... | collective-permute-start | bytes 786440 | tf_op jit(solution)/shard_map/ppermute | solution.py:117
  55.8 21.3 %collective-permute-start.9 = (bf16[512,256]{1,0:T(8,128)(2,1)S(1)}, bf16[512,256]{1,0:T(8,128)(2,1)S(1)}, u32[]{:S(2)}, u32[]{:S(2)}) collective-permute-start(bf16[512,256]{1,0:T(8,128)(2,1)S(1)} %bitcast.37), channel_id=1, source_target_pairs={{0,2},{2,0},{1,3},{3,1},{4,6},{6,4},{5,7},{7,5},{8,10},{10,8},{9,1... | collective-permute-start | bytes 786440 | tf_op jit(solution)/shard_map/ppermute | solution.py:117
  59.8 17.3 %collective-permute-start.10 = (bf16[512,256]{1,0:T(8,128)(2,1)S(1)}, bf16[512,256]{1,0:T(8,128)(2,1)S(1)}, u32[]{:S(2)}, u32[]{:S(2)}) collective-permute-start(bf16[512,256]{1,0:T(8,128)(2,1)S(1)} %bitcast.38), channel_id=1, source_target_pairs={{0,6},{2,4},{4,2},{6,0},{8,14},{10,12},{12,10},{14,8},{1,7},{3,5},... | collective-permute-start | bytes 786440 | tf_op jit(solution)/shard_map/ppermute | solution.py:117
  67.2 10.1 %collective-permute-start.17 = (bf16[4,512,256]{2,1,0:T(8,128)(2,1)S(1)}, bf16[4,512,256]{2,1,0:T(8,128)(2,1)S(1)}, u32[]{:S(2)}, u32[]{:S(2)}) collective-permute-start(bf16[4,512,256]{2,1,0:T(8,128)(2,1)S(1)} %pad_maximum_fusion.1), channel_id=1, source_target_pairs={{0,1},{1,0},{2,3},{3,2},{4,5},{5,4},{6,7},{7,6},{8,9},{9,8},{10,11... | collective-permute-start | bytes 3145736 | tf_op jit(solution)/shard_map/ppermute | solution.py:117
  77.2 2.7 %collective-permute-start.11 = (bf16[4,512,256]{2,1,0:T(8,128)(2,1)S(1)}, bf16[4,512,256]{2,1,0:T(8,128)(2,1)S(1)}, u32[]{:S(2)}, u32[]{:S(2)}) collective-permute-start(bf16[4,512,256]{2,1,0:T(8,128)(2,1)S(1)} %pad_maximum_fusion), channel_id=1, source_target_pairs={{0,1},{1,0},{2,3},{3,2},{4,5},{5,4},{6,7},{7,6},{8,9},{9,8},{10,11... | collective-permute-start | bytes 3145736 | tf_op jit(solution)/shard_map/ppermute | solution.py:117
  79.2 11.1 %collective-permute-start.20 = (bf16[256,512]{1,0:T(8,128)(2,1)S(1)}, bf16[256,512]{1,0:T(8,128)(2,1)S(1)}, u32[]{:S(2)}, u32[]{:S(2)}) collective-permute-start(bf16[256,512]{1,0:T(8,128)(2,1)S(1)} %get-tuple-element.22), channel_id=1, source_target_pairs={{0,12},{4,8},{8,4},{12,0},{1,13},{5,9},{9,5},{13,1},{2,14},{6,10},... | collective-permute-start | bytes 786440 | tf_op jit(solution)/shard_map/ppermute | solution.py:122
  81.8 15.1 %collective-permute-start.19 = (bf16[256,512]{1,0:T(8,128)(2,1)S(1)}, bf16[256,512]{1,0:T(8,128)(2,1)S(1)}, u32[]{:S(2)}, u32[]{:S(2)}) collective-permute-start(bf16[256,512]{1,0:T(8,128)(2,1)S(1)} %slice_bitcast_fusion.1), channel_id=1, source_target_pairs={{0,4},{4,0},{8,12},{12,8},{1,5},{5,1},{9,13},{13,9},{2,6},{6,2},{1... | collective-permute-start | bytes 786440 | tf_op jit(solution)/shard_map/ppermute | solution.py:122
  83.0 22.4 %collective-permute-start.18 = (bf16[256,512]{1,0:T(8,128)(2,1)S(1)}, bf16[256,512]{1,0:T(8,128)(2,1)S(1)}, u32[]{:S(2)}, u32[]{:S(2)}) collective-permute-start(bf16[256,512]{1,0:T(8,128)(2,1)S(1)} %get-tuple-element.21), channel_id=1, source_target_pairs={{0,8},{4,12},{8,0},{12,4},{1,9},{5,13},{9,1},{13,5},{2,10},{6,14},... | collective-permute-start | bytes 786440 | tf_op jit(solution)/shard_map/ppermute | solution.py:122

commit v3 on v1

--- a/solution.py
+++ b/solution.py
@@ -122,38 +122,47 @@
     return lax.ppermute(value, "ctx", [(i, i ^ distance) for i in range(count)])
 
 
-def conv_kernel(place, row_ref, *refs):
-    pieces, conv_ref, padded = refs[:4], refs[4], refs[5]
-    block, width = pieces[0].shape
+def gated_kernel(place, row_ref, *refs):
+    pieces, outs, padded, gates = refs[:4], refs[4:6], refs[6], refs[7]
+    _, block, width = pieces[0].shape
     groups, span = row_ref.shape
     per_group = width // groups
     padded[0] = jnp.zeros((block, width), padded.dtype)
     padded[1] = jnp.zeros((block, width), padded.dtype)
     for distance in range(4):
-        padded[2 + (place[0] ^ distance)] = pieces[distance][...]
+        token = place[0] ^ distance
+        padded[2 + token] = pieces[distance][0]
+        gates[token] = pieces[distance][1]
     for group in range(groups):
         columns = pl.ds(group * per_group, per_group)
         rows = jnp.broadcast_to(row_ref[group : group + 1, :], (block, span))
         toeplitz = pltpu.roll(rows, 0, 1, stride=1, stride_axis=0).astype(jnp.bfloat16)
-        for token in range(4):
-            source = jnp.concatenate([padded[token + step, :, columns] for step in range(3)], axis=0)
-            conv_ref[token, :, columns] = jnp.dot(
-                toeplitz, source, preferred_element_type=jnp.float32
-            )
-
-
-def causal_conv(place, first_rows, pieces):
-    block, width = pieces[0].shape
+        for out_ref, pair in zip(outs, (1 - place[4], place[4])):
+            for part in range(2):
+                token = 2 * pair + part
+                source = jnp.concatenate(
+                    [padded[token + step, :, columns] for step in range(3)], axis=0
+                )
+                conv = jnp.dot(toeplitz, source, preferred_element_type=jnp.float32)
+                gated = gates[token, :, columns].astype(jnp.float32) * conv
+                out_ref[pl.ds(part * block, block), columns] = gated.astype(out_ref.dtype)
+
+
+def gated_conv(place, first_rows, pieces):
+    _, block, width = pieces[0].shape
     return pl.pallas_call(
-        conv_kernel,
-        out_shape=jax.ShapeDtypeStruct((4, block, width), jnp.float32),
+        gated_kernel,
+        out_shape=[jax.ShapeDtypeStruct((2 * block, width), jnp.bfloat16)] * 2,
         grid_spec=pltpu.PrefetchScalarGridSpec(
             num_scalar_prefetch=1,
             grid=(1,),
             in_specs=[pl.BlockSpec(first_rows.shape, lambda i, s: (0, 0))]
-            + [pl.BlockSpec((block, width), lambda i, s: (0, 0))] * 4,
-            out_specs=pl.BlockSpec((4, block, width), lambda i, s: (0, 0, 0)),
-            scratch_shapes=[pltpu.VMEM((6, block, width), jnp.bfloat16)],
+            + [pl.BlockSpec((2, block, width), lambda i, s: (0, 0, 0))] * 4,
+            out_specs=[pl.BlockSpec((2 * block, width), lambda i, s: (0, 0))] * 2,
+            scratch_shapes=[
+                pltpu.VMEM((6, block, width), jnp.bfloat16),
+                pltpu.VMEM((4, block, width), jnp.bfloat16),
+            ],
         ),
         compiler_params=pltpu.CompilerParams(vmem_limit_bytes=32 * 2**20),
         cost_estimate=pl.CostEstimate(
@@ -163,104 +172,118 @@
 
 
 def project_kernel(place, *refs):
-    mine, other, own_w, got_w, out_ref = refs[:4], refs[4], refs[5], refs[6], refs[7]
-    bit, quarter, same = place[1], place[2], place[3]
+    mine, other, own_w, near_w, far_w, out_ref = refs[:4], *refs[4:9]
+    bit, quarter, same, group = place[1], place[2], place[3], place[5]
     tokens, width = mine[0].shape
     half = tokens // 2
+    columns = near_w.shape[1]
     for part in range(2):
         rows = pl.ds(part * half, half)
-        total = jnp.zeros((half, out_ref.shape[2]), jnp.float32)
-        for flip in range(4):
-            here, there = mine[flip][rows, :], other[flip, rows, :]
-            first = jnp.where(same == 1, here, there)
-            second = jnp.where(same == 1, there, here)
-            block = pl.ds(pl.multiple_of((quarter ^ flip) * width, width), width)
-            total += jnp.dot(first, own_w[block, :], preferred_element_type=jnp.float32)
-            total += jnp.dot(second, got_w[block, :], preferred_element_type=jnp.float32)
-        out_ref[part ^ bit] = total.astype(out_ref.dtype)
-
-
-def project(place, mine, other, out_weight, got_w):
+        for got_w, index in ((near_w, group), (far_w, 1 - group)):
+            place_of = pl.ds(pl.multiple_of(index * columns, columns), columns)
+            total = jnp.zeros((half, columns), jnp.float32)
+            for flip in range(4):
+                here, there = mine[flip][rows, :], other[flip, rows, :]
+                first = jnp.where(same == 1, here, there)
+                second = jnp.where(same == 1, there, here)
+                block = pl.ds(pl.multiple_of((quarter ^ flip) * width, width), width)
+                total += jnp.dot(first, own_w[block, place_of], preferred_element_type=jnp.float32)
+                total += jnp.dot(second, got_w[block, :], preferred_element_type=jnp.float32)
+            out_ref[part ^ bit, :, place_of] = total.astype(out_ref.dtype)
+
+
+def project(place, mine, other, out_weight, near_w, far_w):
     tokens, width = mine[0].shape
-    depth, columns = got_w.shape
+    depth, columns = near_w.shape
     return pl.pallas_call(
         project_kernel,
-        out_shape=jax.ShapeDtypeStruct((2, tokens // 2, columns), jnp.bfloat16),
+        out_shape=jax.ShapeDtypeStruct((2, tokens // 2, 2 * columns), jnp.bfloat16),
         grid_spec=pltpu.PrefetchScalarGridSpec(
             num_scalar_prefetch=1,
             grid=(1,),
             in_specs=[pl.BlockSpec((tokens, width), lambda i, s: (0, 0))] * 4
             + [
                 pl.BlockSpec((4, tokens, width), lambda i, s: (0, 0, 0)),
-                pl.BlockSpec((depth, columns), lambda i, s: (0, s[1])),
+                pl.BlockSpec((depth, 2 * columns), lambda i, s: (0, s[1])),
+                pl.BlockSpec((depth, columns), lambda i, s: (0, 0)),
                 pl.BlockSpec((depth, columns), lambda i, s: (0, 0)),
             ],
-            out_specs=pl.BlockSpec((2, tokens // 2, columns), lambda i, s: (0, 0, 0)),
+            out_specs=pl.BlockSpec((2, tokens // 2, 2 * columns), lambda i, s: (0, 0, 0)),
         ),
         compiler_params=pltpu.CompilerParams(vmem_limit_bytes=32 * 2**20),
         cost_estimate=pl.CostEstimate(
-            flops=2 * tokens * 8 * width * columns, bytes_accessed=2**22, transcendentals=0
+            flops=2 * tokens * 8 * width * 2 * columns, bytes_accessed=2**22, transcendentals=0
         ),
-    )(place, *mine, other, out_weight, got_w)
+    )(place, *mine, other, out_weight, near_w, far_w)
 
 
 def paired_plan(q_proj, k_proj, v_proj, filters, filter_blocks, out_weight):
     block, channels = q_proj.shape
     groups = filters.shape[0]
-    z, x, c = lax.axis_index("ctx"), lax.axis_index("chan"), lax.axis_index("sub")
+    g, z = lax.axis_index("group"), lax.axis_index("ctx")
+    x, c = lax.axis_index("chan"), lax.axis_index("sub")
     pair, bit = z // 2, z % 2
     quarter = 2 * x + bit
     half, fourth = channels // 2, channels // 4
-    place = jnp.stack([z, bit, quarter, (c == bit).astype(jnp.int32)]).astype(jnp.int32)
+    place = jnp.stack([z, bit, quarter, (c == bit).astype(jnp.int32), pair, g]).astype(jnp.int32)
+
+    def packed(quarter_index):
+        k, v, q = (
+            lax.dynamic_slice_in_dim(array, quarter_index * fourth, fourth, 1)
+            for array in (k_proj, v_proj, q_proj)
+        )
+        product = (k.astype(jnp.float32) * v.astype(jnp.float32)).astype(jnp.bfloat16)
+        return jnp.stack([product, q])
 
     tap_index = jnp.arange(filters.shape[1], dtype=jnp.int32)
     masked = jnp.where(tap_index[None, :] < filter_blocks[:, None] * block, filters, 0.0)
+    masked = masked.astype(jnp.bfloat16)
     taken = groups // 4
     for_other = lax.dynamic_slice_in_dim(masked, (2 * (1 - x) + bit) * taken, taken, 0)
+    filter_rows = for_other.reshape(-1, fourth)
+    filter_rows = jnp.concatenate(
+        [filter_rows, jnp.zeros((16 - filter_rows.shape[0], fourth), jnp.bfloat16)], axis=0
+    )
+
+    same_send = packed(2 * (1 - x) + bit)
+    flip_send = jnp.concatenate(
+        [packed(2 * (1 - x) + 1 - bit).reshape(2 * block, fourth), filter_rows], axis=0
+    )
+    same_came = swap(same_send, "chan")
+    flip_came = swap(flip_send, "chan")
+    same_own, flip_own = packed(2 * x + bit), packed(2 * x + 1 - bit)
+
+    other_cols = (1 - bit) * half + g * fourth
+    w_near = across(lax.dynamic_slice_in_dim(out_weight, other_cols, fourth, 1), 1)
+    w_far = swap(w_near, "group")
+
+    inside = pair == x
+    piece_2 = across(jnp.where(inside, same_came, same_own), 2)
+    piece_0 = jnp.where(inside, same_own, same_came)
+    flip_came_pieces = flip_came[: 2 * block].reshape(2, block, fourth)
+    piece_3 = across(jnp.where(inside, flip_came_pieces, flip_own), 3)
+    piece_1 = across(jnp.where(inside, flip_own, flip_came_pieces), 1)
+
     taps = jnp.where(
-        pair == x, lax.dynamic_slice_in_dim(masked, quarter * taken, taken, 0), swap(for_other, "chan")
-    )
+        inside,
+        lax.dynamic_slice_in_dim(masked, quarter * taken, taken, 0),
+        flip_came[2 * block :].reshape(-1)[: taken * filters.shape[1]].reshape(taken, -1),
+    ).astype(jnp.float32)
     first_rows = jnp.concatenate(
         [jnp.zeros((taken, 1), jnp.float32), taps[:, ::-1], jnp.zeros((taken, block - 1), jnp.float32)],
         axis=1,
     )
-
-    product = (k_proj.astype(jnp.float32) * v_proj.astype(jnp.float32)).astype(jnp.bfloat16)
-
-    def spread(array):
-        kept = lax.dynamic_slice_in_dim(array, x * half, half, 1)
-        came = swap(lax.dynamic_slice_in_dim(array, (1 - x) * half, half, 1), "chan")
-        pieces = []
-        for distance in range(4):
-            target = z ^ distance
-            start = (target % 2) * fourth
-            pieces.append(
-                jnp.where(
-                    target // 2 == x,
-                    lax.dynamic_slice_in_dim(kept, start, fourth, 1),
-                    lax.dynamic_slice_in_dim(came, start, fourth, 1),
-                )
-            )
-        return [pieces[0]] + [across(pieces[distance], distance) for distance in (1, 2, 3)]
-
-    product_pieces = spread(product)
-    q_pieces = spread(q_proj)
-    got_w = across(lax.dynamic_slice_in_dim(out_weight, (1 - bit) * half, half, 1), 1)
-    conv = causal_conv(place, first_rows, product_pieces)
-
-    def mixed_partials(own, near, which):
-        low = jnp.where(bit == 0, own, near)
-        high = jnp.where(bit == 0, near, own)
-        gate = jnp.stack([low, high])
-        signal = lax.dynamic_slice_in_dim(conv, 2 * which, 2, 0)
-        gated = (gate.astype(jnp.float32) * signal).astype(jnp.bfloat16).reshape(2 * block, fourth)
+    first_rows, w_near, w_far = lax.optimization_barrier((first_rows, w_near, w_far))
+    gated_far, gated_near = gated_conv(place, first_rows, (piece_0, piece_1, piece_2, piece_3))
+
+    def partials(gated):
         mine = [gated, swap(gated, "ctx"), swap(gated, "chan"), swap(gated, "ctx", "chan")]
         other = swap(jnp.stack(mine), "sub")
-        return project(place, mine, other, out_weight, got_w)
-
-    far = mixed_partials(q_pieces[2], q_pieces[3], 1 - pair)
+        return project(place, mine, other, out_weight, w_near, w_far)
+
+    far = partials(gated_far)
     far_own, far_near = across(far[0], 2), across(far[1], 3)
-    close = mixed_partials(q_pieces[0], q_pieces[1], pair)
+    close = partials(gated_near)
     near = across(close[1], 1)
     this_half = close[0].astype(jnp.float32) + far_own.astype(jnp.float32)
     that_half = near.astype(jnp.float32) + far_near.astype(jnp.float32)
@@ -276,8 +299,9 @@
         block, channels = q_proj.shape
         groups, taps = filters.shape
         paired = (
-            (sizes["ctx"], sizes["chan"], sizes["sub"]) == (4, 2, 2)
+            (sizes["group"], sizes["ctx"], sizes["chan"], sizes["sub"]) == (2, 4, 2, 2)
             and taps == 2 * block
+            and taps == channels // 2
             and groups % 4 == 0
             and (channels // groups) % 128 == 0
             and out_weight.shape == (channels, channels)

time: 120 us -> 94.7 us (0.79)
  waiting for transfers between devices: 81.9 us -> 54.3 us
  other arithmetic: 5.19 us -> 2 us
  local copies, waits for them, and re-layouts: 1.62 us -> 4.65 us
  starting transfers between devices: 25.9 us -> 28 us
    ppermute x11, waiting for transfers between devices: 47.1 us -> 29.4 us  [swap(): return lax.ppermute(value, axes, [(i, i ^ flip) for i in range(total)])]
    ppermute x10 -> x7, waiting for transfers between devices: 34.8 us -> 24.9 us  [across(): return lax.ppermute(value, 'ctx', [(i, i ^ distance) for i in range(count)])]
    ppermute x11, starting transfers between devices: 9.51 us -> 11.7 us  [swap(): return lax.ppermute(value, axes, [(i, i ^ flip) for i in range(total)])]
    slice x0 -> x2, local copies, waits for them, and re-layouts: none -> 1.63 us  [the longest x1 0.97 us: paired_plan(): flip_came_pieces = flip_came[:2 * block].reshape(2, block, fourth)]
    convert_element_type x2, other arithmetic: 1.55 us -> 0.08 us  [the longest x1 0.07 us: paired_plan(): masked = masked.astype(jnp.bfloat16)]
    another operation x0 -> x2, local copies, waits for them, and re-layouts: none -> 1.22 us  [the longest x1 1.13 us: packed(): return jnp.stack([product, q])]
    ppermute x10 -> x7, starting transfers between devices: 16.4 us -> 16.2 us  [across(): return lax.ppermute(value, 'ctx', [(i, i ^ distance) for i in range(count)])]
  transfers between devices with their start and end apart: 21 -> 18, of which waited for: 11 -> 11; matrix products, arithmetic and copies ran while one was open for 3% -> 5% of each run, Pallas kernels for 4% -> 4%
where the time goes in v3:
time: 94.7 us; the launch traced here: 94.5 us
  waiting for transfers between devices  54.3 us (57%)
  starting transfers between devices  28 us (30%)
  Pallas kernels  5.33 us (6%)
  local copies, waits for them, and re-layouts  4.65 us (5%)
  other arithmetic  2 us (2%)
    ppermute x11, waiting for transfers between devices, swap(): return lax.ppermute(value, axes, [(i, i ^ flip) for i in range(total)])  29.4 us
    ppermute x7, waiting for transfers between devices, across(): return lax.ppermute(value, 'ctx', [(i, i ^ distance) for i in range(count)])  24.9 us
    ppermute x7, starting transfers between devices, across(): return lax.ppermute(value, 'ctx', [(i, i ^ distance) for i in range(count)])  16.2 us
    ppermute x11, starting transfers between devices, swap(): return lax.ppermute(value, axes, [(i, i ^ flip) for i in range(total)])  11.7 us
    pallas_call x2, Pallas kernels, project(): pl.pallas_call(project_kernel, out_shape=jax.ShapeDtypeStruct((2, tokens...  3.75 us
  transfers between devices with their start and end apart: 18, of which 11 were waited for; matrix products, arithmetic and copies ran while one was open for 5% of the time, Pallas kernels for 4%

profile of v3, /device:TPU:0, one launch (start us, length us, event | category | flops | bytes accessed | tf_op | source)
XLA Modules:
  0.0 94.5 jit_solution(14363841720688665004)
XLA Ops:
  1.2 3.1 %collective-permute-start.1 = (bf16[1024,256]{1,0:T(8,128)(2,1)S(1)}, bf16[1024,256]{1,0:T(8,128)(2,1)S(1)}, u32[]{:S(2)}, u32[]{:S(2)}) collective-permute-start(bf16[1024,256]{1,0:T(8,128)(2,1)S(1)} %constant_dynamic-slice_fusion), channel_id=1, source_target_pairs={{0,4},{4,0},{8,12},{12,8},{1,5},{5,1},{9,13},{13,9},{2,6},{6,2},{1... | collective-permute-start | bytes 1572872 | tf_op jit(solution)/shard_map/ppermute | solution.py:122
  5.8 1.6 %collective-permute-start.3 = (bf16[2,256,256]{2,1,0:T(8,128)(2,1)S(1)}, bf16[2,256,256]{2,1,0:T(8,128)(2,1)S(1)}, u32[]{:S(2)}, u32[]{:S(2)}) collective-permute-start(bf16[2,256,256]{2,1,0:T(8,128)(2,1)S(1)} %pad_maximum_fusion.5), channel_id=1, source_target_pairs={{0,2},{2,0},{1,3},{3,1},{4,6},{6,4},{5,7},{7,5},{8,10},{10,8},{9,1... | collective-permute-start | bytes 786440 | tf_op jit(solution)/shard_map/ppermute | solution.py:117
  8.5 6.6 %collective-permute-done.3 = bf16[2,256,256]{2,1,0:T(8,128)(2,1)S(1)} collective-permute-done((bf16[2,256,256]{2,1,0:T(8,128)(2,1)S(1)}, bf16[2,256,256]{2,1,0:T(8,128)(2,1)S(1)}, u32[]{:S(2)}, u32[]{:S(2)}) %collective-permute-start.3) | collective-permute-done | bytes 262176 | tf_op jit(solution)/shard_map/ppermute | solution.py:117
  15.1 2.7 %collective-permute-start.5 = (bf16[2,256,256]{2,1,0:T(8,128)(2,1)S(1)}, bf16[2,256,256]{2,1,0:T(8,128)(2,1)S(1)}, u32[]{:S(2)}, u32[]{:S(2)}) collective-permute-start(bf16[2,256,256]{2,1,0:T(8,128)(2,1)S(1)} %get-tuple-element.25), channel_id=1, source_target_pairs={{0,8},{4,12},{8,0},{12,4},{1,9},{5,13},{9,1},{13,5},{2,10},{6,14},... | collective-permute-start | bytes 786440 | tf_op jit(solution)/shard_map/ppermute | solution.py:122
  17.7 1.7 %collective-permute-done = bf16[528,256]{1,0:T(8,128)(2,1)} collective-permute-done((bf16[528,256]{1,0:T(8,128)(2,1)S(1)}, bf16[528,256]{1,0:T(8,128)(2,1)}, u32[]{:S(2)}, u32[]{:S(2)}) %collective-permute-start) | collective-permute-done | bytes 270368 | tf_op jit(solution)/shard_map/ppermute | solution.py:117
  20.5 1.6 %collective-permute-start.2 = (bf16[1024,256]{1,0:T(8,128)(2,1)S(1)}, bf16[1024,256]{1,0:T(8,128)(2,1)S(1)}, u32[]{:S(2)}, u32[]{:S(2)}) collective-permute-start(bf16[1024,256]{1,0:T(8,128)(2,1)S(1)} %collective-permute-done.1.refs_6_), channel_id=1, source_target_pairs={{0,16},{16,0},{1,17},{17,1},{2,18},{18,2},{3,19},{19,3},{4,20},{20... | collective-permute-start | bytes 1572872 | tf_op jit(solution)/shard_map/ppermute | solution.py:117
  23.2 3.6 %collective-permute-start.6 = (bf16[2,256,256]{2,1,0:T(8,128)(2,1)S(1)}, bf16[2,256,256]{2,1,0:T(8,128)(2,1)S(1)}, u32[]{:S(2)}, u32[]{:S(2)}) collective-permute-start(bf16[2,256,256]{2,1,0:T(8,128)(2,1)S(1)} %get-tuple-element.23), channel_id=1, source_target_pairs={{0,12},{4,8},{8,4},{12,0},{1,13},{5,9},{9,5},{13,1},{2,14},{6,10},... | collective-permute-start | bytes 786440 | tf_op jit(solution)/shard_map/ppermute | solution.py:122
  27.3 5.7 %collective-permute-done.2.refs_7_ = bf16[1024,256]{1,0:T(8,128)(2,1)S(1)} collective-permute-done((bf16[1024,256]{1,0:T(8,128)(2,1)S(1)}, bf16[1024,256]{1,0:T(8,128)(2,1)S(1)}, u32[]{:S(2)}, u32[]{:S(2)}) %collective-permute-start.2) | collective-permute-done | bytes 524320 | tf_op jit(solution)/shard_map/ppermute | solution.py:117
  33.0 5.0 %collective-permute-done.4.refs_1_ = bf16[2,256,256]{2,1,0:T(8,128)(2,1)S(1)} collective-permute-done((bf16[2,256,256]{2,1,0:T(8,128)(2,1)S(1)}, bf16[2,256,256]{2,1,0:T(8,128)(2,1)S(1)}, u32[]{:S(2)}, u32[]{:S(2)}) %collective-permute-start.4) | collective-permute-done | bytes 262176 | tf_op jit(solution)/shard_map/ppermute | solution.py:122
  38.0 1.6 %shard_map.64 = (bf16[512,256]{1,0:T(8,128)(2,1)S(1)}, bf16[512,256]{1,0:T(8,128)(2,1)S(1)}) custom-call(s32[6]{0:T(128)S(1)} %stack.97.place, f32[2,768]{1,0:T(2,128)S(1)} %maximum_maximum_fusion.1.row_ref, bf16[2,256,256]{2,1,0:T(8,128)(2,1)S(1)} %get-tuple-element.26.refs_0_, bf16[2,256,256]{2,1,0:T(8,128)(2,1)S(1)} %collective-permute-done.4.refs_1_, ...), custom_call_target="tpu_custom_call" | custom-call | flops 402653184 | bytes 2097152 | tf_op jit(solution)/shard_map/pallas_call | solution.py:153
  40.6 1.5 %collective-permute-start.12 = (bf16[512,256]{1,0:T(8,128)(2,1)S(1)}, bf16[512,256]{1,0:T(8,128)(2,1)S(1)}, u32[]{:S(2)}, u32[]{:S(2)}) collective-permute-start(bf16[512,256]{1,0:T(8,128)(2,1)S(1)} %get-tuple-element.14.refs_0_), channel_id=1, source_target_pairs={{0,2},{2,0},{1,3},{3,1},{4,6},{6,4},{5,7},{7,5},{8,10},{10,8},{9,1... | collective-permute-start | bytes 786440 | tf_op jit(solution)/shard_map/ppermute | solution.py:117
  44.1 1.5 %collective-permute-start.8 = (bf16[512,256]{1,0:T(8,128)(2,1)S(1)}, bf16[512,256]{1,0:T(8,128)(2,1)S(1)}, u32[]{:S(2)}, u32[]{:S(2)}) collective-permute-start(bf16[512,256]{1,0:T(8,128)(2,1)S(1)} %get-tuple-element.11.refs_0_), channel_id=1, source_target_pairs={{0,2},{2,0},{1,3},{3,1},{4,6},{6,4},{5,7},{7,5},{8,10},{10,8},{9,1... | collective-permute-start | bytes 786440 | tf_op jit(solution)/shard_map/ppermute | solution.py:117
  45.6 3.3 %collective-permute-done.11.refs_1_ = bf16[512,256]{1,0:T(8,128)(2,1)S(1)} collective-permute-done((bf16[512,256]{1,0:T(8,128)(2,1)S(1)}, bf16[512,256]{1,0:T(8,128)(2,1)S(1)}, u32[]{:S(2)}, u32[]{:S(2)}) %collective-permute-start.11) | collective-permute-done | bytes 262176 | tf_op jit(solution)/shard_map/ppermute | solution.py:117
  48.9 1.9 %collective-permute-start.9 = (bf16[512,256]{1,0:T(8,128)(2,1)S(1)}, bf16[512,256]{1,0:T(8,128)(2,1)S(1)}, u32[]{:S(2)}, u32[]{:S(2)}) collective-permute-start(bf16[512,256]{1,0:T(8,128)(2,1)S(1)} %get-tuple-element.11.refs_0_), channel_id=1, source_target_pairs={{0,6},{2,4},{4,2},{6,0},{8,14},{10,12},{12,10},{14,8},{1,7},{3,5},... | collective-permute-start | bytes 786440 | tf_op jit(solution)/shard_map/ppermute | solution.py:117
  50.7 4.9 %collective-permute-done.12.refs_2_ = bf16[512,256]{1,0:T(8,128)(2,1)S(1)} collective-permute-done((bf16[512,256]{1,0:T(8,128)(2,1)S(1)}, bf16[512,256]{1,0:T(8,128)(2,1)S(1)}, u32[]{:S(2)}, u32[]{:S(2)}) %collective-permute-start.12) | collective-permute-done | bytes 262176 | tf_op jit(solution)/shard_map/ppermute | solution.py:117
  55.8 3.0 %collective-permute-done.7.refs_1_ = bf16[512,256]{1,0:T(8,128)(2,1)S(1)} collective-permute-done((bf16[512,256]{1,0:T(8,128)(2,1)S(1)}, bf16[512,256]{1,0:T(8,128)(2,1)S(1)}, u32[]{:S(2)}, u32[]{:S(2)}) %collective-permute-start.7) | collective-permute-done | bytes 262176 | tf_op jit(solution)/shard_map/ppermute | solution.py:117
  58.8 4.2 %collective-permute-done.8.refs_2_ = bf16[512,256]{1,0:T(8,128)(2,1)S(1)} collective-permute-done((bf16[512,256]{1,0:T(8,128)(2,1)S(1)}, bf16[512,256]{1,0:T(8,128)(2,1)S(1)}, u32[]{:S(2)}, u32[]{:S(2)}) %collective-permute-start.8) | collective-permute-done | bytes 262176 | tf_op jit(solution)/shard_map/ppermute | solution.py:117
  63.3 1.9 %shard_map.66 = bf16[2,256,512]{2,1,0:T(8,128)(2,1)S(1)} custom-call(s32[6]{0:T(128)S(1)} %stack.97.place, bf16[512,256]{1,0:T(8,128)(2,1)S(1)} %get-tuple-element.14.refs_0_, bf16[512,256]{1,0:T(8,128)(2,1)S(1)} %collective-permute-done.11.refs_1_, bf16[512,256]{1,0:T(8,128)(2,1)S(1)} %collective-permute-done.12.refs_2_, ...), custom_call_target="tpu_custom_call" | custom-call | flops 1073741824 | bytes 4194304 | tf_op jit(solution)/shard_map/pallas_call | solution.py:198
  65.2 5.2 %collective-permute-start.17 = (bf16[256,512]{1,0:T(8,128)(2,1)S(1)}, bf16[256,512]{1,0:T(8,128)(2,1)S(1)}, u32[]{:S(2)}, u32[]{:S(2)}) collective-permute-start(bf16[256,512]{1,0:T(8,128)(2,1)S(1)} %get-tuple-element.22), channel_id=1, source_target_pairs={{0,12},{4,8},{8,4},{12,0},{1,13},{5,9},{9,5},{13,1},{2,14},{6,10},... | collective-permute-start | bytes 786440 | tf_op jit(solution)/shard_map/ppermute | solution.py:122
  70.4 1.9 %shard_map.65 = bf16[2,256,512]{2,1,0:T(8,128)(2,1)S(1)} custom-call(s32[6]{0:T(128)S(1)} %stack.97.place, bf16[512,256]{1,0:T(8,128)(2,1)S(1)} %get-tuple-element.11.refs_0_, bf16[512,256]{1,0:T(8,128)(2,1)S(1)} %collective-permute-done.7.refs_1_, bf16[512,256]{1,0:T(8,128)(2,1)S(1)} %collective-permute-done.8.refs_2_, ...), custom_call_target="tpu_custom_call" | custom-call | flops 1073741824 | bytes 4194304 | tf_op jit(solution)/shard_map/pallas_call | solution.py:198
  72.4 1.2 %collective-permute-start.15 = (bf16[256,512]{1,0:T(8,128)(2,1)S(1)}, bf16[256,512]{1,0:T(8,128)(2,1)S(1)}, u32[]{:S(2)}, u32[]{:S(2)}) collective-permute-start(bf16[256,512]{1,0:T(8,128)(2,1)S(1)} %get-tuple-element.21), channel_id=1, source_target_pairs={{0,8},{4,12},{8,0},{12,4},{1,9},{5,13},{9,1},{13,5},{2,10},{6,14},... | collective-permute-start | bytes 786440 | tf_op jit(solution)/shard_map/ppermute | solution.py:122
  73.6 4.0 %collective-permute-done.17 = bf16[256,512]{1,0:T(8,128)(2,1)S(1)} collective-permute-done((bf16[256,512]{1,0:T(8,128)(2,1)S(1)}, bf16[256,512]{1,0:T(8,128)(2,1)S(1)}, u32[]{:S(2)}, u32[]{:S(2)}) %collective-permute-start.17) | collective-permute-done | bytes 262176 | tf_op jit(solution)/shard_map/ppermute | solution.py:122
  77.6 6.3 %collective-permute-done.16 = bf16[256,512]{1,0:T(8,128)(2,1)S(1)} collective-permute-done((bf16[256,512]{1,0:T(8,128)(2,1)S(1)}, bf16[256,512]{1,0:T(8,128)(2,1)S(1)}, u32[]{:S(2)}, u32[]{:S(2)}) %collective-permute-start.16) | collective-permute-done | bytes 262176 | tf_op jit(solution)/shard_map/ppermute | solution.py:122
  83.9 9.6 %collective-permute-done.15 = bf16[256,512]{1,0:T(8,128)(2,1)S(1)} collective-permute-done((bf16[256,512]{1,0:T(8,128)(2,1)S(1)}, bf16[256,512]{1,0:T(8,128)(2,1)S(1)}, u32[]{:S(2)}, u32[]{:S(2)}) %collective-permute-start.15) | collective-permute-done | bytes 262176 | tf_op jit(solution)/shard_map/ppermute | solution.py:122
  (55 shorter events, 10.9 us)
Async XLA Ops:
  0.0 5.4 %copy-start.1 = (bf16[256,1024]{1,0:T(8,128)(2,1)S(1)}, bf16[256,1024]{1,0:T(8,128)(2,1)}, u32[]{:S(2)}) copy-start(bf16[256,1024]{1,0:T(8,128)(2,1)} %param.8) | copy-start | bytes 1572868
  0.0 5.4 %copy-start.2 = (bf16[256,1024]{1,0:T(8,128)(2,1)S(1)}, bf16[256,1024]{1,0:T(8,128)(2,1)}, u32[]{:S(2)}) copy-start(bf16[256,1024]{1,0:T(8,128)(2,1)} %param.7) | copy-start | bytes 1572868
  0.0 7.3 %copy-start.4 = (s32[8]{0:T(128)S(1)}, s32[8]{0:T(128)}, u32[]{:S(2)}) copy-start(s32[8]{0:T(128)} %param.10) | copy-start | bytes 100
  0.0 7.3 %copy-start.3 = (f32[8,512]{1,0:T(8,128)S(1)}, f32[8,512]{1,0:T(8,128)}, u32[]{:S(2)}) copy-start(f32[8,512]{1,0:T(8,128)} %param.9) | copy-start | bytes 49156
  1.2 19.3 %collective-permute-start.1 = (bf16[1024,256]{1,0:T(8,128)(2,1)S(1)}, bf16[1024,256]{1,0:T(8,128)(2,1)S(1)}, u32[]{:S(2)}, u32[]{:S(2)}) collective-permute-start(bf16[1024,256]{1,0:T(8,128)(2,1)S(1)} %constant_dynamic-slice_fusion), channel_id=1, source_target_pairs={{0,4},{4,0},{8,12},{12,8},{1,5},{5,1},{9,13},{13,9},{2,6},{6,2},{1... | collective-permute-start | bytes 1572872 | tf_op jit(solution)/shard_map/ppermute | solution.py:122
  5.8 9.3 %collective-permute-start.3 = (bf16[2,256,256]{2,1,0:T(8,128)(2,1)S(1)}, bf16[2,256,256]{2,1,0:T(8,128)(2,1)S(1)}, u32[]{:S(2)}, u32[]{:S(2)}) collective-permute-start(bf16[2,256,256]{2,1,0:T(8,128)(2,1)S(1)} %pad_maximum_fusion.5), channel_id=1, source_target_pairs={{0,2},{2,0},{1,3},{3,1},{4,6},{6,4},{5,7},{7,5},{8,10},{10,8},{9,1... | collective-permute-start | bytes 786440 | tf_op jit(solution)/shard_map/ppermute | solution.py:117
  7.7 11.8 %collective-permute-start = (bf16[528,256]{1,0:T(8,128)(2,1)S(1)}, bf16[528,256]{1,0:T(8,128)(2,1)}, u32[]{:S(2)}, u32[]{:S(2)}) collective-permute-start(bf16[528,256]{1,0:T(8,128)(2,1)S(1)} %maximum_maximum_fusion), channel_id=1, source_target_pairs={{0,2},{2,0},{1,3},{3,1},{4,6},{6,4},{5,7},{7,5},{8,10},{10,8},{9,1... | collective-permute-start | bytes 811016 | tf_op jit(solution)/shard_map/ppermute | solution.py:117
  15.1 17.9 %collective-permute-start.5 = (bf16[2,256,256]{2,1,0:T(8,128)(2,1)S(1)}, bf16[2,256,256]{2,1,0:T(8,128)(2,1)S(1)}, u32[]{:S(2)}, u32[]{:S(2)}) collective-permute-start(bf16[2,256,256]{2,1,0:T(8,128)(2,1)S(1)} %get-tuple-element.25), channel_id=1, source_target_pairs={{0,8},{4,12},{8,0},{12,4},{1,9},{5,13},{9,1},{13,5},{2,10},{6,14},... | collective-permute-start | bytes 786440 | tf_op jit(solution)/shard_map/ppermute | solution.py:122
  20.5 12.5 %collective-permute-start.2 = (bf16[1024,256]{1,0:T(8,128)(2,1)S(1)}, bf16[1024,256]{1,0:T(8,128)(2,1)S(1)}, u32[]{:S(2)}, u32[]{:S(2)}) collective-permute-start(bf16[1024,256]{1,0:T(8,128)(2,1)S(1)} %collective-permute-done.1.refs_6_), channel_id=1, source_target_pairs={{0,16},{16,0},{1,17},{17,1},{2,18},{18,2},{3,19},{19,3},{4,20},{20... | collective-permute-start | bytes 1572872 | tf_op jit(solution)/shard_map/ppermute | solution.py:117
  22.8 15.2 %collective-permute-start.4 = (bf16[2,256,256]{2,1,0:T(8,128)(2,1)S(1)}, bf16[2,256,256]{2,1,0:T(8,128)(2,1)S(1)}, u32[]{:S(2)}, u32[]{:S(2)}) collective-permute-start(bf16[2,256,256]{2,1,0:T(8,128)(2,1)S(1)} %get-tuple-element.24), channel_id=1, source_target_pairs={{0,4},{4,0},{8,12},{12,8},{1,5},{5,1},{9,13},{13,9},{2,6},{6,2},{1... | collective-permute-start | bytes 786440 | tf_op jit(solution)/shard_map/ppermute | solution.py:122
  23.2 14.8 %collective-permute-start.6 = (bf16[2,256,256]{2,1,0:T(8,128)(2,1)S(1)}, bf16[2,256,256]{2,1,0:T(8,128)(2,1)S(1)}, u32[]{:S(2)}, u32[]{:S(2)}) collective-permute-start(bf16[2,256,256]{2,1,0:T(8,128)(2,1)S(1)} %get-tuple-element.23), channel_id=1, source_target_pairs={{0,12},{4,8},{8,4},{12,0},{1,13},{5,9},{9,5},{13,1},{2,14},{6,10},... | collective-permute-start | bytes 786440 | tf_op jit(solution)/shard_map/ppermute | solution.py:122
  39.6 9.3 %collective-permute-start.11 = (bf16[512,256]{1,0:T(8,128)(2,1)S(1)}, bf16[512,256]{1,0:T(8,128)(2,1)S(1)}, u32[]{:S(2)}, u32[]{:S(2)}) collective-permute-start(bf16[512,256]{1,0:T(8,128)(2,1)S(1)} %get-tuple-element.14.refs_0_), channel_id=1, source_target_pairs={{0,4},{4,0},{8,12},{12,8},{1,5},{5,1},{9,13},{13,9},{2,6},{6,2},{1... | collective-permute-start | bytes 786440 | tf_op jit(solution)/shard_map/ppermute | solution.py:117
  40.6 15.0 %collective-permute-start.12 = (bf16[512,256]{1,0:T(8,128)(2,1)S(1)}, bf16[512,256]{1,0:T(8,128)(2,1)S(1)}, u32[]{:S(2)}, u32[]{:S(2)}) collective-permute-start(bf16[512,256]{1,0:T(8,128)(2,1)S(1)} %get-tuple-element.14.refs_0_), channel_id=1, source_target_pairs={{0,2},{2,0},{1,3},{3,1},{4,6},{6,4},{5,7},{7,5},{8,10},{10,8},{9,1... | collective-permute-start | bytes 786440 | tf_op jit(solution)/shard_map/ppermute | solution.py:117
  42.1 13.6 %collective-permute-start.13 = (bf16[512,256]{1,0:T(8,128)(2,1)S(1)}, bf16[512,256]{1,0:T(8,128)(2,1)S(1)}, u32[]{:S(2)}, u32[]{:S(2)}) collective-permute-start(bf16[512,256]{1,0:T(8,128)(2,1)S(1)} %get-tuple-element.14.refs_0_), channel_id=1, source_target_pairs={{0,6},{2,4},{4,2},{6,0},{8,14},{10,12},{12,10},{14,8},{1,7},{3,5},... | collective-permute-start | bytes 786440 | tf_op jit(solution)/shard_map/ppermute | solution.py:117
  43.1 15.7 %collective-permute-start.7 = (bf16[512,256]{1,0:T(8,128)(2,1)S(1)}, bf16[512,256]{1,0:T(8,128)(2,1)S(1)}, u32[]{:S(2)}, u32[]{:S(2)}) collective-permute-start(bf16[512,256]{1,0:T(8,128)(2,1)S(1)} %get-tuple-element.11.refs_0_), channel_id=1, source_target_pairs={{0,4},{4,0},{8,12},{12,8},{1,5},{5,1},{9,13},{13,9},{2,6},{6,2},{1... | collective-permute-start | bytes 786440 | tf_op jit(solution)/shard_map/ppermute | solution.py:117
  44.1 19.0 %collective-permute-start.8 = (bf16[512,256]{1,0:T(8,128)(2,1)S(1)}, bf16[512,256]{1,0:T(8,128)(2,1)S(1)}, u32[]{:S(2)}, u32[]{:S(2)}) collective-permute-start(bf16[512,256]{1,0:T(8,128)(2,1)S(1)} %get-tuple-element.11.refs_0_), channel_id=1, source_target_pairs={{0,2},{2,0},{1,3},{3,1},{4,6},{6,4},{5,7},{7,5},{8,10},{10,8},{9,1... | collective-permute-start | bytes 786440 | tf_op jit(solution)/shard_map/ppermute | solution.py:117
  48.9 14.2 %collective-permute-start.9 = (bf16[512,256]{1,0:T(8,128)(2,1)S(1)}, bf16[512,256]{1,0:T(8,128)(2,1)S(1)}, u32[]{:S(2)}, u32[]{:S(2)}) collective-permute-start(bf16[512,256]{1,0:T(8,128)(2,1)S(1)} %get-tuple-element.11.refs_0_), channel_id=1, source_target_pairs={{0,6},{2,4},{4,2},{6,0},{8,14},{10,12},{12,10},{14,8},{1,7},{3,5},... | collective-permute-start | bytes 786440 | tf_op jit(solution)/shard_map/ppermute | solution.py:117
  55.6 7.6 %copy-start = (bf16[1024,1024]{1,0:T(8,128)(2,1)S(1)}, bf16[1024,1024]{1,0:T(8,128)(2,1)}, u32[]{:S(2)}) copy-start(bf16[1024,1024]{1,0:T(8,128)(2,1)} %refs_5_.3) | copy-start | bytes 6291460
  55.8 7.5 %collective-permute-start.14 = (bf16[4,512,256]{2,1,0:T(8,128)(2,1)S(1)}, bf16[4,512,256]{2,1,0:T(8,128)(2,1)S(1)}, u32[]{:S(2)}, u32[]{:S(2)}) collective-permute-start(bf16[4,512,256]{2,1,0:T(8,128)(2,1)S(1)} %pad_maximum_fusion.1), channel_id=1, source_target_pairs={{0,1},{1,0},{2,3},{3,2},{4,5},{5,4},{6,7},{7,6},{8,9},{9,8},{10,11... | collective-permute-start | bytes 3145736 | tf_op jit(solution)/shard_map/ppermute | solution.py:117
  63.2 7.2 %collective-permute-start.10 = (bf16[4,512,256]{2,1,0:T(8,128)(2,1)S(1)}, bf16[4,512,256]{2,1,0:T(8,128)(2,1)S(1)}, u32[]{:S(2)}, u32[]{:S(2)}) collective-permute-start(bf16[4,512,256]{2,1,0:T(8,128)(2,1)S(1)} %pad_maximum_fusion), channel_id=1, source_target_pairs={{0,1},{1,0},{2,3},{3,2},{4,5},{5,4},{6,7},{7,6},{8,9},{9,8},{10,11... | collective-permute-start | bytes 3145736 | tf_op jit(solution)/shard_map/ppermute | solution.py:117
  65.2 12.4 %collective-permute-start.17 = (bf16[256,512]{1,0:T(8,128)(2,1)S(1)}, bf16[256,512]{1,0:T(8,128)(2,1)S(1)}, u32[]{:S(2)}, u32[]{:S(2)}) collective-permute-start(bf16[256,512]{1,0:T(8,128)(2,1)S(1)} %get-tuple-element.22), channel_id=1, source_target_pairs={{0,12},{4,8},{8,4},{12,0},{1,13},{5,9},{9,5},{13,1},{2,14},{6,10},... | collective-permute-start | bytes 786440 | tf_op jit(solution)/shard_map/ppermute | solution.py:122
  72.3 11.6 %collective-permute-start.16 = (bf16[256,512]{1,0:T(8,128)(2,1)S(1)}, bf16[256,512]{1,0:T(8,128)(2,1)S(1)}, u32[]{:S(2)}, u32[]{:S(2)}) collective-permute-start(bf16[256,512]{1,0:T(8,128)(2,1)S(1)} %slice_bitcast_fusion.1), channel_id=1, source_target_pairs={{0,4},{4,0},{8,12},{12,8},{1,5},{5,1},{9,13},{13,9},{2,6},{6,2},{1... | collective-permute-start | bytes 786440 | tf_op jit(solution)/shard_map/ppermute | solution.py:122
  72.4 21.1 %collective-permute-start.15 = (bf16[256,512]{1,0:T(8,128)(2,1)S(1)}, bf16[256,512]{1,0:T(8,128)(2,1)S(1)}, u32[]{:S(2)}, u32[]{:S(2)}) collective-permute-start(bf16[256,512]{1,0:T(8,128)(2,1)S(1)} %get-tuple-element.21), channel_id=1, source_target_pairs={{0,8},{4,12},{8,0},{12,4},{1,9},{5,13},{9,1},{13,5},{2,10},{6,14},... | collective-permute-start | bytes 786440 | tf_op jit(solution)/shard_map/ppermute | solution.py:122

commit v4 on v3

--- a/solution.py
+++ b/solution.py
@@ -164,7 +164,7 @@
                 pltpu.VMEM((4, block, width), jnp.bfloat16),
             ],
         ),
-        compiler_params=pltpu.CompilerParams(vmem_limit_bytes=32 * 2**20),
+        compiler_params=pltpu.CompilerParams(vmem_limit_bytes=16 * 2**20),
         cost_estimate=pl.CostEstimate(
             flops=2 * 4 * block * 3 * block * width, bytes_accessed=2**21, transcendentals=0
         ),
@@ -210,7 +210,7 @@
             ],
             out_specs=pl.BlockSpec((2, tokens // 2, 2 * columns), lambda i, s: (0, 0, 0)),
         ),
-        compiler_params=pltpu.CompilerParams(vmem_limit_bytes=32 * 2**20),
+        compiler_params=pltpu.CompilerParams(vmem_limit_bytes=16 * 2**20),
         cost_estimate=pl.CostEstimate(
             flops=2 * tokens * 8 * width * 2 * columns, bytes_accessed=2**22, transcendentals=0
         ),
@@ -276,16 +276,29 @@
     first_rows, w_near, w_far = lax.optimization_barrier((first_rows, w_near, w_far))
     gated_far, gated_near = gated_conv(place, first_rows, (piece_0, piece_1, piece_2, piece_3))
 
-    def partials(gated):
-        mine = [gated, swap(gated, "ctx"), swap(gated, "chan"), swap(gated, "ctx", "chan")]
-        other = swap(jnp.stack(mine), "sub")
-        return project(place, mine, other, out_weight, w_near, w_far)
-
-    far = partials(gated_far)
+    def gathered(gated):
+        return [gated, swap(gated, "ctx"), swap(gated, "chan"), swap(gated, "ctx", "chan")]
+
+    def partials(mine):
+        return project(place, mine, swap(jnp.stack(mine), "sub"), out_weight, w_near, w_far)
+
+    far = partials(gathered(gated_far))
     far_own, far_near = across(far[0], 2), across(far[1], 3)
-    close = partials(gated_near)
-    near = across(close[1], 1)
-    this_half = close[0].astype(jnp.float32) + far_own.astype(jnp.float32)
+
+    def close_partials(mine):
+        gated, beside, cross = mine
+        close = partials([gated, beside, cross, swap(beside, "chan")])
+        return close[0], across(close[1], 1)
+
+    def no_taps(mine):
+        zeros = jnp.zeros((block, half), jnp.bfloat16)
+        return zeros, zeros
+
+    close_own, near = lax.cond(
+        jnp.max(filter_blocks) > 0, close_partials, no_taps,
+        [gated_near, swap(gated_near, "ctx"), swap(gated_near, "chan")],
+    )
+    this_half = close_own.astype(jnp.float32) + far_own.astype(jnp.float32)
     that_half = near.astype(jnp.float32) + far_near.astype(jnp.float32)
     left = jnp.where(bit == 0, this_half, that_half)
     right = jnp.where(bit == 0, that_half, this_half)

time: 94.7 us -> 91.2 us (0.963)
  waiting for transfers between devices: 54.3 us -> 46.6 us
  starting transfers between devices: 28 us -> 21 us
  other arithmetic: 2 us -> 8.77 us
  Pallas kernels: 5.33 us -> 7.86 us
  local copies, waits for them, and re-layouts: 4.65 us -> 5.89 us
    ppermute x7, waiting for transfers between devices: 24.9 us -> 16.4 us  [across(): return lax.ppermute(value, 'ctx', [(i, i ^ distance) for i in range(count)])]
    ppermute x7, starting transfers between devices: 16.2 us -> 9.98 us  [across(): return lax.ppermute(value, 'ctx', [(i, i ^ distance) for i in range(count)])]
    pallas_call x2, Pallas kernels: 3.75 us -> 6.15 us  [project(): pl.pallas_call(project_kernel, out_shape=jax.ShapeDtypeStruct((2, tokens...]
    another operation x3, other arithmetic: 0.34 us -> 2.21 us  [packed(): return jnp.stack([product, q])]
    select_n x1, other arithmetic: 0.04 us -> 1.71 us  [paired_plan(): piece_2 = across(jnp.where(inside, same_came, same_own), 2)]
    another operation x3, other arithmetic: 0.42 us -> 1.46 us  [the longest x2 0.26 us: partials(): other = swap(jnp.stack(mine), 'sub')]
  transfers between devices with their start and end apart: 18 -> 18, of which waited for: 11 -> 11; matrix products, arithmetic and copies ran while one was open for 5% -> 10% of each run, Pallas kernels for 4% -> 7%
where the time goes in v4:
time: 91.2 us; the launch traced here: 90.9 us
  waiting for transfers between devices  46.6 us (51%)
  starting transfers between devices  21 us (23%)
  other arithmetic  8.77 us (10%)
  Pallas kernels  7.86 us (9%)
  local copies, waits for them, and re-layouts  5.89 us (6%)
    ppermute x11, waiting for transfers between devices, swap(): return lax.ppermute(value, axes, [(i, i ^ flip) for i in range(total)])  30.2 us
    ppermute x7, waiting for transfers between devices, across(): return lax.ppermute(value, 'ctx', [(i, i ^ distance) for i in range(count)])  16.4 us
    ppermute x11, starting transfers between devices, swap(): return lax.ppermute(value, axes, [(i, i ^ flip) for i in range(total)])  11 us
    ppermute x7, starting transfers between devices, across(): return lax.ppermute(value, 'ctx', [(i, i ^ distance) for i in range(count)])  9.98 us
    pallas_call x2, Pallas kernels, project(): pl.pallas_call(project_kernel, out_shape=jax.ShapeDtypeStruct((2, tokens...  6.15 us
    another operation x3, other arithmetic, packed(): return jnp.stack([product, q])  2.21 us
  transfers between devices with their start and end apart: 18, of which 11 were waited for; matrix products, arithmetic and copies ran while one was open for 10% of the time, Pallas kernels for 7%

profile of v4, /device:TPU:0, one launch (start us, length us, event | category | flops | bytes accessed | tf_op | source)
XLA Modules:
  0.0 90.9 jit_solution(13177814690952860202)
XLA Ops:
  0.0 1.3 %dynamic-slice_bitcast_fusion = (bf16[1,256,256]{2,1,0:T(8,128)(2,1)S(1)}, bf16[1,256,256]{2,1,0:T(8,128)(2,1)S(1)}, bf16[1,256,256]{2,1,0:T(8,128)(2,1)S(1)}, bf16[1,256,256]{2,1,0:T(8,128)(2,1)S(1)}) fusion(bf16[256,1024]{1,0:T(8,128)(2,1)} %param.8, s32[]{:T(128)S(6)} %select_n.98, s32[]{:T(128)S(6)} %select_n.95, s32[]{:T(128)S(6)} %select_n.90, ...), kind=kLoop, calls=%fused_computation.29 | loop fusion | bytes 1048592 | tf_op jit(solution)/shard_map/stack | solution.py:236
  1.3 1.4 %fusion.4 = (bf16[1,256,256]{2,1,0:T(8,128)(2,1)S(1)}, bf16[1,256,256]{2,1,0:T(8,128)(2,1)S(1)}, bf16[1,256,256]{2,1,0:T(8,128)(2,1)S(1)}, bf16[1,256,256]{2,1,0:T(8,128)(2,1)S(1)}) fusion(bf16[256,1024]{1,0:T(8,128)(2,1)} %param.10, s32[]{:T(128)S(6)} %select_n.98, bf16[256,1024]{1,0:T(8,128)(2,1)} %param.9, s32[]{:T(128)S(6)} %select_n.95, ...), kind=kLoop, calls=%fused_computation.28 | loop fusion | flops 1048576 | bytes 1572880 | tf_op jit(solution)/shard_map/stack | solution.py:236
  3.5 2.9 %collective-permute-start.6 = (bf16[2,256,256]{2,1,0:T(8,128)(2,1)}, bf16[2,256,256]{2,1,0:T(8,128)(2,1)}, u32[]{:S(2)}, u32[]{:S(2)}) collective-permute-start(bf16[2,256,256]{2,1,0:T(8,128)(2,1)} %pad_maximum_fusion.5), channel_id=1, source_target_pairs={{0,2},{2,0},{1,3},{3,1},{4,6},{6,4},{5,7},{7,5},{8,10},{10,8},{9,1... | collective-permute-start | bytes 786440 | tf_op jit(solution)/shard_map/ppermute | solution.py:117
  7.3 1.6 %collective-permute-start.4 = (bf16[1024,256]{1,0:T(8,128)(2,1)}, bf16[1024,256]{1,0:T(8,128)(2,1)}, u32[]{:S(2)}, u32[]{:S(2)}) collective-permute-start(bf16[1024,256]{1,0:T(8,128)(2,1)} %constant_dynamic-slice_fusion), channel_id=1, source_target_pairs={{0,4},{4,0},{8,12},{12,8},{1,5},{5,1},{9,13},{13,9},{2,6},{6,2},{1... | collective-permute-start | bytes 1572872 | tf_op jit(solution)/shard_map/ppermute | solution.py:122
  11.9 1.6 %collective-permute-done.6 = bf16[2,256,256]{2,1,0:T(8,128)(2,1)} collective-permute-done((bf16[2,256,256]{2,1,0:T(8,128)(2,1)}, bf16[2,256,256]{2,1,0:T(8,128)(2,1)}, u32[]{:S(2)}, u32[]{:S(2)}) %collective-permute-start.6) | collective-permute-done | bytes 262176 | tf_op jit(solution)/shard_map/ppermute | solution.py:117
  13.5 1.7 %broadcast_select_fusion.1 = (bf16[2,256,256]{2,1,0:T(8,128)(2,1)}, bf16[2,256,256]{2,1,0:T(8,128)(2,1)S(1)}) fusion(bf16[2,256,256]{2,1,0:T(8,128)(2,1)} %collective-permute-done.6, pred[]{:T(512)S(6)} %eq.14, bf16[1,256,256]{2,1,0:T(8,128)(2,1)S(1)} %get-tuple-element.57, bf16[1,256,256]{2,1,0:T(8,128)(2,1)S(1)} %get-tuple-element.47), kind=kLoop, calls=%fused_computation.22 | loop fusion | flops 393216 | bytes 1048577 | tf_op jit(solution)/shard_map/jit(_where)/select_n | solution.py:261
  15.2 2.9 %collective-permute-start.8 = (bf16[2,256,256]{2,1,0:T(8,128)(2,1)}, bf16[2,256,256]{2,1,0:T(8,128)(2,1)S(1)}, u32[]{:S(2)}, u32[]{:S(2)}) collective-permute-start(bf16[2,256,256]{2,1,0:T(8,128)(2,1)} %get-tuple-element.54), channel_id=1, source_target_pairs={{0,8},{4,12},{8,0},{12,4},{1,9},{5,13},{9,1},{13,5},{2,10},{6,14},... | collective-permute-start | bytes 786440 | tf_op jit(solution)/shard_map/ppermute | solution.py:122
  19.8 6.4 %collective-permute-done.4.refs_6_ = bf16[1024,256]{1,0:T(8,128)(2,1)} collective-permute-done((bf16[1024,256]{1,0:T(8,128)(2,1)}, bf16[1024,256]{1,0:T(8,128)(2,1)}, u32[]{:S(2)}, u32[]{:S(2)}) %collective-permute-start.4) | collective-permute-done | bytes 524320 | tf_op jit(solution)/shard_map/ppermute | solution.py:122
  26.2 1.6 %collective-permute-start.5 = (bf16[1024,256]{1,0:T(8,128)(2,1)}, bf16[1024,256]{1,0:T(8,128)(2,1)}, u32[]{:S(2)}, u32[]{:S(2)}) collective-permute-start(bf16[1024,256]{1,0:T(8,128)(2,1)} %collective-permute-done.4.refs_6_), channel_id=1, source_target_pairs={{0,16},{16,0},{1,17},{17,1},{2,18},{18,2},{3,19},{19,3},{4,20},{20... | collective-permute-start | bytes 1572872 | tf_op jit(solution)/shard_map/ppermute | solution.py:117
  28.5 1.3 %collective-permute-start.9 = (bf16[2,256,256]{2,1,0:T(8,128)(2,1)S(1)}, bf16[2,256,256]{2,1,0:T(8,128)(2,1)S(1)}, u32[]{:S(2)}, u32[]{:S(2)}) collective-permute-start(bf16[2,256,256]{2,1,0:T(8,128)(2,1)S(1)} %get-tuple-element.52), channel_id=1, source_target_pairs={{0,12},{4,8},{8,4},{12,0},{1,13},{5,9},{9,5},{13,1},{2,14},{6,10},... | collective-permute-start | bytes 786440 | tf_op jit(solution)/shard_map/ppermute | solution.py:122
  31.1 8.0 %collective-permute-done.5.refs_7_ = bf16[1024,256]{1,0:T(8,128)(2,1)} collective-permute-done((bf16[1024,256]{1,0:T(8,128)(2,1)}, bf16[1024,256]{1,0:T(8,128)(2,1)}, u32[]{:S(2)}, u32[]{:S(2)}) %collective-permute-start.5) | collective-permute-done | bytes 524320 | tf_op jit(solution)/shard_map/ppermute | solution.py:117
  39.0 1.9 %collective-permute-done.7.refs_1_ = bf16[2,256,256]{2,1,0:T(8,128)(2,1)S(1)} collective-permute-done((bf16[2,256,256]{2,1,0:T(8,128)(2,1)}, bf16[2,256,256]{2,1,0:T(8,128)(2,1)S(1)}, u32[]{:S(2)}, u32[]{:S(2)}) %collective-permute-start.7) | collective-permute-done | bytes 262176 | tf_op jit(solution)/shard_map/ppermute | solution.py:122
  41.0 1.7 %shard_map.64 = (bf16[512,256]{1,0:T(8,128)(2,1)S(1)}, bf16[512,256]{1,0:T(8,128)(2,1)S(1)}) custom-call(s32[6]{0:T(128)} %stack.97.place, f32[2,768]{1,0:T(2,128)S(1)} %maximum_maximum_fusion.1.row_ref, bf16[2,256,256]{2,1,0:T(8,128)(2,1)S(1)} %get-tuple-element.55.refs_0_, bf16[2,256,256]{2,1,0:T(8,128)(2,1)S(1)} %collective-permute-done.7.refs_1_, ...), custom_call_target="tpu_custom_call" | custom-call | flops 402653184 | bytes 2097152 | tf_op jit(solution)/shard_map/pallas_call | solution.py:153
  42.7 1.6 %collective-permute-start.12 = (bf16[512,256]{1,0:T(8,128)(2,1)S(1)}, bf16[512,256]{1,0:T(8,128)(2,1)S(1)}, u32[]{:S(2)}, u32[]{:S(2)}) collective-permute-start(bf16[512,256]{1,0:T(8,128)(2,1)S(1)} %get-tuple-element.40.refs_0_), channel_id=1, source_target_pairs={{0,4},{4,0},{8,12},{12,8},{1,5},{5,1},{9,13},{13,9},{2,6},{6,2},{1... | collective-permute-start | bytes 786440 | tf_op jit(solution)/shard_map/ppermute | solution.py:117
  44.3 2.0 %collective-permute-start.14 = (bf16[512,256]{1,0:T(8,128)(2,1)S(1)}, bf16[512,256]{1,0:T(8,128)(2,1)S(1)}, u32[]{:S(2)}, u32[]{:S(2)}) collective-permute-start(bf16[512,256]{1,0:T(8,128)(2,1)S(1)} %get-tuple-element.40.refs_0_), channel_id=1, source_target_pairs={{0,6},{2,4},{4,2},{6,0},{8,14},{10,12},{12,10},{14,8},{1,7},{3,5},... | collective-permute-start | bytes 786440 | tf_op jit(solution)/shard_map/ppermute | solution.py:117
  46.2 4.9 %collective-permute-done.12.refs_1_ = bf16[512,256]{1,0:T(8,128)(2,1)S(1)} collective-permute-done((bf16[512,256]{1,0:T(8,128)(2,1)S(1)}, bf16[512,256]{1,0:T(8,128)(2,1)S(1)}, u32[]{:S(2)}, u32[]{:S(2)}) %collective-permute-start.12) | collective-permute-done | bytes 262176 | tf_op jit(solution)/shard_map/ppermute | solution.py:117
  51.1 4.0 %collective-permute-done.13.refs_2_ = bf16[512,256]{1,0:T(8,128)(2,1)S(1)} collective-permute-done((bf16[512,256]{1,0:T(8,128)(2,1)S(1)}, bf16[512,256]{1,0:T(8,128)(2,1)S(1)}, u32[]{:S(2)}, u32[]{:S(2)}) %collective-permute-start.13) | collective-permute-done | bytes 262176 | tf_op jit(solution)/shard_map/ppermute | solution.py:117
  57.9 3.1 %shard_map.65 = bf16[2,256,512]{2,1,0:T(8,128)(2,1)S(1)} custom-call(s32[6]{0:T(128)} %stack.97.place, bf16[512,256]{1,0:T(8,128)(2,1)S(1)} %get-tuple-element.40.refs_0_, bf16[512,256]{1,0:T(8,128)(2,1)S(1)} %collective-permute-done.12.refs_1_, bf16[512,256]{1,0:T(8,128)(2,1)S(1)} %collective-permute-done.13.refs_2_, ...), custom_call_target="tpu_custom_call" | custom-call | flops 1073741824 | bytes 4194304 | tf_op jit(solution)/shard_map/pallas_call | solution.py:198
  61.9 2.8 %collective-permute-start.16 = (bf16[256,512]{1,0:T(8,128)(2,1)}, bf16[256,512]{1,0:T(8,128)(2,1)}, u32[]{:S(2)}, u32[]{:S(2)}) collective-permute-start(bf16[256,512]{1,0:T(8,128)(2,1)} %get-tuple-element.51), channel_id=1, source_target_pairs={{0,8},{4,12},{8,0},{12,4},{1,9},{5,13},{9,1},{13,5},{2,10},{6,14},... | collective-permute-start | bytes 786440 | tf_op jit(solution)/shard_map/ppermute | solution.py:122
  66.1 22.7 %conditional.1 = (f32[256,512]{1,0:T(8,128)S(1)}, f32[256,512]{1,0:T(8,128)S(1)}) conditional(s32[]{:T(128)} %convert_element_type.67, () %tuple.18, (bf16[512,256]{1,0:T(8,128)(2,1)S(1)}, bf16[512,256]{1,0:T(8,128)(2,1)S(1)}, bf16[512,256]{1,0:T(8,128)(2,1)S(1)}, s32[6]{0:T(128)S(1)}, bf16[1024,1024]{1,0:T(8,128)(2,1)S(1)}, ...), branch_computations={%region_1.2_spmd, %region_2.3_spmd} | conditional | flops 1075576832 | bytes 14680200 | solution.py:297
  67.0 7.2 %collective-permute-done.refs_3_ = bf16[512,256]{1,0:T(8,128)(2,1)S(1)} collective-permute-done((bf16[512,256]{1,0:T(8,128)(2,1)S(1)}, bf16[512,256]{1,0:T(8,128)(2,1)S(1)}, u32[]{:S(2)}, u32[]{:S(2)}) %collective-permute-start) | collective-permute-done | bytes 262176 | tf_op jit(solution)/shard_map/cond/branch_1_fun/ppermute | solution.py:117
  74.4 2.6 %collective-permute-done.1.refs_4_ = bf16[4,512,256]{2,1,0:T(8,128)(2,1)S(1)} collective-permute-done((bf16[4,512,256]{2,1,0:T(8,128)(2,1)S(1)}, bf16[4,512,256]{2,1,0:T(8,128)(2,1)S(1)}, u32[]{:S(2)}, u32[]{:S(2)}) %collective-permute-start.1) | collective-permute-done | bytes 1048608 | tf_op jit(solution)/shard_map/cond/branch_1_fun/ppermute | solution.py:117
  77.0 3.0 %branch_1_fun.1 = bf16[2,256,512]{2,1,0:T(8,128)(2,1)S(1)} custom-call(s32[6]{0:T(128)S(1)} %get-tuple-element.21.place, bf16[512,256]{1,0:T(8,128)(2,1)S(1)} %get-tuple-element.22.refs_0_, bf16[512,256]{1,0:T(8,128)(2,1)S(1)} %get-tuple-element.23.refs_1_, bf16[512,256]{1,0:T(8,128)(2,1)S(1)} %get-tuple-element.24.refs_2_, ...), custom_call_target="tpu_custom_call" | custom-call | flops 1073741824 | bytes 4194304 | tf_op jit(solution)/shard_map/cond/branch_1_fun/pallas_call | solution.py:198
  80.7 8.0 %collective-permute-done.2 = bf16[256,512]{1,0:T(8,128)(2,1)S(1)} collective-permute-done((bf16[256,512]{1,0:T(8,128)(2,1)S(1)}, bf16[256,512]{1,0:T(8,128)(2,1)S(1)}, u32[]{:S(2)}, u32[]{:S(2)}) %collective-permute-start.2) | collective-permute-done | bytes 262176 | tf_op jit(solution)/shard_map/cond/branch_1_fun/ppermute | solution.py:122
  (55 shorter events, 16.6 us)
Async XLA Ops:
  0.0 6.4 %copy-start = (bf16[1024,1024]{1,0:T(8,128)(2,1)S(1)}, bf16[1024,1024]{1,0:T(8,128)(2,1)}, u32[]{:S(2)}) copy-start(bf16[1024,1024]{1,0:T(8,128)(2,1)} %refs_5_.1) | copy-start | bytes 6291460
  0.0 8.9 %copy-start.3 = (s32[8]{0:T(128)S(1)}, s32[8]{0:T(128)}, u32[]{:S(2)}) copy-start(s32[8]{0:T(128)} %param.12) | copy-start | bytes 100
  1.3 8.3 %copy-start.1 = (f32[8,512]{1,0:T(8,128)S(1)}, f32[8,512]{1,0:T(8,128)}, u32[]{:S(2)}) copy-start(f32[8,512]{1,0:T(8,128)} %param.11) | copy-start | bytes 49156
  3.5 10.0 %collective-permute-start.6 = (bf16[2,256,256]{2,1,0:T(8,128)(2,1)}, bf16[2,256,256]{2,1,0:T(8,128)(2,1)}, u32[]{:S(2)}, u32[]{:S(2)}) collective-permute-start(bf16[2,256,256]{2,1,0:T(8,128)(2,1)} %pad_maximum_fusion.5), channel_id=1, source_target_pairs={{0,2},{2,0},{1,3},{3,1},{4,6},{6,4},{5,7},{7,5},{8,10},{10,8},{9,1... | collective-permute-start | bytes 786440 | tf_op jit(solution)/shard_map/ppermute | solution.py:117
  7.3 18.9 %collective-permute-start.4 = (bf16[1024,256]{1,0:T(8,128)(2,1)}, bf16[1024,256]{1,0:T(8,128)(2,1)}, u32[]{:S(2)}, u32[]{:S(2)}) collective-permute-start(bf16[1024,256]{1,0:T(8,128)(2,1)} %constant_dynamic-slice_fusion), channel_id=1, source_target_pairs={{0,4},{4,0},{8,12},{12,8},{1,5},{5,1},{9,13},{13,9},{2,6},{6,2},{1... | collective-permute-start | bytes 1572872 | tf_op jit(solution)/shard_map/ppermute | solution.py:122
  10.6 8.2 %collective-permute-start.3 = (bf16[528,256]{1,0:T(8,128)(2,1)}, bf16[528,256]{1,0:T(8,128)(2,1)}, u32[]{:S(2)}, u32[]{:S(2)}) collective-permute-start(bf16[528,256]{1,0:T(8,128)(2,1)} %maximum_maximum_fusion), channel_id=1, source_target_pairs={{0,2},{2,0},{1,3},{3,1},{4,6},{6,4},{5,7},{7,5},{8,10},{10,8},{9,1... | collective-permute-start | bytes 811016 | tf_op jit(solution)/shard_map/ppermute | solution.py:117
  15.2 23.8 %collective-permute-start.8 = (bf16[2,256,256]{2,1,0:T(8,128)(2,1)}, bf16[2,256,256]{2,1,0:T(8,128)(2,1)S(1)}, u32[]{:S(2)}, u32[]{:S(2)}) collective-permute-start(bf16[2,256,256]{2,1,0:T(8,128)(2,1)} %get-tuple-element.54), channel_id=1, source_target_pairs={{0,8},{4,12},{8,0},{12,4},{1,9},{5,13},{9,1},{13,5},{2,10},{6,14},... | collective-permute-start | bytes 786440 | tf_op jit(solution)/shard_map/ppermute | solution.py:122
  26.2 12.8 %collective-permute-start.5 = (bf16[1024,256]{1,0:T(8,128)(2,1)}, bf16[1024,256]{1,0:T(8,128)(2,1)}, u32[]{:S(2)}, u32[]{:S(2)}) collective-permute-start(bf16[1024,256]{1,0:T(8,128)(2,1)} %collective-permute-done.4.refs_6_), channel_id=1, source_target_pairs={{0,16},{16,0},{1,17},{17,1},{2,18},{18,2},{3,19},{19,3},{4,20},{20... | collective-permute-start | bytes 1572872 | tf_op jit(solution)/shard_map/ppermute | solution.py:117
  28.5 12.4 %collective-permute-start.7 = (bf16[2,256,256]{2,1,0:T(8,128)(2,1)}, bf16[2,256,256]{2,1,0:T(8,128)(2,1)S(1)}, u32[]{:S(2)}, u32[]{:S(2)}) collective-permute-start(bf16[2,256,256]{2,1,0:T(8,128)(2,1)} %get-tuple-element.53), channel_id=1, source_target_pairs={{0,4},{4,0},{8,12},{12,8},{1,5},{5,1},{9,13},{13,9},{2,6},{6,2},{1... | collective-permute-start | bytes 786440 | tf_op jit(solution)/shard_map/ppermute | solution.py:122
  28.5 12.4 %collective-permute-start.9 = (bf16[2,256,256]{2,1,0:T(8,128)(2,1)S(1)}, bf16[2,256,256]{2,1,0:T(8,128)(2,1)S(1)}, u32[]{:S(2)}, u32[]{:S(2)}) collective-permute-start(bf16[2,256,256]{2,1,0:T(8,128)(2,1)S(1)} %get-tuple-element.52), channel_id=1, source_target_pairs={{0,12},{4,8},{8,4},{12,0},{1,13},{5,9},{9,5},{13,1},{2,14},{6,10},... | collective-permute-start | bytes 786440 | tf_op jit(solution)/shard_map/ppermute | solution.py:122
  42.7 8.4 %collective-permute-start.12 = (bf16[512,256]{1,0:T(8,128)(2,1)S(1)}, bf16[512,256]{1,0:T(8,128)(2,1)S(1)}, u32[]{:S(2)}, u32[]{:S(2)}) collective-permute-start(bf16[512,256]{1,0:T(8,128)(2,1)S(1)} %get-tuple-element.40.refs_0_), channel_id=1, source_target_pairs={{0,4},{4,0},{8,12},{12,8},{1,5},{5,1},{9,13},{13,9},{2,6},{6,2},{1... | collective-permute-start | bytes 786440 | tf_op jit(solution)/shard_map/ppermute | solution.py:117
  44.3 10.8 %collective-permute-start.13 = (bf16[512,256]{1,0:T(8,128)(2,1)S(1)}, bf16[512,256]{1,0:T(8,128)(2,1)S(1)}, u32[]{:S(2)}, u32[]{:S(2)}) collective-permute-start(bf16[512,256]{1,0:T(8,128)(2,1)S(1)} %get-tuple-element.40.refs_0_), channel_id=1, source_target_pairs={{0,2},{2,0},{1,3},{3,1},{4,6},{6,4},{5,7},{7,5},{8,10},{10,8},{9,1... | collective-permute-start | bytes 786440 | tf_op jit(solution)/shard_map/ppermute | solution.py:117
  44.3 10.8 %collective-permute-start.14 = (bf16[512,256]{1,0:T(8,128)(2,1)S(1)}, bf16[512,256]{1,0:T(8,128)(2,1)S(1)}, u32[]{:S(2)}, u32[]{:S(2)}) collective-permute-start(bf16[512,256]{1,0:T(8,128)(2,1)S(1)} %get-tuple-element.40.refs_0_), channel_id=1, source_target_pairs={{0,6},{2,4},{4,2},{6,0},{8,14},{10,12},{12,10},{14,8},{1,7},{3,5},... | collective-permute-start | bytes 786440 | tf_op jit(solution)/shard_map/ppermute | solution.py:117
  55.2 2.7 %collective-permute-start.15 = (bf16[4,512,256]{2,1,0:T(8,128)(2,1)S(1)}, bf16[4,512,256]{2,1,0:T(8,128)(2,1)S(1)}, u32[]{:S(2)}, u32[]{:S(2)}) collective-permute-start(bf16[4,512,256]{2,1,0:T(8,128)(2,1)S(1)} %pad_maximum_fusion.1), channel_id=1, source_target_pairs={{0,1},{1,0},{2,3},{3,2},{4,5},{5,4},{6,7},{7,6},{8,9},{9,8},{10,11... | collective-permute-start | bytes 3145736 | tf_op jit(solution)/shard_map/ppermute | solution.py:117
  55.2 10.8 %copy-start.2 = (s32[6]{0:T(128)S(1)}, s32[6]{0:T(128)}, u32[]{:S(2)}) copy-start(s32[6]{0:T(128)} %stack.97.place) | copy-start | bytes 76
  55.3 10.8 %collective-permute-start.10 = (bf16[512,256]{1,0:T(8,128)(2,1)S(1)}, bf16[512,256]{1,0:T(8,128)(2,1)S(1)}, u32[]{:S(2)}, u32[]{:S(2)}) collective-permute-start(bf16[512,256]{1,0:T(8,128)(2,1)S(1)} %get-tuple-element.36), channel_id=1, source_target_pairs={{0,4},{4,0},{8,12},{12,8},{1,5},{5,1},{9,13},{13,9},{2,6},{6,2},{1... | collective-permute-start | bytes 786440 | tf_op jit(solution)/shard_map/ppermute | solution.py:117
  56.5 9.6 %collective-permute-start.11 = (bf16[512,256]{1,0:T(8,128)(2,1)S(1)}, bf16[512,256]{1,0:T(8,128)(2,1)S(1)}, u32[]{:S(2)}, u32[]{:S(2)}) collective-permute-start(bf16[512,256]{1,0:T(8,128)(2,1)S(1)} %get-tuple-element.36), channel_id=1, source_target_pairs={{0,2},{2,0},{1,3},{3,1},{4,6},{6,4},{5,7},{7,5},{8,10},{10,8},{9,1... | collective-permute-start | bytes 786440 | tf_op jit(solution)/shard_map/ppermute | solution.py:117
  61.9 26.9 %collective-permute-start.16 = (bf16[256,512]{1,0:T(8,128)(2,1)}, bf16[256,512]{1,0:T(8,128)(2,1)}, u32[]{:S(2)}, u32[]{:S(2)}) collective-permute-start(bf16[256,512]{1,0:T(8,128)(2,1)} %get-tuple-element.51), channel_id=1, source_target_pairs={{0,8},{4,12},{8,0},{12,4},{1,9},{5,13},{9,1},{13,5},{2,10},{6,14},... | collective-permute-start | bytes 786440 | tf_op jit(solution)/shard_map/ppermute | solution.py:122
  64.7 24.1 %collective-permute-start.17 = (bf16[256,512]{1,0:T(8,128)(2,1)}, bf16[256,512]{1,0:T(8,128)(2,1)}, u32[]{:S(2)}, u32[]{:S(2)}) collective-permute-start(bf16[256,512]{1,0:T(8,128)(2,1)} %get-tuple-element.50), channel_id=1, source_target_pairs={{0,12},{4,8},{8,4},{12,0},{1,13},{5,9},{9,5},{13,1},{2,14},{6,10},... | collective-permute-start | bytes 786440 | tf_op jit(solution)/shard_map/ppermute | solution.py:122
  66.1 8.0 %collective-permute-start = (bf16[512,256]{1,0:T(8,128)(2,1)S(1)}, bf16[512,256]{1,0:T(8,128)(2,1)S(1)}, u32[]{:S(2)}, u32[]{:S(2)}) collective-permute-start(bf16[512,256]{1,0:T(8,128)(2,1)S(1)} %get-tuple-element.23.refs_1_), channel_id=1, source_target_pairs={{0,2},{2,0},{1,3},{3,1},{4,6},{6,4},{5,7},{7,5},{8,10},{10,8},{9,1... | collective-permute-start | bytes 786440 | tf_op jit(solution)/shard_map/cond/branch_1_fun/ppermute | solution.py:117
  74.3 2.7 %collective-permute-start.1 = (bf16[4,512,256]{2,1,0:T(8,128)(2,1)S(1)}, bf16[4,512,256]{2,1,0:T(8,128)(2,1)S(1)}, u32[]{:S(2)}, u32[]{:S(2)}) collective-permute-start(bf16[4,512,256]{2,1,0:T(8,128)(2,1)S(1)} %pad_maximum_fusion), channel_id=1, source_target_pairs={{0,1},{1,0},{2,3},{3,2},{4,5},{5,4},{6,7},{7,6},{8,9},{9,8},{10,11... | collective-permute-start | bytes 3145736 | tf_op jit(solution)/shard_map/cond/branch_1_fun/ppermute | solution.py:117
  80.1 8.6 %collective-permute-start.2 = (bf16[256,512]{1,0:T(8,128)(2,1)S(1)}, bf16[256,512]{1,0:T(8,128)(2,1)S(1)}, u32[]{:S(2)}, u32[]{:S(2)}) collective-permute-start(bf16[256,512]{1,0:T(8,128)(2,1)S(1)} %get-tuple-element.42), channel_id=1, source_target_pairs={{0,4},{4,0},{8,12},{12,8},{1,5},{5,1},{9,13},{13,9},{2,6},{6,2},{1... | collective-permute-start | bytes 786440 | tf_op jit(solution)/shard_map/cond/branch_1_fun/ppermute | solution.py:122

commit v5 on v4

--- a/solution.py
+++ b/solution.py
@@ -120,6 +120,32 @@
 def across(value, distance):
     count = lax.axis_size("ctx")
     return lax.ppermute(value, "ctx", [(i, i ^ distance) for i in range(count)])
+
+
+VMEM = pl.BlockSpec(memory_space=pltpu.VMEM)
+
+
+def local_call(kernel, out_shapes, *operands, scratch=(), flops=0):
+    moved = sum(math.prod(o.shape) * o.dtype.itemsize for o in operands)
+    return pl.pallas_call(
+        kernel,
+        out_shape=[jax.ShapeDtypeStruct(shape, jnp.bfloat16) for shape in out_shapes],
+        in_specs=[VMEM] * len(operands),
+        out_specs=[VMEM] * len(out_shapes),
+        scratch_shapes=list(scratch),
+        compiler_params=pltpu.CompilerParams(vmem_limit_bytes=16 * 2**20),
+        cost_estimate=pl.CostEstimate(flops=flops, bytes_accessed=moved, transcendentals=0),
+    )(*operands)
+
+
+def where_am_i():
+    z, x = lax.axis_index("ctx"), lax.axis_index("chan")
+    pair, bit = z // 2, z % 2
+    return z, x, pair, bit
+
+
+def span(index, size):
+    return pl.ds(pl.multiple_of(index * size, size), size)
 
 
 def gated_kernel(place, row_ref, *refs):
@@ -217,6 +243,28 @@
     )(place, *mine, other, out_weight, near_w, far_w)
 
 
+def project_whole_kernel(*refs):
+    mine, other, own_w, near_w, far_w, outs = refs[:4], *refs[4:8], refs[8:10]
+    _, x, _, bit = where_am_i()
+    group, same = lax.axis_index("group"), lax.axis_index("sub") == bit
+    tokens, width = mine[0].shape
+    half = tokens // 2
+    columns = near_w.shape[1]
+    for slot in range(2):
+        rows = span(slot ^ bit, half)
+        for got_w, index in ((near_w, group), (far_w, 1 - group)):
+            total = jnp.zeros((half, columns), jnp.float32)
+            for flip in range(4):
+                here, there = mine[flip][rows, :], other[flip, rows, :]
+                first = jnp.where(same, here, there)
+                second = jnp.where(same, there, here)
+                block = span((2 * x + bit) ^ flip, width)
+                own_part = own_w[block, span(2 * bit + index, columns)]
+                total += jnp.dot(first, own_part, preferred_element_type=jnp.float32)
+                total += jnp.dot(second, got_w[block, :], preferred_element_type=jnp.float32)
+            outs[slot][:, span(index, columns)] = total.astype(outs[slot].dtype)
+
+
 def paired_plan(q_proj, k_proj, v_proj, filters, filter_blocks, out_weight):
     block, channels = q_proj.shape
     groups = filters.shape[0]
@@ -280,7 +328,11 @@
         return [gated, swap(gated, "ctx"), swap(gated, "chan"), swap(gated, "ctx", "chan")]
 
     def partials(mine):
-        return project(place, mine, swap(jnp.stack(mine), "sub"), out_weight, w_near, w_far)
+        other = swap(jnp.stack(mine), "sub")
+        return local_call(
+            project_whole_kernel, [(block, half)] * 2, *mine, other, out_weight, w_near, w_far,
+            flops=8 * block * channels * half // 2,
+        )
 
     far = partials(gathered(gated_far))
     far_own, far_near = across(far[0], 2), across(far[1], 3)

time: 91.2 us -> 89.3 us (0.979)
  Pallas kernels: 7.86 us -> 6.53 us
    pallas_call x2, Pallas kernels: 6.15 us -> 4.94 us  [local_call(): pl.pallas_call(kernel, out_shape=[jax.ShapeDtypeStruct(shape, jnp.bfloat1...]
  transfers between devices with their start and end apart: 18 -> 18, of which waited for: 11 -> 12; matrix products, arithmetic and copies ran while one was open for 10% -> 10% of each run, Pallas kernels for 7% -> 6%
where the time goes in v5:
time: 89.3 us; the launch traced here: 88.9 us
  waiting for transfers between devices  46.4 us (52%)
  starting transfers between devices  20.8 us (23%)
  other arithmetic  9.43 us (11%)
  Pallas kernels  6.53 us (7%)
  local copies, waits for them, and re-layouts  5.05 us (6%)
    ppermute x11, waiting for transfers between devices, swap(): return lax.ppermute(value, axes, [(i, i ^ flip) for i in range(total)])  29.8 us
    ppermute x7, waiting for transfers between devices, across(): return lax.ppermute(value, 'ctx', [(i, i ^ distance) for i in range(count)])  16.6 us
    ppermute x11, starting transfers between devices, swap(): return lax.ppermute(value, axes, [(i, i ^ flip) for i in range(total)])  10.9 us
    ppermute x7, starting transfers between devices, across(): return lax.ppermute(value, 'ctx', [(i, i ^ distance) for i in range(count)])  9.93 us
    pallas_call x2, Pallas kernels, local_call(): pl.pallas_call(kernel, out_shape=[jax.ShapeDtypeStruct(shape, jnp.bfloat1...  4.94 us
    another operation x3, other arithmetic, packed(): return jnp.stack([product, q])  2.21 us
  transfers between devices with their start and end apart: 18, of which 12 were waited for; matrix products, arithmetic and copies ran while one was open for 10% of the time, Pallas kernels for 6%

profile of v5, /device:TPU:0, one launch (start us, length us, event | category | flops | bytes accessed | tf_op | source)
XLA Modules:
  0.0 88.9 jit_solution(5442046741878722565)
XLA Ops:
  0.0 1.3 %dynamic-slice_bitcast_fusion = (bf16[1,256,256]{2,1,0:T(8,128)(2,1)S(1)}, bf16[1,256,256]{2,1,0:T(8,128)(2,1)S(1)}, bf16[1,256,256]{2,1,0:T(8,128)(2,1)S(1)}, bf16[1,256,256]{2,1,0:T(8,128)(2,1)S(1)}) fusion(bf16[256,1024]{1,0:T(8,128)(2,1)} %param.8, s32[]{:T(128)S(6)} %select_n.98, s32[]{:T(128)S(6)} %select_n.95, s32[]{:T(128)S(6)} %select_n.90, ...), kind=kLoop, calls=%fused_computation.24 | loop fusion | bytes 1048592 | tf_op jit(solution)/shard_map/stack | solution.py:284
  1.3 1.4 %fusion.3 = (bf16[1,256,256]{2,1,0:T(8,128)(2,1)S(1)}, bf16[1,256,256]{2,1,0:T(8,128)(2,1)S(1)}, bf16[1,256,256]{2,1,0:T(8,128)(2,1)S(1)}, bf16[1,256,256]{2,1,0:T(8,128)(2,1)S(1)}) fusion(bf16[256,1024]{1,0:T(8,128)(2,1)} %param.10, s32[]{:T(128)S(6)} %select_n.98, bf16[256,1024]{1,0:T(8,128)(2,1)} %param.9, s32[]{:T(128)S(6)} %select_n.95, ...), kind=kLoop, calls=%fused_computation.23 | loop fusion | flops 1048576 | bytes 1572880 | tf_op jit(solution)/shard_map/stack | solution.py:284
  3.5 2.9 %collective-permute-start.6 = (bf16[2,256,256]{2,1,0:T(8,128)(2,1)}, bf16[2,256,256]{2,1,0:T(8,128)(2,1)}, u32[]{:S(2)}, u32[]{:S(2)}) collective-permute-start(bf16[2,256,256]{2,1,0:T(8,128)(2,1)} %pad_maximum_fusion.5), channel_id=1, source_target_pairs={{0,2},{2,0},{1,3},{3,1},{4,6},{6,4},{5,7},{7,5},{8,10},{10,8},{9,1... | collective-permute-start | bytes 786440 | tf_op jit(solution)/shard_map/ppermute | solution.py:117
  7.3 1.6 %collective-permute-start.4 = (bf16[1024,256]{1,0:T(8,128)(2,1)}, bf16[1024,256]{1,0:T(8,128)(2,1)}, u32[]{:S(2)}, u32[]{:S(2)}) collective-permute-start(bf16[1024,256]{1,0:T(8,128)(2,1)} %constant_dynamic-slice_fusion), channel_id=1, source_target_pairs={{0,4},{4,0},{8,12},{12,8},{1,5},{5,1},{9,13},{13,9},{2,6},{6,2},{1... | collective-permute-start | bytes 1572872 | tf_op jit(solution)/shard_map/ppermute | solution.py:122
  11.9 1.6 %collective-permute-done.6 = bf16[2,256,256]{2,1,0:T(8,128)(2,1)} collective-permute-done((bf16[2,256,256]{2,1,0:T(8,128)(2,1)}, bf16[2,256,256]{2,1,0:T(8,128)(2,1)}, u32[]{:S(2)}, u32[]{:S(2)}) %collective-permute-start.6) | collective-permute-done | bytes 262176 | tf_op jit(solution)/shard_map/ppermute | solution.py:117
  13.5 1.7 %broadcast_select_fusion.1 = (bf16[2,256,256]{2,1,0:T(8,128)(2,1)}, bf16[2,256,256]{2,1,0:T(8,128)(2,1)S(1)}) fusion(bf16[2,256,256]{2,1,0:T(8,128)(2,1)} %collective-permute-done.6, pred[]{:T(512)S(6)} %eq.14, bf16[1,256,256]{2,1,0:T(8,128)(2,1)S(1)} %get-tuple-element.56, bf16[1,256,256]{2,1,0:T(8,128)(2,1)S(1)} %get-tuple-element.48), kind=kLoop, calls=%fused_computation.17 | loop fusion | flops 393216 | bytes 1048577 | tf_op jit(solution)/shard_map/jit(_where)/select_n | solution.py:309
  15.2 2.9 %collective-permute-start.8 = (bf16[2,256,256]{2,1,0:T(8,128)(2,1)}, bf16[2,256,256]{2,1,0:T(8,128)(2,1)S(1)}, u32[]{:S(2)}, u32[]{:S(2)}) collective-permute-start(bf16[2,256,256]{2,1,0:T(8,128)(2,1)} %get-tuple-element.53), channel_id=1, source_target_pairs={{0,8},{4,12},{8,0},{12,4},{1,9},{5,13},{9,1},{13,5},{2,10},{6,14},... | collective-permute-start | bytes 786440 | tf_op jit(solution)/shard_map/ppermute | solution.py:122
  19.8 6.4 %collective-permute-done.4.refs_6_ = bf16[1024,256]{1,0:T(8,128)(2,1)} collective-permute-done((bf16[1024,256]{1,0:T(8,128)(2,1)}, bf16[1024,256]{1,0:T(8,128)(2,1)}, u32[]{:S(2)}, u32[]{:S(2)}) %collective-permute-start.4) | collective-permute-done | bytes 524320 | tf_op jit(solution)/shard_map/ppermute | solution.py:122
  26.2 1.6 %collective-permute-start.5 = (bf16[1024,256]{1,0:T(8,128)(2,1)}, bf16[1024,256]{1,0:T(8,128)(2,1)}, u32[]{:S(2)}, u32[]{:S(2)}) collective-permute-start(bf16[1024,256]{1,0:T(8,128)(2,1)} %collective-permute-done.4.refs_6_), channel_id=1, source_target_pairs={{0,16},{16,0},{1,17},{17,1},{2,18},{18,2},{3,19},{19,3},{4,20},{20... | collective-permute-start | bytes 1572872 | tf_op jit(solution)/shard_map/ppermute | solution.py:117
  28.5 1.3 %collective-permute-start.9 = (bf16[2,256,256]{2,1,0:T(8,128)(2,1)S(1)}, bf16[2,256,256]{2,1,0:T(8,128)(2,1)S(1)}, u32[]{:S(2)}, u32[]{:S(2)}) collective-permute-start(bf16[2,256,256]{2,1,0:T(8,128)(2,1)S(1)} %get-tuple-element.51), channel_id=1, source_target_pairs={{0,12},{4,8},{8,4},{12,0},{1,13},{5,9},{9,5},{13,1},{2,14},{6,10},... | collective-permute-start | bytes 786440 | tf_op jit(solution)/shard_map/ppermute | solution.py:122
  31.7 7.3 %collective-permute-done.5.refs_7_ = bf16[1024,256]{1,0:T(8,128)(2,1)} collective-permute-done((bf16[1024,256]{1,0:T(8,128)(2,1)}, bf16[1024,256]{1,0:T(8,128)(2,1)}, u32[]{:S(2)}, u32[]{:S(2)}) %collective-permute-start.5) | collective-permute-done | bytes 524320 | tf_op jit(solution)/shard_map/ppermute | solution.py:117
  39.0 1.9 %collective-permute-done.7.refs_1_ = bf16[2,256,256]{2,1,0:T(8,128)(2,1)S(1)} collective-permute-done((bf16[2,256,256]{2,1,0:T(8,128)(2,1)}, bf16[2,256,256]{2,1,0:T(8,128)(2,1)S(1)}, u32[]{:S(2)}, u32[]{:S(2)}) %collective-permute-start.7) | collective-permute-done | bytes 262176 | tf_op jit(solution)/shard_map/ppermute | solution.py:122
  41.0 1.6 %shard_map.64 = (bf16[512,256]{1,0:T(8,128)(2,1)S(1)}, bf16[512,256]{1,0:T(8,128)(2,1)S(1)}) custom-call(s32[6]{0:T(128)S(1)} %stack.97.place, f32[2,768]{1,0:T(2,128)S(1)} %maximum_maximum_fusion.1.row_ref, bf16[2,256,256]{2,1,0:T(8,128)(2,1)S(1)} %get-tuple-element.54.refs_0_, bf16[2,256,256]{2,1,0:T(8,128)(2,1)S(1)} %collective-permute-done.7.refs_1_, ...), custom_call_target="tpu_custom_call" | custom-call | flops 402653184 | bytes 2097152 | tf_op jit(solution)/shard_map/pallas_call | solution.py:179
  42.5 1.6 %collective-permute-start.12 = (bf16[512,256]{1,0:T(8,128)(2,1)S(1)}, bf16[512,256]{1,0:T(8,128)(2,1)S(1)}, u32[]{:S(2)}, u32[]{:S(2)}) collective-permute-start(bf16[512,256]{1,0:T(8,128)(2,1)S(1)} %get-tuple-element.41.refs_0_), channel_id=1, source_target_pairs={{0,4},{4,0},{8,12},{12,8},{1,5},{5,1},{9,13},{13,9},{2,6},{6,2},{1... | collective-permute-start | bytes 786440 | tf_op jit(solution)/shard_map/ppermute | solution.py:117
  44.1 2.0 %collective-permute-start.14 = (bf16[512,256]{1,0:T(8,128)(2,1)S(1)}, bf16[512,256]{1,0:T(8,128)(2,1)S(1)}, u32[]{:S(2)}, u32[]{:S(2)}) collective-permute-start(bf16[512,256]{1,0:T(8,128)(2,1)S(1)} %get-tuple-element.41.refs_0_), channel_id=1, source_target_pairs={{0,6},{2,4},{4,2},{6,0},{8,14},{10,12},{12,10},{14,8},{1,7},{3,5},... | collective-permute-start | bytes 786440 | tf_op jit(solution)/shard_map/ppermute | solution.py:117
  46.1 4.9 %collective-permute-done.12.refs_1_ = bf16[512,256]{1,0:T(8,128)(2,1)S(1)} collective-permute-done((bf16[512,256]{1,0:T(8,128)(2,1)S(1)}, bf16[512,256]{1,0:T(8,128)(2,1)S(1)}, u32[]{:S(2)}, u32[]{:S(2)}) %collective-permute-start.12) | collective-permute-done | bytes 262176 | tf_op jit(solution)/shard_map/ppermute | solution.py:117
  51.0 4.0 %collective-permute-done.13.refs_2_ = bf16[512,256]{1,0:T(8,128)(2,1)S(1)} collective-permute-done((bf16[512,256]{1,0:T(8,128)(2,1)S(1)}, bf16[512,256]{1,0:T(8,128)(2,1)S(1)}, u32[]{:S(2)}, u32[]{:S(2)}) %collective-permute-start.13) | collective-permute-done | bytes 262176 | tf_op jit(solution)/shard_map/ppermute | solution.py:117
  57.8 2.5 %shard_map.65 = (bf16[256,512]{1,0:T(8,128)(2,1)S(1)}, bf16[256,512]{1,0:T(8,128)(2,1)S(1)}) custom-call(bf16[512,256]{1,0:T(8,128)(2,1)S(1)} %get-tuple-element.41.refs_0_, bf16[512,256]{1,0:T(8,128)(2,1)S(1)} %collective-permute-done.12.refs_1_, bf16[512,256]{1,0:T(8,128)(2,1)S(1)} %collective-permute-done.13.refs_2_, ...), custom_call_target="tpu_custom_call" | custom-call | flops 536870912 | bytes 5242880 | tf_op jit(solution)/shard_map/pallas_call | solution.py:130
  60.2 2.9 %collective-permute-start.16 = (bf16[256,512]{1,0:T(8,128)(2,1)S(1)}, bf16[256,512]{1,0:T(8,128)(2,1)}, u32[]{:S(2)}, u32[]{:S(2)}) collective-permute-start(bf16[256,512]{1,0:T(8,128)(2,1)S(1)} %get-tuple-element.42), channel_id=1, source_target_pairs={{0,8},{4,12},{8,0},{12,4},{1,9},{5,13},{9,1},{13,5},{2,10},{6,14},... | collective-permute-start | bytes 786440 | tf_op jit(solution)/shard_map/ppermute | solution.py:122
  64.7 22.1 %conditional.1 = (f32[256,512]{1,0:T(8,128)S(1)}, f32[256,512]{1,0:T(8,128)S(1)}) conditional(s32[]{:T(128)} %convert_element_type.64, () %tuple.18, (bf16[512,256]{1,0:T(8,128)(2,1)S(1)}, bf16[512,256]{1,0:T(8,128)(2,1)S(1)}, bf16[512,256]{1,0:T(8,128)(2,1)S(1)}, bf16[1024,1024]{1,0:T(8,128)(2,1)S(1)}, bf16[1024,256]{1,0:T(8,128)(2,1)}, ...), branch_computations={%region_1.2_spmd, %region_2.3_spmd} | conditional | flops 538705920 | bytes 15204488 | solution.py:349
  65.5 7.2 %collective-permute-done.refs_3_ = bf16[512,256]{1,0:T(8,128)(2,1)S(1)} collective-permute-done((bf16[512,256]{1,0:T(8,128)(2,1)S(1)}, bf16[512,256]{1,0:T(8,128)(2,1)S(1)}, u32[]{:S(2)}, u32[]{:S(2)}) %collective-permute-start) | collective-permute-done | bytes 262176 | tf_op jit(solution)/shard_map/cond/branch_1_fun/ppermute | solution.py:117
  72.9 2.6 %collective-permute-done.1.refs_4_ = bf16[4,512,256]{2,1,0:T(8,128)(2,1)S(1)} collective-permute-done((bf16[4,512,256]{2,1,0:T(8,128)(2,1)S(1)}, bf16[4,512,256]{2,1,0:T(8,128)(2,1)S(1)}, u32[]{:S(2)}, u32[]{:S(2)}) %collective-permute-start.1) | collective-permute-done | bytes 1048608 | tf_op jit(solution)/shard_map/cond/branch_1_fun/ppermute | solution.py:117
  75.5 2.5 %branch_1_fun.1 = (bf16[256,512]{1,0:T(8,128)(2,1)S(1)}, bf16[256,512]{1,0:T(8,128)(2,1)S(1)}) custom-call(bf16[512,256]{1,0:T(8,128)(2,1)S(1)} %get-tuple-element.19.refs_0_, bf16[512,256]{1,0:T(8,128)(2,1)S(1)} %get-tuple-element.20.refs_1_, bf16[512,256]{1,0:T(8,128)(2,1)S(1)} %get-tuple-element.21.refs_2_, ...), custom_call_target="tpu_custom_call" | custom-call | flops 536870912 | bytes 5242880 | tf_op jit(solution)/shard_map/cond/branch_1_fun/pallas_call | solution.py:130
  78.6 8.2 %collective-permute-done.2 = bf16[256,512]{1,0:T(8,128)(2,1)S(1)} collective-permute-done((bf16[256,512]{1,0:T(8,128)(2,1)S(1)}, bf16[256,512]{1,0:T(8,128)(2,1)S(1)}, u32[]{:S(2)}, u32[]{:S(2)}) %collective-permute-start.2) | collective-permute-done | bytes 262176 | tf_op jit(solution)/shard_map/cond/branch_1_fun/ppermute | solution.py:122
  (52 shorter events, 16.4 us)
Async XLA Ops:
  0.0 6.4 %copy-start = (bf16[1024,1024]{1,0:T(8,128)(2,1)S(1)}, bf16[1024,1024]{1,0:T(8,128)(2,1)}, u32[]{:S(2)}) copy-start(bf16[1024,1024]{1,0:T(8,128)(2,1)} %refs_5_.1) | copy-start | bytes 6291460
  0.0 8.9 %copy-start.2 = (s32[8]{0:T(128)S(1)}, s32[8]{0:T(128)}, u32[]{:S(2)}) copy-start(s32[8]{0:T(128)} %param.12) | copy-start | bytes 100
  1.3 8.3 %copy-start.1 = (f32[8,512]{1,0:T(8,128)S(1)}, f32[8,512]{1,0:T(8,128)}, u32[]{:S(2)}) copy-start(f32[8,512]{1,0:T(8,128)} %param.11) | copy-start | bytes 49156
  3.5 10.0 %collective-permute-start.6 = (bf16[2,256,256]{2,1,0:T(8,128)(2,1)}, bf16[2,256,256]{2,1,0:T(8,128)(2,1)}, u32[]{:S(2)}, u32[]{:S(2)}) collective-permute-start(bf16[2,256,256]{2,1,0:T(8,128)(2,1)} %pad_maximum_fusion.5), channel_id=1, source_target_pairs={{0,2},{2,0},{1,3},{3,1},{4,6},{6,4},{5,7},{7,5},{8,10},{10,8},{9,1... | collective-permute-start | bytes 786440 | tf_op jit(solution)/shard_map/ppermute | solution.py:117
  7.3 18.9 %collective-permute-start.4 = (bf16[1024,256]{1,0:T(8,128)(2,1)}, bf16[1024,256]{1,0:T(8,128)(2,1)}, u32[]{:S(2)}, u32[]{:S(2)}) collective-permute-start(bf16[1024,256]{1,0:T(8,128)(2,1)} %constant_dynamic-slice_fusion), channel_id=1, source_target_pairs={{0,4},{4,0},{8,12},{12,8},{1,5},{5,1},{9,13},{13,9},{2,6},{6,2},{1... | collective-permute-start | bytes 1572872 | tf_op jit(solution)/shard_map/ppermute | solution.py:122
  10.6 8.2 %collective-permute-start.3 = (bf16[528,256]{1,0:T(8,128)(2,1)}, bf16[528,256]{1,0:T(8,128)(2,1)}, u32[]{:S(2)}, u32[]{:S(2)}) collective-permute-start(bf16[528,256]{1,0:T(8,128)(2,1)} %maximum_maximum_fusion), channel_id=1, source_target_pairs={{0,2},{2,0},{1,3},{3,1},{4,6},{6,4},{5,7},{7,5},{8,10},{10,8},{9,1... | collective-permute-start | bytes 811016 | tf_op jit(solution)/shard_map/ppermute | solution.py:117
  15.2 23.8 %collective-permute-start.8 = (bf16[2,256,256]{2,1,0:T(8,128)(2,1)}, bf16[2,256,256]{2,1,0:T(8,128)(2,1)S(1)}, u32[]{:S(2)}, u32[]{:S(2)}) collective-permute-start(bf16[2,256,256]{2,1,0:T(8,128)(2,1)} %get-tuple-element.53), channel_id=1, source_target_pairs={{0,8},{4,12},{8,0},{12,4},{1,9},{5,13},{9,1},{13,5},{2,10},{6,14},... | collective-permute-start | bytes 786440 | tf_op jit(solution)/shard_map/ppermute | solution.py:122
  26.2 12.8 %collective-permute-start.5 = (bf16[1024,256]{1,0:T(8,128)(2,1)}, bf16[1024,256]{1,0:T(8,128)(2,1)}, u32[]{:S(2)}, u32[]{:S(2)}) collective-permute-start(bf16[1024,256]{1,0:T(8,128)(2,1)} %collective-permute-done.4.refs_6_), channel_id=1, source_target_pairs={{0,16},{16,0},{1,17},{17,1},{2,18},{18,2},{3,19},{19,3},{4,20},{20... | collective-permute-start | bytes 1572872 | tf_op jit(solution)/shard_map/ppermute | solution.py:117
  28.5 12.4 %collective-permute-start.7 = (bf16[2,256,256]{2,1,0:T(8,128)(2,1)}, bf16[2,256,256]{2,1,0:T(8,128)(2,1)S(1)}, u32[]{:S(2)}, u32[]{:S(2)}) collective-permute-start(bf16[2,256,256]{2,1,0:T(8,128)(2,1)} %get-tuple-element.52), channel_id=1, source_target_pairs={{0,4},{4,0},{8,12},{12,8},{1,5},{5,1},{9,13},{13,9},{2,6},{6,2},{1... | collective-permute-start | bytes 786440 | tf_op jit(solution)/shard_map/ppermute | solution.py:122
  28.5 12.4 %collective-permute-start.9 = (bf16[2,256,256]{2,1,0:T(8,128)(2,1)S(1)}, bf16[2,256,256]{2,1,0:T(8,128)(2,1)S(1)}, u32[]{:S(2)}, u32[]{:S(2)}) collective-permute-start(bf16[2,256,256]{2,1,0:T(8,128)(2,1)S(1)} %get-tuple-element.51), channel_id=1, source_target_pairs={{0,12},{4,8},{8,4},{12,0},{1,13},{5,9},{9,5},{13,1},{2,14},{6,10},... | collective-permute-start | bytes 786440 | tf_op jit(solution)/shard_map/ppermute | solution.py:122
  42.5 8.4 %collective-permute-start.12 = (bf16[512,256]{1,0:T(8,128)(2,1)S(1)}, bf16[512,256]{1,0:T(8,128)(2,1)S(1)}, u32[]{:S(2)}, u32[]{:S(2)}) collective-permute-start(bf16[512,256]{1,0:T(8,128)(2,1)S(1)} %get-tuple-element.41.refs_0_), channel_id=1, source_target_pairs={{0,4},{4,0},{8,12},{12,8},{1,5},{5,1},{9,13},{13,9},{2,6},{6,2},{1... | collective-permute-start | bytes 786440 | tf_op jit(solution)/shard_map/ppermute | solution.py:117
  44.1 10.8 %collective-permute-start.13 = (bf16[512,256]{1,0:T(8,128)(2,1)S(1)}, bf16[512,256]{1,0:T(8,128)(2,1)S(1)}, u32[]{:S(2)}, u32[]{:S(2)}) collective-permute-start(bf16[512,256]{1,0:T(8,128)(2,1)S(1)} %get-tuple-element.41.refs_0_), channel_id=1, source_target_pairs={{0,2},{2,0},{1,3},{3,1},{4,6},{6,4},{5,7},{7,5},{8,10},{10,8},{9,1... | collective-permute-start | bytes 786440 | tf_op jit(solution)/shard_map/ppermute | solution.py:117
  44.1 10.8 %collective-permute-start.14 = (bf16[512,256]{1,0:T(8,128)(2,1)S(1)}, bf16[512,256]{1,0:T(8,128)(2,1)S(1)}, u32[]{:S(2)}, u32[]{:S(2)}) collective-permute-start(bf16[512,256]{1,0:T(8,128)(2,1)S(1)} %get-tuple-element.41.refs_0_), channel_id=1, source_target_pairs={{0,6},{2,4},{4,2},{6,0},{8,14},{10,12},{12,10},{14,8},{1,7},{3,5},... | collective-permute-start | bytes 786440 | tf_op jit(solution)/shard_map/ppermute | solution.py:117
  55.0 2.7 %collective-permute-start.15 = (bf16[4,512,256]{2,1,0:T(8,128)(2,1)S(1)}, bf16[4,512,256]{2,1,0:T(8,128)(2,1)S(1)}, u32[]{:S(2)}, u32[]{:S(2)}) collective-permute-start(bf16[4,512,256]{2,1,0:T(8,128)(2,1)S(1)} %pad_maximum_fusion.1), channel_id=1, source_target_pairs={{0,1},{1,0},{2,3},{3,2},{4,5},{5,4},{6,7},{7,6},{8,9},{9,8},{10,11... | collective-permute-start | bytes 3145736 | tf_op jit(solution)/shard_map/ppermute | solution.py:117
  55.1 9.4 %collective-permute-start.10 = (bf16[512,256]{1,0:T(8,128)(2,1)S(1)}, bf16[512,256]{1,0:T(8,128)(2,1)S(1)}, u32[]{:S(2)}, u32[]{:S(2)}) collective-permute-start(bf16[512,256]{1,0:T(8,128)(2,1)S(1)} %get-tuple-element.37), channel_id=1, source_target_pairs={{0,4},{4,0},{8,12},{12,8},{1,5},{5,1},{9,13},{13,9},{2,6},{6,2},{1... | collective-permute-start | bytes 786440 | tf_op jit(solution)/shard_map/ppermute | solution.py:117
  56.4 8.4 %collective-permute-start.11 = (bf16[512,256]{1,0:T(8,128)(2,1)S(1)}, bf16[512,256]{1,0:T(8,128)(2,1)S(1)}, u32[]{:S(2)}, u32[]{:S(2)}) collective-permute-start(bf16[512,256]{1,0:T(8,128)(2,1)S(1)} %get-tuple-element.37), channel_id=1, source_target_pairs={{0,2},{2,0},{1,3},{3,1},{4,6},{6,4},{5,7},{7,5},{8,10},{10,8},{9,1... | collective-permute-start | bytes 786440 | tf_op jit(solution)/shard_map/ppermute | solution.py:117
  60.2 26.6 %collective-permute-start.16 = (bf16[256,512]{1,0:T(8,128)(2,1)S(1)}, bf16[256,512]{1,0:T(8,128)(2,1)}, u32[]{:S(2)}, u32[]{:S(2)}) collective-permute-start(bf16[256,512]{1,0:T(8,128)(2,1)S(1)} %get-tuple-element.42), channel_id=1, source_target_pairs={{0,8},{4,12},{8,0},{12,4},{1,9},{5,13},{9,1},{13,5},{2,10},{6,14},... | collective-permute-start | bytes 786440 | tf_op jit(solution)/shard_map/ppermute | solution.py:122
  63.1 23.7 %collective-permute-start.17 = (bf16[256,512]{1,0:T(8,128)(2,1)S(1)}, bf16[256,512]{1,0:T(8,128)(2,1)}, u32[]{:S(2)}, u32[]{:S(2)}) collective-permute-start(bf16[256,512]{1,0:T(8,128)(2,1)S(1)} %get-tuple-element.44), channel_id=1, source_target_pairs={{0,12},{4,8},{8,4},{12,0},{1,13},{5,9},{9,5},{13,1},{2,14},{6,10},... | collective-permute-start | bytes 786440 | tf_op jit(solution)/shard_map/ppermute | solution.py:122
  64.7 7.9 %collective-permute-start = (bf16[512,256]{1,0:T(8,128)(2,1)S(1)}, bf16[512,256]{1,0:T(8,128)(2,1)S(1)}, u32[]{:S(2)}, u32[]{:S(2)}) collective-permute-start(bf16[512,256]{1,0:T(8,128)(2,1)S(1)} %get-tuple-element.20.refs_1_), channel_id=1, source_target_pairs={{0,2},{2,0},{1,3},{3,1},{4,6},{6,4},{5,7},{7,5},{8,10},{10,8},{9,1... | collective-permute-start | bytes 786440 | tf_op jit(solution)/shard_map/cond/branch_1_fun/ppermute | solution.py:117
  72.8 2.7 %collective-permute-start.1 = (bf16[4,512,256]{2,1,0:T(8,128)(2,1)S(1)}, bf16[4,512,256]{2,1,0:T(8,128)(2,1)S(1)}, u32[]{:S(2)}, u32[]{:S(2)}) collective-permute-start(bf16[4,512,256]{2,1,0:T(8,128)(2,1)S(1)} %pad_maximum_fusion), channel_id=1, source_target_pairs={{0,1},{1,0},{2,3},{3,2},{4,5},{5,4},{6,7},{7,6},{8,9},{9,8},{10,11... | collective-permute-start | bytes 3145736 | tf_op jit(solution)/shard_map/cond/branch_1_fun/ppermute | solution.py:117
  78.0 8.8 %collective-permute-start.2 = (bf16[256,512]{1,0:T(8,128)(2,1)S(1)}, bf16[256,512]{1,0:T(8,128)(2,1)S(1)}, u32[]{:S(2)}, u32[]{:S(2)}) collective-permute-start(bf16[256,512]{1,0:T(8,128)(2,1)S(1)} %get-tuple-element.26), channel_id=1, source_target_pairs={{0,4},{4,0},{8,12},{12,8},{1,5},{5,1},{9,13},{13,9},{2,6},{6,2},{1... | collective-permute-start | bytes 786440 | tf_op jit(solution)/shard_map/cond/branch_1_fun/ppermute | solution.py:122

commit v6 on v5

--- a/solution.py
+++ b/solution.py
@@ -250,19 +250,36 @@
     tokens, width = mine[0].shape
     half = tokens // 2
     columns = near_w.shape[1]
-    for slot in range(2):
-        rows = span(slot ^ bit, half)
+    blocks = [span((2 * x + bit) ^ flip, width) for flip in range(4)]
+
+    def fill(first, second):
         for got_w, index in ((near_w, group), (far_w, 1 - group)):
-            total = jnp.zeros((half, columns), jnp.float32)
-            for flip in range(4):
-                here, there = mine[flip][rows, :], other[flip, rows, :]
-                first = jnp.where(same, here, there)
-                second = jnp.where(same, there, here)
-                block = span((2 * x + bit) ^ flip, width)
-                own_part = own_w[block, span(2 * bit + index, columns)]
-                total += jnp.dot(first, own_part, preferred_element_type=jnp.float32)
-                total += jnp.dot(second, got_w[block, :], preferred_element_type=jnp.float32)
-            outs[slot][:, span(index, columns)] = total.astype(outs[slot].dtype)
+            place = span(2 * bit + index, columns)
+            own_part = jnp.concatenate([own_w[block, place] for block in blocks], axis=0)
+            got_part = jnp.concatenate([got_w[block, :] for block in blocks], axis=0)
+            for slot in range(2):
+                rows = span(slot ^ bit, half)
+                total = jnp.dot(
+                    jnp.concatenate([ref[rows, :] for ref in first], axis=1),
+                    own_part,
+                    preferred_element_type=jnp.float32,
+                )
+                total += jnp.dot(
+                    jnp.concatenate([ref[rows, :] for ref in second], axis=1),
+                    got_part,
+                    preferred_element_type=jnp.float32,
+                )
+                outs[slot][:, span(index, columns)] = total.astype(outs[slot].dtype)
+
+    others = [other.at[flip] for flip in range(4)]
+
+    @pl.when(same)
+    def _():
+        fill(mine, others)
+
+    @pl.when(jnp.logical_not(same))
+    def _():
+        fill(others, mine)
 
 
 def paired_plan(q_proj, k_proj, v_proj, filters, filter_blocks, out_weight):
@@ -294,6 +311,7 @@
     )
 
     same_send = packed(2 * (1 - x) + bit)
+    k_proj, v_proj, q_proj, same_send = lax.optimization_barrier((k_proj, v_proj, q_proj, same_send))
     flip_send = jnp.concatenate(
         [packed(2 * (1 - x) + 1 - bit).reshape(2 * block, fourth), filter_rows], axis=0
     )

time: 89.3 us -> 88.4 us (0.990)
  other arithmetic: 9.43 us -> 6.22 us
  starting transfers between devices: 20.8 us -> 22.7 us
  waiting for transfers between devices: 46.4 us -> 47.3 us
    ppermute x7, starting transfers between devices: 9.93 us -> 11.6 us  [across(): return lax.ppermute(value, 'ctx', [(i, i ^ distance) for i in range(count)])]
    ppermute x7, waiting for transfers between devices: 16.6 us -> 17.7 us  [across(): return lax.ppermute(value, 'ctx', [(i, i ^ distance) for i in range(count)])]
    select_n x1, other arithmetic: 1.71 us -> 0.74 us  [paired_plan(): piece_2 = across(jnp.where(inside, same_came, same_own), 2)]
    another operation x3 -> x4, other arithmetic: 2.21 us -> 1.27 us  [packed(): return jnp.stack([product, q])]
  transfers between devices with their start and end apart: 18 -> 18, of which waited for: 12 -> 12; matrix products, arithmetic and copies ran while one was open for 10% -> 7% of each run, Pallas kernels for 6% -> 6%
where the time goes in v6:
time: 88.4 us; the launch traced here: 88 us
  waiting for transfers between devices  47.3 us (54%)
  starting transfers between devices  22.7 us (26%)
  Pallas kernels  6.48 us (7%)
  other arithmetic  6.22 us (7%)
  local copies, waits for them, and re-layouts  4.49 us (5%)
    ppermute x11, waiting for transfers between devices, swap(): return lax.ppermute(value, axes, [(i, i ^ flip) for i in range(total)])  29.7 us
    ppermute x7, waiting for transfers between devices, across(): return lax.ppermute(value, 'ctx', [(i, i ^ distance) for i in range(count)])  17.7 us
    ppermute x7, starting transfers between devices, across(): return lax.ppermute(value, 'ctx', [(i, i ^ distance) for i in range(count)])  11.6 us
    ppermute x11, starting transfers between devices, swap(): return lax.ppermute(value, axes, [(i, i ^ flip) for i in range(total)])  11.1 us
    pallas_call x2, Pallas kernels, local_call(): pl.pallas_call(kernel, out_shape=[jax.ShapeDtypeStruct(shape, jnp.bfloat1...  4.89 us
  transfers between devices with their start and end apart: 18, of which 12 were waited for; matrix products, arithmetic and copies ran while one was open for 7% of the time, Pallas kernels for 6%

profile of v6, /device:TPU:0, one launch (start us, length us, event | category | flops | bytes accessed | tf_op | source)
XLA Modules:
  0.0 88.0 jit_solution(3204924356092237726)
XLA Ops:
  2.1 3.0 %collective-permute-start.6 = (bf16[2,256,256]{2,1,0:T(8,128)(2,1)S(1)}, bf16[2,256,256]{2,1,0:T(8,128)(2,1)S(1)}, u32[]{:S(2)}, u32[]{:S(2)}) collective-permute-start(bf16[2,256,256]{2,1,0:T(8,128)(2,1)S(1)} %pad_maximum_fusion.3), channel_id=1, source_target_pairs={{0,2},{2,0},{1,3},{3,1},{4,6},{6,4},{5,7},{7,5},{8,10},{10,8},{9,1... | collective-permute-start | bytes 786440 | tf_op jit(solution)/shard_map/ppermute | solution.py:117
  6.2 1.6 %collective-permute-start.4 = (bf16[1024,256]{1,0:T(8,128)(2,1)S(1)}, bf16[1024,256]{1,0:T(8,128)(2,1)}, u32[]{:S(2)}, u32[]{:S(2)}) collective-permute-start(bf16[1024,256]{1,0:T(8,128)(2,1)S(1)} %constant_dynamic-slice_fusion), channel_id=1, source_target_pairs={{0,4},{4,0},{8,12},{12,8},{1,5},{5,1},{9,13},{13,9},{2,6},{6,2},{1... | collective-permute-start | bytes 1572872 | tf_op jit(solution)/shard_map/ppermute | solution.py:122
  9.9 1.9 %collective-permute-done.6 = bf16[2,256,256]{2,1,0:T(8,128)(2,1)S(1)} collective-permute-done((bf16[2,256,256]{2,1,0:T(8,128)(2,1)S(1)}, bf16[2,256,256]{2,1,0:T(8,128)(2,1)S(1)}, u32[]{:S(2)}, u32[]{:S(2)}) %collective-permute-start.6) | collective-permute-done | bytes 262176 | tf_op jit(solution)/shard_map/ppermute | solution.py:117
  12.6 3.0 %collective-permute-start.8 = (bf16[2,256,256]{2,1,0:T(8,128)(2,1)}, bf16[2,256,256]{2,1,0:T(8,128)(2,1)S(1)}, u32[]{:S(2)}, u32[]{:S(2)}) collective-permute-start(bf16[2,256,256]{2,1,0:T(8,128)(2,1)} %get-tuple-element.60), channel_id=1, source_target_pairs={{0,8},{4,12},{8,0},{12,4},{1,9},{5,13},{9,1},{13,5},{2,10},{6,14},... | collective-permute-start | bytes 786440 | tf_op jit(solution)/shard_map/ppermute | solution.py:122
  15.6 1.8 %collective-permute-done.3 = bf16[528,256]{1,0:T(8,128)(2,1)} collective-permute-done((bf16[528,256]{1,0:T(8,128)(2,1)S(1)}, bf16[528,256]{1,0:T(8,128)(2,1)}, u32[]{:S(2)}, u32[]{:S(2)}) %collective-permute-start.3) | collective-permute-done | bytes 270368 | tf_op jit(solution)/shard_map/ppermute | solution.py:117
  18.3 7.1 %collective-permute-done.4.refs_6_ = bf16[1024,256]{1,0:T(8,128)(2,1)} collective-permute-done((bf16[1024,256]{1,0:T(8,128)(2,1)S(1)}, bf16[1024,256]{1,0:T(8,128)(2,1)}, u32[]{:S(2)}, u32[]{:S(2)}) %collective-permute-start.4) | collective-permute-done | bytes 524320 | tf_op jit(solution)/shard_map/ppermute | solution.py:122
  25.4 1.5 %collective-permute-start.5 = (bf16[1024,256]{1,0:T(8,128)(2,1)}, bf16[1024,256]{1,0:T(8,128)(2,1)}, u32[]{:S(2)}, u32[]{:S(2)}) collective-permute-start(bf16[1024,256]{1,0:T(8,128)(2,1)} %collective-permute-done.4.refs_6_), channel_id=1, source_target_pairs={{0,16},{16,0},{1,17},{17,1},{2,18},{18,2},{3,19},{19,3},{4,20},{20... | collective-permute-start | bytes 1572872 | tf_op jit(solution)/shard_map/ppermute | solution.py:117
  27.8 2.2 %collective-permute-start.9 = (bf16[2,256,256]{2,1,0:T(8,128)(2,1)}, bf16[2,256,256]{2,1,0:T(8,128)(2,1)S(1)}, u32[]{:S(2)}, u32[]{:S(2)}) collective-permute-start(bf16[2,256,256]{2,1,0:T(8,128)(2,1)} %get-tuple-element.58), channel_id=1, source_target_pairs={{0,12},{4,8},{8,4},{12,0},{1,13},{5,9},{9,5},{13,1},{2,14},{6,10},... | collective-permute-start | bytes 786440 | tf_op jit(solution)/shard_map/ppermute | solution.py:122
  31.1 7.0 %collective-permute-done.5.refs_7_ = bf16[1024,256]{1,0:T(8,128)(2,1)} collective-permute-done((bf16[1024,256]{1,0:T(8,128)(2,1)}, bf16[1024,256]{1,0:T(8,128)(2,1)}, u32[]{:S(2)}, u32[]{:S(2)}) %collective-permute-start.5) | collective-permute-done | bytes 524320 | tf_op jit(solution)/shard_map/ppermute | solution.py:117
  38.2 2.6 %collective-permute-done.9.refs_3_ = bf16[2,256,256]{2,1,0:T(8,128)(2,1)S(1)} collective-permute-done((bf16[2,256,256]{2,1,0:T(8,128)(2,1)}, bf16[2,256,256]{2,1,0:T(8,128)(2,1)S(1)}, u32[]{:S(2)}, u32[]{:S(2)}) %collective-permute-start.9) | collective-permute-done | bytes 262176 | tf_op jit(solution)/shard_map/ppermute | solution.py:122
  40.8 1.6 %shard_map.64 = (bf16[512,256]{1,0:T(8,128)(2,1)S(1)}, bf16[512,256]{1,0:T(8,128)(2,1)S(1)}) custom-call(s32[6]{0:T(128)S(1)} %stack.97.place, f32[2,768]{1,0:T(2,128)S(1)} %maximum_maximum_fusion.1.row_ref, bf16[2,256,256]{2,1,0:T(8,128)(2,1)S(1)} %get-tuple-element.61.refs_0_, bf16[2,256,256]{2,1,0:T(8,128)(2,1)S(1)} %collective-permute-done.7.refs_1_, ...), custom_call_target="tpu_custom_call" | custom-call | flops 402653184 | bytes 2097152 | tf_op jit(solution)/shard_map/pallas_call | solution.py:179
  42.4 1.2 %collective-permute-start.12 = (bf16[512,256]{1,0:T(8,128)(2,1)S(1)}, bf16[512,256]{1,0:T(8,128)(2,1)S(1)}, u32[]{:S(2)}, u32[]{:S(2)}) collective-permute-start(bf16[512,256]{1,0:T(8,128)(2,1)S(1)} %get-tuple-element.49.refs_0_), channel_id=1, source_target_pairs={{0,4},{4,0},{8,12},{12,8},{1,5},{5,1},{9,13},{13,9},{2,6},{6,2},{1... | collective-permute-start | bytes 786440 | tf_op jit(solution)/shard_map/ppermute | solution.py:117
  43.9 2.0 %collective-permute-start.14 = (bf16[512,256]{1,0:T(8,128)(2,1)S(1)}, bf16[512,256]{1,0:T(8,128)(2,1)S(1)}, u32[]{:S(2)}, u32[]{:S(2)}) collective-permute-start(bf16[512,256]{1,0:T(8,128)(2,1)S(1)} %get-tuple-element.49.refs_0_), channel_id=1, source_target_pairs={{0,6},{2,4},{4,2},{6,0},{8,14},{10,12},{12,10},{14,8},{1,7},{3,5},... | collective-permute-start | bytes 786440 | tf_op jit(solution)/shard_map/ppermute | solution.py:117
  45.9 5.1 %collective-permute-done.12.refs_1_ = bf16[512,256]{1,0:T(8,128)(2,1)S(1)} collective-permute-done((bf16[512,256]{1,0:T(8,128)(2,1)S(1)}, bf16[512,256]{1,0:T(8,128)(2,1)S(1)}, u32[]{:S(2)}, u32[]{:S(2)}) %collective-permute-start.12) | collective-permute-done | bytes 262176 | tf_op jit(solution)/shard_map/ppermute | solution.py:117
  51.1 2.9 %collective-permute-done.13.refs_2_ = bf16[512,256]{1,0:T(8,128)(2,1)S(1)} collective-permute-done((bf16[512,256]{1,0:T(8,128)(2,1)S(1)}, bf16[512,256]{1,0:T(8,128)(2,1)S(1)}, u32[]{:S(2)}, u32[]{:S(2)}) %collective-permute-start.13) | collective-permute-done | bytes 262176 | tf_op jit(solution)/shard_map/ppermute | solution.py:117
  54.2 1.7 %collective-permute-start.10 = (bf16[512,256]{1,0:T(8,128)(2,1)S(1)}, bf16[512,256]{1,0:T(8,128)(2,1)S(1)}, u32[]{:S(2)}, u32[]{:S(2)}) collective-permute-start(bf16[512,256]{1,0:T(8,128)(2,1)S(1)} %get-tuple-element.45), channel_id=1, source_target_pairs={{0,4},{4,0},{8,12},{12,8},{1,5},{5,1},{9,13},{13,9},{2,6},{6,2},{1... | collective-permute-start | bytes 786440 | tf_op jit(solution)/shard_map/ppermute | solution.py:117
  56.8 2.4 %shard_map.65 = (bf16[256,512]{1,0:T(8,128)(2,1)S(1)}, bf16[256,512]{1,0:T(8,128)(2,1)S(1)}) custom-call(bf16[512,256]{1,0:T(8,128)(2,1)S(1)} %get-tuple-element.49.refs_0_, bf16[512,256]{1,0:T(8,128)(2,1)S(1)} %collective-permute-done.12.refs_1_, bf16[512,256]{1,0:T(8,128)(2,1)S(1)} %collective-permute-done.13.refs_2_, ...), custom_call_target="tpu_custom_call" | custom-call | flops 536870912 | bytes 5242880 | tf_op jit(solution)/shard_map/pallas_call | solution.py:130
  59.3 1.9 %collective-permute-start.16 = (bf16[256,512]{1,0:T(8,128)(2,1)S(1)}, bf16[256,512]{1,0:T(8,128)(2,1)}, u32[]{:S(2)}, u32[]{:S(2)}) collective-permute-start(bf16[256,512]{1,0:T(8,128)(2,1)S(1)} %get-tuple-element.50), channel_id=1, source_target_pairs={{0,8},{4,12},{8,0},{12,4},{1,9},{5,13},{9,1},{13,5},{2,10},{6,14},... | collective-permute-start | bytes 786440 | tf_op jit(solution)/shard_map/ppermute | solution.py:122
  61.1 2.2 %collective-permute-start.17 = (bf16[256,512]{1,0:T(8,128)(2,1)S(1)}, bf16[256,512]{1,0:T(8,128)(2,1)}, u32[]{:S(2)}, u32[]{:S(2)}) collective-permute-start(bf16[256,512]{1,0:T(8,128)(2,1)S(1)} %get-tuple-element.52), channel_id=1, source_target_pairs={{0,12},{4,8},{8,4},{12,0},{1,13},{5,9},{9,5},{13,1},{2,14},{6,10},... | collective-permute-start | bytes 786440 | tf_op jit(solution)/shard_map/ppermute | solution.py:122
  64.3 21.7 %conditional.1 = (f32[256,512]{1,0:T(8,128)S(1)}, f32[256,512]{1,0:T(8,128)S(1)}) conditional(s32[]{:T(128)} %convert_element_type.64, () %tuple.19, (bf16[512,256]{1,0:T(8,128)(2,1)S(1)}, bf16[512,256]{1,0:T(8,128)(2,1)S(1)}, bf16[512,256]{1,0:T(8,128)(2,1)S(1)}, bf16[1024,1024]{1,0:T(8,128)(2,1)S(1)}, bf16[1024,256]{1,0:T(8,128)(2,1)}, ...), branch_computations={%region_1.2_spmd, %region_2.3_spmd} | conditional | flops 538705920 | bytes 15204488 | solution.py:367
  64.6 7.3 %collective-permute-done.refs_3_ = bf16[512,256]{1,0:T(8,128)(2,1)S(1)} collective-permute-done((bf16[512,256]{1,0:T(8,128)(2,1)S(1)}, bf16[512,256]{1,0:T(8,128)(2,1)S(1)}, u32[]{:S(2)}, u32[]{:S(2)}) %collective-permute-start) | collective-permute-done | bytes 262176 | tf_op jit(solution)/shard_map/cond/branch_1_fun/ppermute | solution.py:117
  72.0 2.6 %collective-permute-done.1.refs_4_ = bf16[4,512,256]{2,1,0:T(8,128)(2,1)S(1)} collective-permute-done((bf16[4,512,256]{2,1,0:T(8,128)(2,1)S(1)}, bf16[4,512,256]{2,1,0:T(8,128)(2,1)S(1)}, u32[]{:S(2)}, u32[]{:S(2)}) %collective-permute-start.1) | collective-permute-done | bytes 1048608 | tf_op jit(solution)/shard_map/cond/branch_1_fun/ppermute | solution.py:117
  74.7 2.4 %branch_1_fun.1 = (bf16[256,512]{1,0:T(8,128)(2,1)S(1)}, bf16[256,512]{1,0:T(8,128)(2,1)S(1)}) custom-call(bf16[512,256]{1,0:T(8,128)(2,1)S(1)} %get-tuple-element.19.refs_0_, bf16[512,256]{1,0:T(8,128)(2,1)S(1)} %get-tuple-element.20.refs_1_, bf16[512,256]{1,0:T(8,128)(2,1)S(1)} %get-tuple-element.21.refs_2_, ...), custom_call_target="tpu_custom_call" | custom-call | flops 536870912 | bytes 5242880 | tf_op jit(solution)/shard_map/cond/branch_1_fun/pallas_call | solution.py:130
  77.9 8.0 %collective-permute-done.2 = bf16[256,512]{1,0:T(8,128)(2,1)S(1)} collective-permute-done((bf16[256,512]{1,0:T(8,128)(2,1)S(1)}, bf16[256,512]{1,0:T(8,128)(2,1)S(1)}, u32[]{:S(2)}, u32[]{:S(2)}) %collective-permute-start.2) | collective-permute-done | bytes 262176 | tf_op jit(solution)/shard_map/cond/branch_1_fun/ppermute | solution.py:122
  (60 shorter events, 14.0 us)
Async XLA Ops:
  0.0 8.5 %copy-start.3 = (bf16[256,1024]{1,0:T(8,128)(2,1)S(1)}, bf16[256,1024]{1,0:T(8,128)(2,1)}, u32[]{:S(2)}) copy-start(bf16[256,1024]{1,0:T(8,128)(2,1)} %param.8) | copy-start | bytes 1572868
  0.0 8.5 %copy-start.1 = (bf16[256,1024]{1,0:T(8,128)(2,1)S(1)}, bf16[256,1024]{1,0:T(8,128)(2,1)}, u32[]{:S(2)}) copy-start(bf16[256,1024]{1,0:T(8,128)(2,1)} %param.10) | copy-start | bytes 1572868
  0.0 8.6 %copy-start.2 = (bf16[256,1024]{1,0:T(8,128)(2,1)S(1)}, bf16[256,1024]{1,0:T(8,128)(2,1)}, u32[]{:S(2)}) copy-start(bf16[256,1024]{1,0:T(8,128)(2,1)} %param.9) | copy-start | bytes 1572868
  0.0 7.9 %copy-start.5 = (s32[8]{0:T(128)S(1)}, s32[8]{0:T(128)}, u32[]{:S(2)}) copy-start(s32[8]{0:T(128)} %param.12) | copy-start | bytes 100
  2.1 6.8 %copy-start.4 = (f32[8,512]{1,0:T(8,128)S(1)}, f32[8,512]{1,0:T(8,128)}, u32[]{:S(2)}) copy-start(f32[8,512]{1,0:T(8,128)} %param.11) | copy-start | bytes 49156
  2.1 9.7 %collective-permute-start.6 = (bf16[2,256,256]{2,1,0:T(8,128)(2,1)S(1)}, bf16[2,256,256]{2,1,0:T(8,128)(2,1)S(1)}, u32[]{:S(2)}, u32[]{:S(2)}) collective-permute-start(bf16[2,256,256]{2,1,0:T(8,128)(2,1)S(1)} %pad_maximum_fusion.3), channel_id=1, source_target_pairs={{0,2},{2,0},{1,3},{3,1},{4,6},{6,4},{5,7},{7,5},{8,10},{10,8},{9,1... | collective-permute-start | bytes 786440 | tf_op jit(solution)/shard_map/ppermute | solution.py:117
  6.2 19.2 %collective-permute-start.4 = (bf16[1024,256]{1,0:T(8,128)(2,1)S(1)}, bf16[1024,256]{1,0:T(8,128)(2,1)}, u32[]{:S(2)}, u32[]{:S(2)}) collective-permute-start(bf16[1024,256]{1,0:T(8,128)(2,1)S(1)} %constant_dynamic-slice_fusion), channel_id=1, source_target_pairs={{0,4},{4,0},{8,12},{12,8},{1,5},{5,1},{9,13},{13,9},{2,6},{6,2},{1... | collective-permute-start | bytes 1572872 | tf_op jit(solution)/shard_map/ppermute | solution.py:122
  9.2 8.2 %collective-permute-start.3 = (bf16[528,256]{1,0:T(8,128)(2,1)S(1)}, bf16[528,256]{1,0:T(8,128)(2,1)}, u32[]{:S(2)}, u32[]{:S(2)}) collective-permute-start(bf16[528,256]{1,0:T(8,128)(2,1)S(1)} %maximum_maximum_fusion), channel_id=1, source_target_pairs={{0,2},{2,0},{1,3},{3,1},{4,6},{6,4},{5,7},{7,5},{8,10},{10,8},{9,1... | collective-permute-start | bytes 811016 | tf_op jit(solution)/shard_map/ppermute | solution.py:117
  12.6 25.6 %collective-permute-start.8 = (bf16[2,256,256]{2,1,0:T(8,128)(2,1)}, bf16[2,256,256]{2,1,0:T(8,128)(2,1)S(1)}, u32[]{:S(2)}, u32[]{:S(2)}) collective-permute-start(bf16[2,256,256]{2,1,0:T(8,128)(2,1)} %get-tuple-element.60), channel_id=1, source_target_pairs={{0,8},{4,12},{8,0},{12,4},{1,9},{5,13},{9,1},{13,5},{2,10},{6,14},... | collective-permute-start | bytes 786440 | tf_op jit(solution)/shard_map/ppermute | solution.py:122
  25.4 12.8 %collective-permute-start.5 = (bf16[1024,256]{1,0:T(8,128)(2,1)}, bf16[1024,256]{1,0:T(8,128)(2,1)}, u32[]{:S(2)}, u32[]{:S(2)}) collective-permute-start(bf16[1024,256]{1,0:T(8,128)(2,1)} %collective-permute-done.4.refs_6_), channel_id=1, source_target_pairs={{0,16},{16,0},{1,17},{17,1},{2,18},{18,2},{3,19},{19,3},{4,20},{20... | collective-permute-start | bytes 1572872 | tf_op jit(solution)/shard_map/ppermute | solution.py:117
  26.9 29.9 %copy-start = (bf16[1024,1024]{1,0:T(8,128)(2,1)S(1)}, bf16[1024,1024]{1,0:T(8,128)(2,1)}, u32[]{:S(2)}) copy-start(bf16[1024,1024]{1,0:T(8,128)(2,1)} %refs_5_.1) | copy-start | bytes 6291460
  27.8 10.4 %collective-permute-start.7 = (bf16[2,256,256]{2,1,0:T(8,128)(2,1)}, bf16[2,256,256]{2,1,0:T(8,128)(2,1)S(1)}, u32[]{:S(2)}, u32[]{:S(2)}) collective-permute-start(bf16[2,256,256]{2,1,0:T(8,128)(2,1)} %get-tuple-element.59), channel_id=1, source_target_pairs={{0,4},{4,0},{8,12},{12,8},{1,5},{5,1},{9,13},{13,9},{2,6},{6,2},{1... | collective-permute-start | bytes 786440 | tf_op jit(solution)/shard_map/ppermute | solution.py:122
  27.8 13.0 %collective-permute-start.9 = (bf16[2,256,256]{2,1,0:T(8,128)(2,1)}, bf16[2,256,256]{2,1,0:T(8,128)(2,1)S(1)}, u32[]{:S(2)}, u32[]{:S(2)}) collective-permute-start(bf16[2,256,256]{2,1,0:T(8,128)(2,1)} %get-tuple-element.58), channel_id=1, source_target_pairs={{0,12},{4,8},{8,4},{12,0},{1,13},{5,9},{9,5},{13,1},{2,14},{6,10},... | collective-permute-start | bytes 786440 | tf_op jit(solution)/shard_map/ppermute | solution.py:122
  42.4 8.7 %collective-permute-start.12 = (bf16[512,256]{1,0:T(8,128)(2,1)S(1)}, bf16[512,256]{1,0:T(8,128)(2,1)S(1)}, u32[]{:S(2)}, u32[]{:S(2)}) collective-permute-start(bf16[512,256]{1,0:T(8,128)(2,1)S(1)} %get-tuple-element.49.refs_0_), channel_id=1, source_target_pairs={{0,4},{4,0},{8,12},{12,8},{1,5},{5,1},{9,13},{13,9},{2,6},{6,2},{1... | collective-permute-start | bytes 786440 | tf_op jit(solution)/shard_map/ppermute | solution.py:117
  43.6 10.4 %collective-permute-start.13 = (bf16[512,256]{1,0:T(8,128)(2,1)S(1)}, bf16[512,256]{1,0:T(8,128)(2,1)S(1)}, u32[]{:S(2)}, u32[]{:S(2)}) collective-permute-start(bf16[512,256]{1,0:T(8,128)(2,1)S(1)} %get-tuple-element.49.refs_0_), channel_id=1, source_target_pairs={{0,2},{2,0},{1,3},{3,1},{4,6},{6,4},{5,7},{7,5},{8,10},{10,8},{9,1... | collective-permute-start | bytes 786440 | tf_op jit(solution)/shard_map/ppermute | solution.py:117
  43.9 10.1 %collective-permute-start.14 = (bf16[512,256]{1,0:T(8,128)(2,1)S(1)}, bf16[512,256]{1,0:T(8,128)(2,1)S(1)}, u32[]{:S(2)}, u32[]{:S(2)}) collective-permute-start(bf16[512,256]{1,0:T(8,128)(2,1)S(1)} %get-tuple-element.49.refs_0_), channel_id=1, source_target_pairs={{0,6},{2,4},{4,2},{6,0},{8,14},{10,12},{12,10},{14,8},{1,7},{3,5},... | collective-permute-start | bytes 786440 | tf_op jit(solution)/shard_map/ppermute | solution.py:117
  54.1 2.7 %collective-permute-start.15 = (bf16[4,512,256]{2,1,0:T(8,128)(2,1)S(1)}, bf16[4,512,256]{2,1,0:T(8,128)(2,1)S(1)}, u32[]{:S(2)}, u32[]{:S(2)}) collective-permute-start(bf16[4,512,256]{2,1,0:T(8,128)(2,1)S(1)} %pad_maximum_fusion.1), channel_id=1, source_target_pairs={{0,1},{1,0},{2,3},{3,2},{4,5},{5,4},{6,7},{7,6},{8,9},{9,8},{10,11... | collective-permute-start | bytes 3145736 | tf_op jit(solution)/shard_map/ppermute | solution.py:117
  54.2 9.8 %collective-permute-start.10 = (bf16[512,256]{1,0:T(8,128)(2,1)S(1)}, bf16[512,256]{1,0:T(8,128)(2,1)S(1)}, u32[]{:S(2)}, u32[]{:S(2)}) collective-permute-start(bf16[512,256]{1,0:T(8,128)(2,1)S(1)} %get-tuple-element.45), channel_id=1, source_target_pairs={{0,4},{4,0},{8,12},{12,8},{1,5},{5,1},{9,13},{13,9},{2,6},{6,2},{1... | collective-permute-start | bytes 786440 | tf_op jit(solution)/shard_map/ppermute | solution.py:117
  55.9 8.4 %collective-permute-start.11 = (bf16[512,256]{1,0:T(8,128)(2,1)S(1)}, bf16[512,256]{1,0:T(8,128)(2,1)S(1)}, u32[]{:S(2)}, u32[]{:S(2)}) collective-permute-start(bf16[512,256]{1,0:T(8,128)(2,1)S(1)} %get-tuple-element.45), channel_id=1, source_target_pairs={{0,2},{2,0},{1,3},{3,1},{4,6},{6,4},{5,7},{7,5},{8,10},{10,8},{9,1... | collective-permute-start | bytes 786440 | tf_op jit(solution)/shard_map/ppermute | solution.py:117
  59.3 26.7 %collective-permute-start.16 = (bf16[256,512]{1,0:T(8,128)(2,1)S(1)}, bf16[256,512]{1,0:T(8,128)(2,1)}, u32[]{:S(2)}, u32[]{:S(2)}) collective-permute-start(bf16[256,512]{1,0:T(8,128)(2,1)S(1)} %get-tuple-element.50), channel_id=1, source_target_pairs={{0,8},{4,12},{8,0},{12,4},{1,9},{5,13},{9,1},{13,5},{2,10},{6,14},... | collective-permute-start | bytes 786440 | tf_op jit(solution)/shard_map/ppermute | solution.py:122
  61.1 24.8 %collective-permute-start.17 = (bf16[256,512]{1,0:T(8,128)(2,1)S(1)}, bf16[256,512]{1,0:T(8,128)(2,1)}, u32[]{:S(2)}, u32[]{:S(2)}) collective-permute-start(bf16[256,512]{1,0:T(8,128)(2,1)S(1)} %get-tuple-element.52), channel_id=1, source_target_pairs={{0,12},{4,8},{8,4},{12,0},{1,13},{5,9},{9,5},{13,1},{2,14},{6,10},... | collective-permute-start | bytes 786440 | tf_op jit(solution)/shard_map/ppermute | solution.py:122
  64.3 7.5 %collective-permute-start = (bf16[512,256]{1,0:T(8,128)(2,1)S(1)}, bf16[512,256]{1,0:T(8,128)(2,1)S(1)}, u32[]{:S(2)}, u32[]{:S(2)}) collective-permute-start(bf16[512,256]{1,0:T(8,128)(2,1)S(1)} %get-tuple-element.20.refs_1_), channel_id=1, source_target_pairs={{0,2},{2,0},{1,3},{3,1},{4,6},{6,4},{5,7},{7,5},{8,10},{10,8},{9,1... | collective-permute-start | bytes 786440 | tf_op jit(solution)/shard_map/cond/branch_1_fun/ppermute | solution.py:117
  72.0 2.7 %collective-permute-start.1 = (bf16[4,512,256]{2,1,0:T(8,128)(2,1)S(1)}, bf16[4,512,256]{2,1,0:T(8,128)(2,1)S(1)}, u32[]{:S(2)}, u32[]{:S(2)}) collective-permute-start(bf16[4,512,256]{2,1,0:T(8,128)(2,1)S(1)} %pad_maximum_fusion), channel_id=1, source_target_pairs={{0,1},{1,0},{2,3},{3,2},{4,5},{5,4},{6,7},{7,6},{8,9},{9,8},{10,11... | collective-permute-start | bytes 3145736 | tf_op jit(solution)/shard_map/cond/branch_1_fun/ppermute | solution.py:117
  77.1 8.8 %collective-permute-start.2 = (bf16[256,512]{1,0:T(8,128)(2,1)S(1)}, bf16[256,512]{1,0:T(8,128)(2,1)S(1)}, u32[]{:S(2)}, u32[]{:S(2)}) collective-permute-start(bf16[256,512]{1,0:T(8,128)(2,1)S(1)} %get-tuple-element.26), channel_id=1, source_target_pairs={{0,4},{4,0},{8,12},{12,8},{1,5},{5,1},{9,13},{13,9},{2,6},{6,2},{1... | collective-permute-start | bytes 786440 | tf_op jit(solution)/shard_map/cond/branch_1_fun/ppermute | solution.py:122

commit v7 on v6

--- a/solution.py
+++ b/solution.py
@@ -1,3 +1,4 @@
+import functools
 import math
 
 import jax
@@ -243,8 +244,11 @@
     )(place, *mine, other, out_weight, near_w, far_w)
 
 
-def project_whole_kernel(*refs):
-    mine, other, own_w, near_w, far_w, outs = refs[:4], *refs[4:8], refs[8:10]
+def project_whole_kernel(slots, *refs):
+    outs, refs = refs[-len(slots) :], refs[: -len(slots)]
+    mine, others, (own_w, near_w, far_w) = refs[:4], refs[4:-3], refs[-3:]
+    if len(others) == 1:
+        others = [others[0].at[flip] for flip in range(4)]
     _, x, _, bit = where_am_i()
     group, same = lax.axis_index("group"), lax.axis_index("sub") == bit
     tokens, width = mine[0].shape
@@ -257,7 +261,7 @@
             place = span(2 * bit + index, columns)
             own_part = jnp.concatenate([own_w[block, place] for block in blocks], axis=0)
             got_part = jnp.concatenate([got_w[block, :] for block in blocks], axis=0)
-            for slot in range(2):
+            for slot, out_ref in zip(slots, outs):
                 rows = span(slot ^ bit, half)
                 total = jnp.dot(
                     jnp.concatenate([ref[rows, :] for ref in first], axis=1),
@@ -269,9 +273,7 @@
                     got_part,
                     preferred_element_type=jnp.float32,
                 )
-                outs[slot][:, span(index, columns)] = total.astype(outs[slot].dtype)
-
-    others = [other.at[flip] for flip in range(4)]
+                out_ref[:, span(index, columns)] = total.astype(out_ref.dtype)
 
     @pl.when(same)
     def _():
@@ -345,20 +347,27 @@
     def gathered(gated):
         return [gated, swap(gated, "ctx"), swap(gated, "chan"), swap(gated, "ctx", "chan")]
 
+    def project(mine, other, slots=(0, 1)):
+        return local_call(
+            functools.partial(project_whole_kernel, slots), [(block, half)] * len(slots),
+            *mine, *other, out_weight, w_near, w_far,
+            flops=2 * block * channels * half * len(slots),
+        )
+
     def partials(mine):
         other = swap(jnp.stack(mine), "sub")
-        return local_call(
-            project_whole_kernel, [(block, half)] * 2, *mine, other, out_weight, w_near, w_far,
-            flops=8 * block * channels * half // 2,
-        )
+        return project(mine, [other])
 
     far = partials(gathered(gated_far))
     far_own, far_near = across(far[0], 2), across(far[1], 3)
 
     def close_partials(mine):
         gated, beside, cross = mine
-        close = partials([gated, beside, cross, swap(beside, "chan")])
-        return close[0], across(close[1], 1)
+        crossed = swap(beside, "chan")
+        mine = [*mine, crossed]
+        other = swap(jnp.stack(mine), "sub")
+        near = across(project(mine, [other], (1,))[0], 1)
+        return project(mine, [other], (0,))[0], near
 
     def no_taps(mine):
         zeros = jnp.zeros((block, half), jnp.bfloat16)

time: 88.4 us -> 88.2 us (level)
  waiting for transfers between devices: 47.3 us -> 45.7 us
  Pallas kernels: 6.48 us -> 7.86 us
    ppermute x7, waiting for transfers between devices: 17.7 us -> 16.1 us  [across(): return lax.ppermute(value, 'ctx', [(i, i ^ distance) for i in range(count)])]
    pallas_call x2 -> x3, Pallas kernels: 4.89 us -> 6.28 us  [local_call(): pl.pallas_call(kernel, out_shape=[jax.ShapeDtypeStruct(shape, jnp.bfloat1...]
  transfers between devices with their start and end apart: 18 -> 18, of which waited for: 12 -> 12; matrix products, arithmetic and copies ran while one was open for 7% -> 7% of each run, Pallas kernels for 6% -> 7%
where the time goes in v7:
time: 88.2 us; the launch traced here: 87.8 us
  waiting for transfers between devices  45.7 us (52%)
  starting transfers between devices  22.5 us (26%)
  Pallas kernels  7.86 us (9%)
  other arithmetic  6.31 us (7%)
  local copies, waits for them, and re-layouts  4.5 us (5%)
    ppermute x11, waiting for transfers between devices, swap(): return lax.ppermute(value, axes, [(i, i ^ flip) for i in range(total)])  29.6 us
    ppermute x7, waiting for transfers between devices, across(): return lax.ppermute(value, 'ctx', [(i, i ^ distance) for i in range(count)])  16.1 us
    ppermute x7, starting transfers between devices, across(): return lax.ppermute(value, 'ctx', [(i, i ^ distance) for i in range(count)])  11.4 us
    ppermute x11, starting transfers between devices, swap(): return lax.ppermute(value, axes, [(i, i ^ flip) for i in range(total)])  11.1 us
    pallas_call x3, Pallas kernels, local_call(): pl.pallas_call(kernel, out_shape=[jax.ShapeDtypeStruct(shape, jnp.bfloat1...  6.28 us
  transfers between devices with their start and end apart: 18, of which 12 were waited for; matrix products, arithmetic and copies ran while one was open for 7% of the time, Pallas kernels for 7%

profile of v7, /device:TPU:0, one launch (start us, length us, event | category | flops | bytes accessed | tf_op | source)
XLA Modules:
  0.0 87.8 jit_solution(3391713744020028294)
XLA Ops:
  2.1 3.0 %collective-permute-start.6 = (bf16[2,256,256]{2,1,0:T(8,128)(2,1)S(1)}, bf16[2,256,256]{2,1,0:T(8,128)(2,1)S(1)}, u32[]{:S(2)}, u32[]{:S(2)}) collective-permute-start(bf16[2,256,256]{2,1,0:T(8,128)(2,1)S(1)} %pad_maximum_fusion.3), channel_id=1, source_target_pairs={{0,2},{2,0},{1,3},{3,1},{4,6},{6,4},{5,7},{7,5},{8,10},{10,8},{9,1... | collective-permute-start | bytes 786440 | tf_op jit(solution)/shard_map/ppermute | solution.py:118
  6.2 1.6 %collective-permute-start.4 = (bf16[1024,256]{1,0:T(8,128)(2,1)S(1)}, bf16[1024,256]{1,0:T(8,128)(2,1)}, u32[]{:S(2)}, u32[]{:S(2)}) collective-permute-start(bf16[1024,256]{1,0:T(8,128)(2,1)S(1)} %constant_dynamic-slice_fusion), channel_id=1, source_target_pairs={{0,4},{4,0},{8,12},{12,8},{1,5},{5,1},{9,13},{13,9},{2,6},{6,2},{1... | collective-permute-start | bytes 1572872 | tf_op jit(solution)/shard_map/ppermute | solution.py:123
  10.0 1.8 %collective-permute-done.6 = bf16[2,256,256]{2,1,0:T(8,128)(2,1)S(1)} collective-permute-done((bf16[2,256,256]{2,1,0:T(8,128)(2,1)S(1)}, bf16[2,256,256]{2,1,0:T(8,128)(2,1)S(1)}, u32[]{:S(2)}, u32[]{:S(2)}) %collective-permute-start.6) | collective-permute-done | bytes 262176 | tf_op jit(solution)/shard_map/ppermute | solution.py:118
  12.6 2.9 %collective-permute-start.8 = (bf16[2,256,256]{2,1,0:T(8,128)(2,1)}, bf16[2,256,256]{2,1,0:T(8,128)(2,1)S(1)}, u32[]{:S(2)}, u32[]{:S(2)}) collective-permute-start(bf16[2,256,256]{2,1,0:T(8,128)(2,1)} %get-tuple-element.58), channel_id=1, source_target_pairs={{0,8},{4,12},{8,0},{12,4},{1,9},{5,13},{9,1},{13,5},{2,10},{6,14},... | collective-permute-start | bytes 786440 | tf_op jit(solution)/shard_map/ppermute | solution.py:123
  15.5 1.9 %collective-permute-done.3 = bf16[528,256]{1,0:T(8,128)(2,1)} collective-permute-done((bf16[528,256]{1,0:T(8,128)(2,1)S(1)}, bf16[528,256]{1,0:T(8,128)(2,1)}, u32[]{:S(2)}, u32[]{:S(2)}) %collective-permute-start.3) | collective-permute-done | bytes 270368 | tf_op jit(solution)/shard_map/ppermute | solution.py:118
  18.3 7.1 %collective-permute-done.4.refs_6_ = bf16[1024,256]{1,0:T(8,128)(2,1)} collective-permute-done((bf16[1024,256]{1,0:T(8,128)(2,1)S(1)}, bf16[1024,256]{1,0:T(8,128)(2,1)}, u32[]{:S(2)}, u32[]{:S(2)}) %collective-permute-start.4) | collective-permute-done | bytes 524320 | tf_op jit(solution)/shard_map/ppermute | solution.py:123
  25.4 1.5 %collective-permute-start.5 = (bf16[1024,256]{1,0:T(8,128)(2,1)}, bf16[1024,256]{1,0:T(8,128)(2,1)}, u32[]{:S(2)}, u32[]{:S(2)}) collective-permute-start(bf16[1024,256]{1,0:T(8,128)(2,1)} %collective-permute-done.4.refs_6_), channel_id=1, source_target_pairs={{0,16},{16,0},{1,17},{17,1},{2,18},{18,2},{3,19},{19,3},{4,20},{20... | collective-permute-start | bytes 1572872 | tf_op jit(solution)/shard_map/ppermute | solution.py:118
  27.8 2.2 %collective-permute-start.9 = (bf16[2,256,256]{2,1,0:T(8,128)(2,1)}, bf16[2,256,256]{2,1,0:T(8,128)(2,1)S(1)}, u32[]{:S(2)}, u32[]{:S(2)}) collective-permute-start(bf16[2,256,256]{2,1,0:T(8,128)(2,1)} %get-tuple-element.56), channel_id=1, source_target_pairs={{0,12},{4,8},{8,4},{12,0},{1,13},{5,9},{9,5},{13,1},{2,14},{6,10},... | collective-permute-start | bytes 786440 | tf_op jit(solution)/shard_map/ppermute | solution.py:123
  31.2 7.0 %collective-permute-done.5.refs_7_ = bf16[1024,256]{1,0:T(8,128)(2,1)} collective-permute-done((bf16[1024,256]{1,0:T(8,128)(2,1)}, bf16[1024,256]{1,0:T(8,128)(2,1)}, u32[]{:S(2)}, u32[]{:S(2)}) %collective-permute-start.5) | collective-permute-done | bytes 524320 | tf_op jit(solution)/shard_map/ppermute | solution.py:118
  38.2 2.6 %collective-permute-done.9.refs_3_ = bf16[2,256,256]{2,1,0:T(8,128)(2,1)S(1)} collective-permute-done((bf16[2,256,256]{2,1,0:T(8,128)(2,1)}, bf16[2,256,256]{2,1,0:T(8,128)(2,1)S(1)}, u32[]{:S(2)}, u32[]{:S(2)}) %collective-permute-start.9) | collective-permute-done | bytes 262176 | tf_op jit(solution)/shard_map/ppermute | solution.py:123
  40.8 1.6 %shard_map.64 = (bf16[512,256]{1,0:T(8,128)(2,1)S(1)}, bf16[512,256]{1,0:T(8,128)(2,1)S(1)}) custom-call(s32[6]{0:T(128)S(1)} %stack.97.place, f32[2,768]{1,0:T(2,128)S(1)} %maximum_maximum_fusion.1.row_ref, bf16[2,256,256]{2,1,0:T(8,128)(2,1)S(1)} %get-tuple-element.59.refs_0_, bf16[2,256,256]{2,1,0:T(8,128)(2,1)S(1)} %collective-permute-done.7.refs_1_, ...), custom_call_target="tpu_custom_call" | custom-call | flops 402653184 | bytes 2097152 | tf_op jit(solution)/shard_map/pallas_call | solution.py:180
  43.9 2.0 %collective-permute-start.14 = (bf16[512,256]{1,0:T(8,128)(2,1)S(1)}, bf16[512,256]{1,0:T(8,128)(2,1)S(1)}, u32[]{:S(2)}, u32[]{:S(2)}) collective-permute-start(bf16[512,256]{1,0:T(8,128)(2,1)S(1)} %get-tuple-element.47.refs_0_), channel_id=1, source_target_pairs={{0,6},{2,4},{4,2},{6,0},{8,14},{10,12},{12,10},{14,8},{1,7},{3,5},... | collective-permute-start | bytes 786440 | tf_op jit(solution)/shard_map/ppermute | solution.py:118
  45.9 5.1 %collective-permute-done.12.refs_1_ = bf16[512,256]{1,0:T(8,128)(2,1)S(1)} collective-permute-done((bf16[512,256]{1,0:T(8,128)(2,1)S(1)}, bf16[512,256]{1,0:T(8,128)(2,1)S(1)}, u32[]{:S(2)}, u32[]{:S(2)}) %collective-permute-start.12) | collective-permute-done | bytes 262176 | tf_op jit(solution)/shard_map/ppermute | solution.py:118
  51.1 2.9 %collective-permute-done.13.refs_2_ = bf16[512,256]{1,0:T(8,128)(2,1)S(1)} collective-permute-done((bf16[512,256]{1,0:T(8,128)(2,1)S(1)}, bf16[512,256]{1,0:T(8,128)(2,1)S(1)}, u32[]{:S(2)}, u32[]{:S(2)}) %collective-permute-start.13) | collective-permute-done | bytes 262176 | tf_op jit(solution)/shard_map/ppermute | solution.py:118
  54.2 1.7 %collective-permute-start.10 = (bf16[512,256]{1,0:T(8,128)(2,1)S(1)}, bf16[512,256]{1,0:T(8,128)(2,1)S(1)}, u32[]{:S(2)}, u32[]{:S(2)}) collective-permute-start(bf16[512,256]{1,0:T(8,128)(2,1)S(1)} %get-tuple-element.43), channel_id=1, source_target_pairs={{0,4},{4,0},{8,12},{12,8},{1,5},{5,1},{9,13},{13,9},{2,6},{6,2},{1... | collective-permute-start | bytes 786440 | tf_op jit(solution)/shard_map/ppermute | solution.py:118
  56.8 2.4 %shard_map.65 = (bf16[256,512]{1,0:T(8,128)(2,1)S(1)}, bf16[256,512]{1,0:T(8,128)(2,1)S(1)}) custom-call(bf16[512,256]{1,0:T(8,128)(2,1)S(1)} %get-tuple-element.47.refs_0_, bf16[512,256]{1,0:T(8,128)(2,1)S(1)} %collective-permute-done.12.refs_1_, bf16[512,256]{1,0:T(8,128)(2,1)S(1)} %collective-permute-done.13.refs_2_, ...), custom_call_target="tpu_custom_call" | custom-call | flops 536870912 | bytes 5242880 | tf_op jit(solution)/shard_map/pallas_call | solution.py:131
  59.3 1.9 %collective-permute-start.16 = (bf16[256,512]{1,0:T(8,128)(2,1)S(1)}, bf16[256,512]{1,0:T(8,128)(2,1)}, u32[]{:S(2)}, u32[]{:S(2)}) collective-permute-start(bf16[256,512]{1,0:T(8,128)(2,1)S(1)} %get-tuple-element.48), channel_id=1, source_target_pairs={{0,8},{4,12},{8,0},{12,4},{1,9},{5,13},{9,1},{13,5},{2,10},{6,14},... | collective-permute-start | bytes 786440 | tf_op jit(solution)/shard_map/ppermute | solution.py:123
  61.1 2.2 %collective-permute-start.17 = (bf16[256,512]{1,0:T(8,128)(2,1)S(1)}, bf16[256,512]{1,0:T(8,128)(2,1)}, u32[]{:S(2)}, u32[]{:S(2)}) collective-permute-start(bf16[256,512]{1,0:T(8,128)(2,1)S(1)} %get-tuple-element.50), channel_id=1, source_target_pairs={{0,12},{4,8},{8,4},{12,0},{1,13},{5,9},{9,5},{13,1},{2,14},{6,10},... | collective-permute-start | bytes 786440 | tf_op jit(solution)/shard_map/ppermute | solution.py:123
  64.3 21.5 %conditional.1 = (f32[256,512]{1,0:T(8,128)S(1)}, f32[256,512]{1,0:T(8,128)S(1)}) conditional(s32[]{:T(128)} %convert_element_type.64, () %tuple.19, (bf16[512,256]{1,0:T(8,128)(2,1)S(1)}, bf16[512,256]{1,0:T(8,128)(2,1)S(1)}, bf16[512,256]{1,0:T(8,128)(2,1)S(1)}, bf16[1024,1024]{1,0:T(8,128)(2,1)S(1)}, bf16[1024,256]{1,0:T(8,128)(2,1)}, ...), branch_computations={%region_1.2_spmd, %region_2.3_spmd} | conditional | flops 538705920 | bytes 20447368 | solution.py:376
  64.6 7.4 %collective-permute-done.refs_3_ = bf16[512,256]{1,0:T(8,128)(2,1)S(1)} collective-permute-done((bf16[512,256]{1,0:T(8,128)(2,1)S(1)}, bf16[512,256]{1,0:T(8,128)(2,1)S(1)}, u32[]{:S(2)}, u32[]{:S(2)}) %collective-permute-start) | collective-permute-done | bytes 262176 | tf_op jit(solution)/shard_map/cond/branch_1_fun/ppermute | solution.py:118
  72.2 2.6 %collective-permute-done.1.refs_4_ = bf16[4,512,256]{2,1,0:T(8,128)(2,1)S(1)} collective-permute-done((bf16[4,512,256]{2,1,0:T(8,128)(2,1)S(1)}, bf16[4,512,256]{2,1,0:T(8,128)(2,1)S(1)}, u32[]{:S(2)}, u32[]{:S(2)}) %collective-permute-start.1) | collective-permute-done | bytes 1048608 | tf_op jit(solution)/shard_map/cond/branch_1_fun/ppermute | solution.py:118
  74.8 1.9 %branch_1_fun.3 = bf16[256,512]{1,0:T(8,128)(2,1)S(1)} custom-call(bf16[512,256]{1,0:T(8,128)(2,1)S(1)} %get-tuple-element.19.refs_0_, bf16[512,256]{1,0:T(8,128)(2,1)S(1)} %get-tuple-element.20.refs_1_, bf16[512,256]{1,0:T(8,128)(2,1)S(1)} %get-tuple-element.21.refs_2_, bf16[512,256]{1,0:T(8,128)(2,1)S(1)} %collective-permute-done.refs_3_, ...), custom_call_target="tpu_custom_call" | custom-call | flops 268435456 | bytes 5242880 | tf_op jit(solution)/shard_map/cond/branch_1_fun/pallas_call | solution.py:131
  77.3 1.9 %branch_1_fun.2 = bf16[256,512]{1,0:T(8,128)(2,1)S(1)} custom-call(bf16[512,256]{1,0:T(8,128)(2,1)S(1)} %get-tuple-element.19.refs_0_, bf16[512,256]{1,0:T(8,128)(2,1)S(1)} %get-tuple-element.20.refs_1_, bf16[512,256]{1,0:T(8,128)(2,1)S(1)} %get-tuple-element.21.refs_2_, bf16[512,256]{1,0:T(8,128)(2,1)S(1)} %collective-permute-done.refs_3_, ...), custom_call_target="tpu_custom_call" | custom-call | flops 268435456 | bytes 5242880 | tf_op jit(solution)/shard_map/cond/branch_1_fun/pallas_call | solution.py:131
  79.3 6.4 %collective-permute-done.2 = bf16[256,512]{1,0:T(8,128)(2,1)S(1)} collective-permute-done((bf16[256,512]{1,0:T(8,128)(2,1)S(1)}, bf16[256,512]{1,0:T(8,128)(2,1)S(1)}, u32[]{:S(2)}, u32[]{:S(2)}) %collective-permute-start.2) | collective-permute-done | bytes 262176 | tf_op jit(solution)/shard_map/cond/branch_1_fun/ppermute | solution.py:123
  (61 shorter events, 15.1 us)
Async XLA Ops:
  0.0 8.6 %copy-start.3 = (bf16[256,1024]{1,0:T(8,128)(2,1)S(1)}, bf16[256,1024]{1,0:T(8,128)(2,1)}, u32[]{:S(2)}) copy-start(bf16[256,1024]{1,0:T(8,128)(2,1)} %param.8) | copy-start | bytes 1572868
  0.0 8.6 %copy-start.1 = (bf16[256,1024]{1,0:T(8,128)(2,1)S(1)}, bf16[256,1024]{1,0:T(8,128)(2,1)}, u32[]{:S(2)}) copy-start(bf16[256,1024]{1,0:T(8,128)(2,1)} %param.10) | copy-start | bytes 1572868
  0.0 8.6 %copy-start.2 = (bf16[256,1024]{1,0:T(8,128)(2,1)S(1)}, bf16[256,1024]{1,0:T(8,128)(2,1)}, u32[]{:S(2)}) copy-start(bf16[256,1024]{1,0:T(8,128)(2,1)} %param.9) | copy-start | bytes 1572868
  0.0 7.9 %copy-start.5 = (s32[8]{0:T(128)S(1)}, s32[8]{0:T(128)}, u32[]{:S(2)}) copy-start(s32[8]{0:T(128)} %param.12) | copy-start | bytes 100
  2.1 6.8 %copy-start.4 = (f32[8,512]{1,0:T(8,128)S(1)}, f32[8,512]{1,0:T(8,128)}, u32[]{:S(2)}) copy-start(f32[8,512]{1,0:T(8,128)} %param.11) | copy-start | bytes 49156
  2.1 9.7 %collective-permute-start.6 = (bf16[2,256,256]{2,1,0:T(8,128)(2,1)S(1)}, bf16[2,256,256]{2,1,0:T(8,128)(2,1)S(1)}, u32[]{:S(2)}, u32[]{:S(2)}) collective-permute-start(bf16[2,256,256]{2,1,0:T(8,128)(2,1)S(1)} %pad_maximum_fusion.3), channel_id=1, source_target_pairs={{0,2},{2,0},{1,3},{3,1},{4,6},{6,4},{5,7},{7,5},{8,10},{10,8},{9,1... | collective-permute-start | bytes 786440 | tf_op jit(solution)/shard_map/ppermute | solution.py:118
  6.2 19.2 %collective-permute-start.4 = (bf16[1024,256]{1,0:T(8,128)(2,1)S(1)}, bf16[1024,256]{1,0:T(8,128)(2,1)}, u32[]{:S(2)}, u32[]{:S(2)}) collective-permute-start(bf16[1024,256]{1,0:T(8,128)(2,1)S(1)} %constant_dynamic-slice_fusion), channel_id=1, source_target_pairs={{0,4},{4,0},{8,12},{12,8},{1,5},{5,1},{9,13},{13,9},{2,6},{6,2},{1... | collective-permute-start | bytes 1572872 | tf_op jit(solution)/shard_map/ppermute | solution.py:123
  9.2 8.1 %collective-permute-start.3 = (bf16[528,256]{1,0:T(8,128)(2,1)S(1)}, bf16[528,256]{1,0:T(8,128)(2,1)}, u32[]{:S(2)}, u32[]{:S(2)}) collective-permute-start(bf16[528,256]{1,0:T(8,128)(2,1)S(1)} %maximum_maximum_fusion), channel_id=1, source_target_pairs={{0,2},{2,0},{1,3},{3,1},{4,6},{6,4},{5,7},{7,5},{8,10},{10,8},{9,1... | collective-permute-start | bytes 811016 | tf_op jit(solution)/shard_map/ppermute | solution.py:118
  12.6 25.6 %collective-permute-start.8 = (bf16[2,256,256]{2,1,0:T(8,128)(2,1)}, bf16[2,256,256]{2,1,0:T(8,128)(2,1)S(1)}, u32[]{:S(2)}, u32[]{:S(2)}) collective-permute-start(bf16[2,256,256]{2,1,0:T(8,128)(2,1)} %get-tuple-element.58), channel_id=1, source_target_pairs={{0,8},{4,12},{8,0},{12,4},{1,9},{5,13},{9,1},{13,5},{2,10},{6,14},... | collective-permute-start | bytes 786440 | tf_op jit(solution)/shard_map/ppermute | solution.py:123
  25.4 12.8 %collective-permute-start.5 = (bf16[1024,256]{1,0:T(8,128)(2,1)}, bf16[1024,256]{1,0:T(8,128)(2,1)}, u32[]{:S(2)}, u32[]{:S(2)}) collective-permute-start(bf16[1024,256]{1,0:T(8,128)(2,1)} %collective-permute-done.4.refs_6_), channel_id=1, source_target_pairs={{0,16},{16,0},{1,17},{17,1},{2,18},{18,2},{3,19},{19,3},{4,20},{20... | collective-permute-start | bytes 1572872 | tf_op jit(solution)/shard_map/ppermute | solution.py:118
  26.9 29.9 %copy-start = (bf16[1024,1024]{1,0:T(8,128)(2,1)S(1)}, bf16[1024,1024]{1,0:T(8,128)(2,1)}, u32[]{:S(2)}) copy-start(bf16[1024,1024]{1,0:T(8,128)(2,1)} %refs_5_.1) | copy-start | bytes 6291460
  27.8 10.4 %collective-permute-start.7 = (bf16[2,256,256]{2,1,0:T(8,128)(2,1)}, bf16[2,256,256]{2,1,0:T(8,128)(2,1)S(1)}, u32[]{:S(2)}, u32[]{:S(2)}) collective-permute-start(bf16[2,256,256]{2,1,0:T(8,128)(2,1)} %get-tuple-element.57), channel_id=1, source_target_pairs={{0,4},{4,0},{8,12},{12,8},{1,5},{5,1},{9,13},{13,9},{2,6},{6,2},{1... | collective-permute-start | bytes 786440 | tf_op jit(solution)/shard_map/ppermute | solution.py:123
  27.8 13.0 %collective-permute-start.9 = (bf16[2,256,256]{2,1,0:T(8,128)(2,1)}, bf16[2,256,256]{2,1,0:T(8,128)(2,1)S(1)}, u32[]{:S(2)}, u32[]{:S(2)}) collective-permute-start(bf16[2,256,256]{2,1,0:T(8,128)(2,1)} %get-tuple-element.56), channel_id=1, source_target_pairs={{0,12},{4,8},{8,4},{12,0},{1,13},{5,9},{9,5},{13,1},{2,14},{6,10},... | collective-permute-start | bytes 786440 | tf_op jit(solution)/shard_map/ppermute | solution.py:123
  42.4 8.7 %collective-permute-start.12 = (bf16[512,256]{1,0:T(8,128)(2,1)S(1)}, bf16[512,256]{1,0:T(8,128)(2,1)S(1)}, u32[]{:S(2)}, u32[]{:S(2)}) collective-permute-start(bf16[512,256]{1,0:T(8,128)(2,1)S(1)} %get-tuple-element.47.refs_0_), channel_id=1, source_target_pairs={{0,4},{4,0},{8,12},{12,8},{1,5},{5,1},{9,13},{13,9},{2,6},{6,2},{1... | collective-permute-start | bytes 786440 | tf_op jit(solution)/shard_map/ppermute | solution.py:118
  43.6 10.4 %collective-permute-start.13 = (bf16[512,256]{1,0:T(8,128)(2,1)S(1)}, bf16[512,256]{1,0:T(8,128)(2,1)S(1)}, u32[]{:S(2)}, u32[]{:S(2)}) collective-permute-start(bf16[512,256]{1,0:T(8,128)(2,1)S(1)} %get-tuple-element.47.refs_0_), channel_id=1, source_target_pairs={{0,2},{2,0},{1,3},{3,1},{4,6},{6,4},{5,7},{7,5},{8,10},{10,8},{9,1... | collective-permute-start | bytes 786440 | tf_op jit(solution)/shard_map/ppermute | solution.py:118
  43.9 10.1 %collective-permute-start.14 = (bf16[512,256]{1,0:T(8,128)(2,1)S(1)}, bf16[512,256]{1,0:T(8,128)(2,1)S(1)}, u32[]{:S(2)}, u32[]{:S(2)}) collective-permute-start(bf16[512,256]{1,0:T(8,128)(2,1)S(1)} %get-tuple-element.47.refs_0_), channel_id=1, source_target_pairs={{0,6},{2,4},{4,2},{6,0},{8,14},{10,12},{12,10},{14,8},{1,7},{3,5},... | collective-permute-start | bytes 786440 | tf_op jit(solution)/shard_map/ppermute | solution.py:118
  54.1 2.7 %collective-permute-start.15 = (bf16[4,512,256]{2,1,0:T(8,128)(2,1)S(1)}, bf16[4,512,256]{2,1,0:T(8,128)(2,1)S(1)}, u32[]{:S(2)}, u32[]{:S(2)}) collective-permute-start(bf16[4,512,256]{2,1,0:T(8,128)(2,1)S(1)} %pad_maximum_fusion.1), channel_id=1, source_target_pairs={{0,1},{1,0},{2,3},{3,2},{4,5},{5,4},{6,7},{7,6},{8,9},{9,8},{10,11... | collective-permute-start | bytes 3145736 | tf_op jit(solution)/shard_map/ppermute | solution.py:118
  54.2 9.9 %collective-permute-start.10 = (bf16[512,256]{1,0:T(8,128)(2,1)S(1)}, bf16[512,256]{1,0:T(8,128)(2,1)S(1)}, u32[]{:S(2)}, u32[]{:S(2)}) collective-permute-start(bf16[512,256]{1,0:T(8,128)(2,1)S(1)} %get-tuple-element.43), channel_id=1, source_target_pairs={{0,4},{4,0},{8,12},{12,8},{1,5},{5,1},{9,13},{13,9},{2,6},{6,2},{1... | collective-permute-start | bytes 786440 | tf_op jit(solution)/shard_map/ppermute | solution.py:118
  55.9 8.4 %collective-permute-start.11 = (bf16[512,256]{1,0:T(8,128)(2,1)S(1)}, bf16[512,256]{1,0:T(8,128)(2,1)S(1)}, u32[]{:S(2)}, u32[]{:S(2)}) collective-permute-start(bf16[512,256]{1,0:T(8,128)(2,1)S(1)} %get-tuple-element.43), channel_id=1, source_target_pairs={{0,2},{2,0},{1,3},{3,1},{4,6},{6,4},{5,7},{7,5},{8,10},{10,8},{9,1... | collective-permute-start | bytes 786440 | tf_op jit(solution)/shard_map/ppermute | solution.py:118
  59.3 26.5 %collective-permute-start.16 = (bf16[256,512]{1,0:T(8,128)(2,1)S(1)}, bf16[256,512]{1,0:T(8,128)(2,1)}, u32[]{:S(2)}, u32[]{:S(2)}) collective-permute-start(bf16[256,512]{1,0:T(8,128)(2,1)S(1)} %get-tuple-element.48), channel_id=1, source_target_pairs={{0,8},{4,12},{8,0},{12,4},{1,9},{5,13},{9,1},{13,5},{2,10},{6,14},... | collective-permute-start | bytes 786440 | tf_op jit(solution)/shard_map/ppermute | solution.py:123
  61.1 24.6 %collective-permute-start.17 = (bf16[256,512]{1,0:T(8,128)(2,1)S(1)}, bf16[256,512]{1,0:T(8,128)(2,1)}, u32[]{:S(2)}, u32[]{:S(2)}) collective-permute-start(bf16[256,512]{1,0:T(8,128)(2,1)S(1)} %get-tuple-element.50), channel_id=1, source_target_pairs={{0,12},{4,8},{8,4},{12,0},{1,13},{5,9},{9,5},{13,1},{2,14},{6,10},... | collective-permute-start | bytes 786440 | tf_op jit(solution)/shard_map/ppermute | solution.py:123
  64.3 7.7 %collective-permute-start = (bf16[512,256]{1,0:T(8,128)(2,1)S(1)}, bf16[512,256]{1,0:T(8,128)(2,1)S(1)}, u32[]{:S(2)}, u32[]{:S(2)}) collective-permute-start(bf16[512,256]{1,0:T(8,128)(2,1)S(1)} %get-tuple-element.20.refs_1_), channel_id=1, source_target_pairs={{0,2},{2,0},{1,3},{3,1},{4,6},{6,4},{5,7},{7,5},{8,10},{10,8},{9,1... | collective-permute-start | bytes 786440 | tf_op jit(solution)/shard_map/cond/branch_1_fun/ppermute | solution.py:118
  72.1 2.7 %collective-permute-start.1 = (bf16[4,512,256]{2,1,0:T(8,128)(2,1)S(1)}, bf16[4,512,256]{2,1,0:T(8,128)(2,1)S(1)}, u32[]{:S(2)}, u32[]{:S(2)}) collective-permute-start(bf16[4,512,256]{2,1,0:T(8,128)(2,1)S(1)} %pad_maximum_fusion), channel_id=1, source_target_pairs={{0,1},{1,0},{2,3},{3,2},{4,5},{5,4},{6,7},{7,6},{8,9},{9,8},{10,11... | collective-permute-start | bytes 3145736 | tf_op jit(solution)/shard_map/cond/branch_1_fun/ppermute | solution.py:118
  76.7 9.0 %collective-permute-start.2 = (bf16[256,512]{1,0:T(8,128)(2,1)S(1)}, bf16[256,512]{1,0:T(8,128)(2,1)S(1)}, u32[]{:S(2)}, u32[]{:S(2)}) collective-permute-start(bf16[256,512]{1,0:T(8,128)(2,1)S(1)} %branch_1_fun.3), channel_id=1, source_target_pairs={{0,4},{4,0},{8,12},{12,8},{1,5},{5,1},{9,13},{13,9},{2,6},{6,2},{1... | collective-permute-start | bytes 786440 | tf_op jit(solution)/shard_map/cond/branch_1_fun/ppermute | solution.py:123

commit v8 on v7

--- a/solution.py
+++ b/solution.py
@@ -312,8 +312,12 @@
         [filter_rows, jnp.zeros((16 - filter_rows.shape[0], fourth), jnp.bfloat16)], axis=0
     )
 
+    other_cols = (1 - bit) * half + g * fourth
+    w_send = lax.dynamic_slice_in_dim(out_weight, other_cols, fourth, 1)
     same_send = packed(2 * (1 - x) + bit)
-    k_proj, v_proj, q_proj, same_send = lax.optimization_barrier((k_proj, v_proj, q_proj, same_send))
+    k_proj, v_proj, q_proj, same_send, w_send = lax.optimization_barrier(
+        (k_proj, v_proj, q_proj, same_send, w_send)
+    )
     flip_send = jnp.concatenate(
         [packed(2 * (1 - x) + 1 - bit).reshape(2 * block, fourth), filter_rows], axis=0
     )
@@ -321,8 +325,7 @@
     flip_came = swap(flip_send, "chan")
     same_own, flip_own = packed(2 * x + bit), packed(2 * x + 1 - bit)
 
-    other_cols = (1 - bit) * half + g * fourth
-    w_near = across(lax.dynamic_slice_in_dim(out_weight, other_cols, fourth, 1), 1)
+    w_near = across(w_send, 1)
     w_far = swap(w_near, "group")
 
     inside = pair == x

time: 88.2 us -> 88 us (level)
    ppermute x11, waiting for transfers between devices: 29.6 us -> 32.4 us  [swap(): return lax.ppermute(value, axes, [(i, i ^ flip) for i in range(total)])]
    ppermute x7, waiting for transfers between devices: 16.1 us -> 13.9 us  [across(): return lax.ppermute(value, 'ctx', [(i, i ^ distance) for i in range(count)])]
  transfers between devices with their start and end apart: 18 -> 18, of which waited for: 12 -> 11; matrix products, arithmetic and copies ran while one was open for 7% -> 6% of each run, Pallas kernels for 7% -> 7%
where the time goes in v8:
time: 88 us; the launch traced here: 87.6 us
  waiting for transfers between devices  46.3 us (53%)
  starting transfers between devices  21.8 us (25%)
  Pallas kernels  7.86 us (9%)
  other arithmetic  6.31 us (7%)
  local copies, waits for them, and re-layouts  4.5 us (5%)
  between operations  0.88 us (1%)
    ppermute x11, waiting for transfers between devices, swap(): return lax.ppermute(value, axes, [(i, i ^ flip) for i in range(total)])  32.4 us
    ppermute x7, waiting for transfers between devices, across(): return lax.ppermute(value, 'ctx', [(i, i ^ distance) for i in range(count)])  13.9 us
    ppermute x11, starting transfers between devices, swap(): return lax.ppermute(value, axes, [(i, i ^ flip) for i in range(total)])  10.9 us
    ppermute x7, starting transfers between devices, across(): return lax.ppermute(value, 'ctx', [(i, i ^ distance) for i in range(count)])  10.8 us
    pallas_call x3, Pallas kernels, local_call(): pl.pallas_call(kernel, out_shape=[jax.ShapeDtypeStruct(shape, jnp.bfloat1...  6.28 us
  transfers between devices with their start and end apart: 18, of which 11 were waited for; matrix products, arithmetic and copies ran while one was open for 6% of the time, Pallas kernels for 7%

profile of v8, /device:TPU:0, one launch (start us, length us, event | category | flops | bytes accessed | tf_op | source)
XLA Modules:
  0.0 87.6 jit_solution(3239109146941636156)
XLA Ops:
  3.2 3.0 %collective-permute-start.6 = (bf16[2,256,256]{2,1,0:T(8,128)(2,1)S(1)}, bf16[2,256,256]{2,1,0:T(8,128)(2,1)S(1)}, u32[]{:S(2)}, u32[]{:S(2)}) collective-permute-start(bf16[2,256,256]{2,1,0:T(8,128)(2,1)S(1)} %pad_maximum_fusion.3), channel_id=1, source_target_pairs={{0,2},{2,0},{1,3},{3,1},{4,6},{6,4},{5,7},{7,5},{8,10},{10,8},{9,1... | collective-permute-start | bytes 786440 | tf_op jit(solution)/shard_map/ppermute | solution.py:118
  6.2 1.6 %collective-permute-start.4 = (bf16[1024,256]{1,0:T(8,128)(2,1)S(1)}, bf16[1024,256]{1,0:T(8,128)(2,1)}, u32[]{:S(2)}, u32[]{:S(2)}) collective-permute-start(bf16[1024,256]{1,0:T(8,128)(2,1)S(1)} %constant_dynamic-slice_fusion.1), channel_id=1, source_target_pairs={{0,4},{4,0},{8,12},{12,8},{1,5},{5,1},{9,13},{13,9},{2,6},{6,2},{1... | collective-permute-start | bytes 1572872 | tf_op jit(solution)/shard_map/ppermute | solution.py:123
  10.0 3.4 %collective-permute-done.6 = bf16[2,256,256]{2,1,0:T(8,128)(2,1)S(1)} collective-permute-done((bf16[2,256,256]{2,1,0:T(8,128)(2,1)S(1)}, bf16[2,256,256]{2,1,0:T(8,128)(2,1)S(1)}, u32[]{:S(2)}, u32[]{:S(2)}) %collective-permute-start.6) | collective-permute-done | bytes 262176 | tf_op jit(solution)/shard_map/ppermute | solution.py:118
  14.1 3.2 %collective-permute-start.8 = (bf16[2,256,256]{2,1,0:T(8,128)(2,1)}, bf16[2,256,256]{2,1,0:T(8,128)(2,1)S(1)}, u32[]{:S(2)}, u32[]{:S(2)}) collective-permute-start(bf16[2,256,256]{2,1,0:T(8,128)(2,1)} %get-tuple-element.60), channel_id=1, source_target_pairs={{0,8},{4,12},{8,0},{12,4},{1,9},{5,13},{9,1},{13,5},{2,10},{6,14},... | collective-permute-start | bytes 786440 | tf_op jit(solution)/shard_map/ppermute | solution.py:123
  19.4 5.6 %collective-permute-done.4.refs_6_ = bf16[1024,256]{1,0:T(8,128)(2,1)} collective-permute-done((bf16[1024,256]{1,0:T(8,128)(2,1)S(1)}, bf16[1024,256]{1,0:T(8,128)(2,1)}, u32[]{:S(2)}, u32[]{:S(2)}) %collective-permute-start.4) | collective-permute-done | bytes 524320 | tf_op jit(solution)/shard_map/ppermute | solution.py:123
  25.1 1.4 %collective-permute-start.5 = (bf16[1024,256]{1,0:T(8,128)(2,1)}, bf16[1024,256]{1,0:T(8,128)(2,1)}, u32[]{:S(2)}, u32[]{:S(2)}) collective-permute-start(bf16[1024,256]{1,0:T(8,128)(2,1)} %collective-permute-done.4.refs_6_), channel_id=1, source_target_pairs={{0,16},{16,0},{1,17},{17,1},{2,18},{18,2},{3,19},{19,3},{4,20},{20... | collective-permute-start | bytes 1572872 | tf_op jit(solution)/shard_map/ppermute | solution.py:118
  27.3 1.5 %collective-permute-start.9 = (bf16[2,256,256]{2,1,0:T(8,128)(2,1)}, bf16[2,256,256]{2,1,0:T(8,128)(2,1)S(1)}, u32[]{:S(2)}, u32[]{:S(2)}) collective-permute-start(bf16[2,256,256]{2,1,0:T(8,128)(2,1)} %get-tuple-element.58), channel_id=1, source_target_pairs={{0,12},{4,8},{8,4},{12,0},{1,13},{5,9},{9,5},{13,1},{2,14},{6,10},... | collective-permute-start | bytes 786440 | tf_op jit(solution)/shard_map/ppermute | solution.py:123
  30.0 7.8 %collective-permute-done.5.refs_7_ = bf16[1024,256]{1,0:T(8,128)(2,1)} collective-permute-done((bf16[1024,256]{1,0:T(8,128)(2,1)}, bf16[1024,256]{1,0:T(8,128)(2,1)}, u32[]{:S(2)}, u32[]{:S(2)}) %collective-permute-start.5) | collective-permute-done | bytes 524320 | tf_op jit(solution)/shard_map/ppermute | solution.py:118
  37.8 1.9 %collective-permute-done.7.refs_1_ = bf16[2,256,256]{2,1,0:T(8,128)(2,1)S(1)} collective-permute-done((bf16[2,256,256]{2,1,0:T(8,128)(2,1)}, bf16[2,256,256]{2,1,0:T(8,128)(2,1)S(1)}, u32[]{:S(2)}, u32[]{:S(2)}) %collective-permute-start.7) | collective-permute-done | bytes 262176 | tf_op jit(solution)/shard_map/ppermute | solution.py:123
  39.7 1.6 %shard_map.64 = (bf16[512,256]{1,0:T(8,128)(2,1)S(1)}, bf16[512,256]{1,0:T(8,128)(2,1)S(1)}) custom-call(s32[6]{0:T(128)S(1)} %stack.97.place, f32[2,768]{1,0:T(2,128)S(1)} %maximum_maximum_fusion.1.row_ref, bf16[2,256,256]{2,1,0:T(8,128)(2,1)S(1)} %get-tuple-element.61.refs_0_, bf16[2,256,256]{2,1,0:T(8,128)(2,1)S(1)} %collective-permute-done.7.refs_1_, ...), custom_call_target="tpu_custom_call" | custom-call | flops 402653184 | bytes 2097152 | tf_op jit(solution)/shard_map/pallas_call | solution.py:180
  41.3 1.8 %collective-permute-start.12 = (bf16[512,256]{1,0:T(8,128)(2,1)S(1)}, bf16[512,256]{1,0:T(8,128)(2,1)S(1)}, u32[]{:S(2)}, u32[]{:S(2)}) collective-permute-start(bf16[512,256]{1,0:T(8,128)(2,1)S(1)} %get-tuple-element.49.refs_0_), channel_id=1, source_target_pairs={{0,4},{4,0},{8,12},{12,8},{1,5},{5,1},{9,13},{13,9},{2,6},{6,2},{1... | collective-permute-start | bytes 786440 | tf_op jit(solution)/shard_map/ppermute | solution.py:118
  43.1 1.7 %collective-permute-start.14 = (bf16[512,256]{1,0:T(8,128)(2,1)S(1)}, bf16[512,256]{1,0:T(8,128)(2,1)S(1)}, u32[]{:S(2)}, u32[]{:S(2)}) collective-permute-start(bf16[512,256]{1,0:T(8,128)(2,1)S(1)} %get-tuple-element.49.refs_0_), channel_id=1, source_target_pairs={{0,6},{2,4},{4,2},{6,0},{8,14},{10,12},{12,10},{14,8},{1,7},{3,5},... | collective-permute-start | bytes 786440 | tf_op jit(solution)/shard_map/ppermute | solution.py:118
  44.9 5.0 %collective-permute-done.12.refs_1_ = bf16[512,256]{1,0:T(8,128)(2,1)S(1)} collective-permute-done((bf16[512,256]{1,0:T(8,128)(2,1)S(1)}, bf16[512,256]{1,0:T(8,128)(2,1)S(1)}, u32[]{:S(2)}, u32[]{:S(2)}) %collective-permute-start.12) | collective-permute-done | bytes 262176 | tf_op jit(solution)/shard_map/ppermute | solution.py:118
  49.9 3.7 %collective-permute-done.13.refs_2_ = bf16[512,256]{1,0:T(8,128)(2,1)S(1)} collective-permute-done((bf16[512,256]{1,0:T(8,128)(2,1)S(1)}, bf16[512,256]{1,0:T(8,128)(2,1)S(1)}, u32[]{:S(2)}, u32[]{:S(2)}) %collective-permute-start.13) | collective-permute-done | bytes 262176 | tf_op jit(solution)/shard_map/ppermute | solution.py:118
  53.9 1.3 %collective-permute-start.10 = (bf16[512,256]{1,0:T(8,128)(2,1)S(1)}, bf16[512,256]{1,0:T(8,128)(2,1)S(1)}, u32[]{:S(2)}, u32[]{:S(2)}) collective-permute-start(bf16[512,256]{1,0:T(8,128)(2,1)S(1)} %get-tuple-element.45), channel_id=1, source_target_pairs={{0,4},{4,0},{8,12},{12,8},{1,5},{5,1},{9,13},{13,9},{2,6},{6,2},{1... | collective-permute-start | bytes 786440 | tf_op jit(solution)/shard_map/ppermute | solution.py:118
  55.2 1.3 %collective-permute-done.15.refs_4_ = bf16[4,512,256]{2,1,0:T(8,128)(2,1)S(1)} collective-permute-done((bf16[4,512,256]{2,1,0:T(8,128)(2,1)S(1)}, bf16[4,512,256]{2,1,0:T(8,128)(2,1)S(1)}, u32[]{:S(2)}, u32[]{:S(2)}) %collective-permute-start.15) | collective-permute-done | bytes 1048608 | tf_op jit(solution)/shard_map/ppermute | solution.py:118
  56.5 2.4 %shard_map.65 = (bf16[256,512]{1,0:T(8,128)(2,1)S(1)}, bf16[256,512]{1,0:T(8,128)(2,1)S(1)}) custom-call(bf16[512,256]{1,0:T(8,128)(2,1)S(1)} %get-tuple-element.49.refs_0_, bf16[512,256]{1,0:T(8,128)(2,1)S(1)} %collective-permute-done.12.refs_1_, bf16[512,256]{1,0:T(8,128)(2,1)S(1)} %collective-permute-done.13.refs_2_, ...), custom_call_target="tpu_custom_call" | custom-call | flops 536870912 | bytes 5242880 | tf_op jit(solution)/shard_map/pallas_call | solution.py:131
  59.0 3.0 %collective-permute-start.16 = (bf16[256,512]{1,0:T(8,128)(2,1)S(1)}, bf16[256,512]{1,0:T(8,128)(2,1)}, u32[]{:S(2)}, u32[]{:S(2)}) collective-permute-start(bf16[256,512]{1,0:T(8,128)(2,1)S(1)} %get-tuple-element.50), channel_id=1, source_target_pairs={{0,8},{4,12},{8,0},{12,4},{1,9},{5,13},{9,1},{13,5},{2,10},{6,14},... | collective-permute-start | bytes 786440 | tf_op jit(solution)/shard_map/ppermute | solution.py:123
  63.7 21.9 %conditional.1 = (f32[256,512]{1,0:T(8,128)S(1)}, f32[256,512]{1,0:T(8,128)S(1)}) conditional(s32[]{:T(128)} %convert_element_type.64, () %tuple.19, (bf16[512,256]{1,0:T(8,128)(2,1)S(1)}, bf16[512,256]{1,0:T(8,128)(2,1)S(1)}, bf16[512,256]{1,0:T(8,128)(2,1)S(1)}, bf16[1024,1024]{1,0:T(8,128)(2,1)S(1)}, bf16[1024,256]{1,0:T(8,128)(2,1)}, ...), branch_computations={%region_1.2_spmd, %region_2.3_spmd} | conditional | flops 538705920 | bytes 20447368 | solution.py:379
  64.5 7.3 %collective-permute-done.refs_3_ = bf16[512,256]{1,0:T(8,128)(2,1)S(1)} collective-permute-done((bf16[512,256]{1,0:T(8,128)(2,1)S(1)}, bf16[512,256]{1,0:T(8,128)(2,1)S(1)}, u32[]{:S(2)}, u32[]{:S(2)}) %collective-permute-start) | collective-permute-done | bytes 262176 | tf_op jit(solution)/shard_map/cond/branch_1_fun/ppermute | solution.py:118
  72.0 2.6 %collective-permute-done.1.refs_4_ = bf16[4,512,256]{2,1,0:T(8,128)(2,1)S(1)} collective-permute-done((bf16[4,512,256]{2,1,0:T(8,128)(2,1)S(1)}, bf16[4,512,256]{2,1,0:T(8,128)(2,1)S(1)}, u32[]{:S(2)}, u32[]{:S(2)}) %collective-permute-start.1) | collective-permute-done | bytes 1048608 | tf_op jit(solution)/shard_map/cond/branch_1_fun/ppermute | solution.py:118
  74.7 1.9 %branch_1_fun.3 = bf16[256,512]{1,0:T(8,128)(2,1)S(1)} custom-call(bf16[512,256]{1,0:T(8,128)(2,1)S(1)} %get-tuple-element.19.refs_0_, bf16[512,256]{1,0:T(8,128)(2,1)S(1)} %get-tuple-element.20.refs_1_, bf16[512,256]{1,0:T(8,128)(2,1)S(1)} %get-tuple-element.21.refs_2_, bf16[512,256]{1,0:T(8,128)(2,1)S(1)} %collective-permute-done.refs_3_, ...), custom_call_target="tpu_custom_call" | custom-call | flops 268435456 | bytes 5242880 | tf_op jit(solution)/shard_map/cond/branch_1_fun/pallas_call | solution.py:131
  77.2 1.9 %branch_1_fun.2 = bf16[256,512]{1,0:T(8,128)(2,1)S(1)} custom-call(bf16[512,256]{1,0:T(8,128)(2,1)S(1)} %get-tuple-element.19.refs_0_, bf16[512,256]{1,0:T(8,128)(2,1)S(1)} %get-tuple-element.20.refs_1_, bf16[512,256]{1,0:T(8,128)(2,1)S(1)} %get-tuple-element.21.refs_2_, bf16[512,256]{1,0:T(8,128)(2,1)S(1)} %collective-permute-done.refs_3_, ...), custom_call_target="tpu_custom_call" | custom-call | flops 268435456 | bytes 5242880 | tf_op jit(solution)/shard_map/cond/branch_1_fun/pallas_call | solution.py:131
  79.2 6.3 %collective-permute-done.2 = bf16[256,512]{1,0:T(8,128)(2,1)S(1)} collective-permute-done((bf16[256,512]{1,0:T(8,128)(2,1)S(1)}, bf16[256,512]{1,0:T(8,128)(2,1)S(1)}, u32[]{:S(2)}, u32[]{:S(2)}) %collective-permute-start.2) | collective-permute-done | bytes 262176 | tf_op jit(solution)/shard_map/cond/branch_1_fun/ppermute | solution.py:123
  (61 shorter events, 15.2 us)
Async XLA Ops:
  0.0 8.5 %copy-start.3 = (bf16[256,1024]{1,0:T(8,128)(2,1)S(1)}, bf16[256,1024]{1,0:T(8,128)(2,1)}, u32[]{:S(2)}) copy-start(bf16[256,1024]{1,0:T(8,128)(2,1)} %param.8) | copy-start | bytes 1572868
  0.0 8.6 %copy-start.1 = (bf16[256,1024]{1,0:T(8,128)(2,1)S(1)}, bf16[256,1024]{1,0:T(8,128)(2,1)}, u32[]{:S(2)}) copy-start(bf16[256,1024]{1,0:T(8,128)(2,1)} %param.10) | copy-start | bytes 1572868
  0.0 8.6 %copy-start.2 = (bf16[256,1024]{1,0:T(8,128)(2,1)S(1)}, bf16[256,1024]{1,0:T(8,128)(2,1)}, u32[]{:S(2)}) copy-start(bf16[256,1024]{1,0:T(8,128)(2,1)} %param.9) | copy-start | bytes 1572868
  0.0 7.8 %copy-start.5 = (s32[8]{0:T(128)S(1)}, s32[8]{0:T(128)}, u32[]{:S(2)}) copy-start(s32[8]{0:T(128)} %param.12) | copy-start | bytes 100
  1.2 7.6 %copy-start.4 = (f32[8,512]{1,0:T(8,128)S(1)}, f32[8,512]{1,0:T(8,128)}, u32[]{:S(2)}) copy-start(f32[8,512]{1,0:T(8,128)} %param.11) | copy-start | bytes 49156
  3.2 10.2 %collective-permute-start.6 = (bf16[2,256,256]{2,1,0:T(8,128)(2,1)S(1)}, bf16[2,256,256]{2,1,0:T(8,128)(2,1)S(1)}, u32[]{:S(2)}, u32[]{:S(2)}) collective-permute-start(bf16[2,256,256]{2,1,0:T(8,128)(2,1)S(1)} %pad_maximum_fusion.3), channel_id=1, source_target_pairs={{0,2},{2,0},{1,3},{3,1},{4,6},{6,4},{5,7},{7,5},{8,10},{10,8},{9,1... | collective-permute-start | bytes 786440 | tf_op jit(solution)/shard_map/ppermute | solution.py:118
  6.2 18.8 %collective-permute-start.4 = (bf16[1024,256]{1,0:T(8,128)(2,1)S(1)}, bf16[1024,256]{1,0:T(8,128)(2,1)}, u32[]{:S(2)}, u32[]{:S(2)}) collective-permute-start(bf16[1024,256]{1,0:T(8,128)(2,1)S(1)} %constant_dynamic-slice_fusion.1), channel_id=1, source_target_pairs={{0,4},{4,0},{8,12},{12,8},{1,5},{5,1},{9,13},{13,9},{2,6},{6,2},{1... | collective-permute-start | bytes 1572872 | tf_op jit(solution)/shard_map/ppermute | solution.py:123
  9.2 9.3 %collective-permute-start.3 = (bf16[528,256]{1,0:T(8,128)(2,1)S(1)}, bf16[528,256]{1,0:T(8,128)(2,1)}, u32[]{:S(2)}, u32[]{:S(2)}) collective-permute-start(bf16[528,256]{1,0:T(8,128)(2,1)S(1)} %maximum_maximum_fusion), channel_id=1, source_target_pairs={{0,2},{2,0},{1,3},{3,1},{4,6},{6,4},{5,7},{7,5},{8,10},{10,8},{9,1... | collective-permute-start | bytes 811016 | tf_op jit(solution)/shard_map/ppermute | solution.py:118
  14.1 23.7 %collective-permute-start.8 = (bf16[2,256,256]{2,1,0:T(8,128)(2,1)}, bf16[2,256,256]{2,1,0:T(8,128)(2,1)S(1)}, u32[]{:S(2)}, u32[]{:S(2)}) collective-permute-start(bf16[2,256,256]{2,1,0:T(8,128)(2,1)} %get-tuple-element.60), channel_id=1, source_target_pairs={{0,8},{4,12},{8,0},{12,4},{1,9},{5,13},{9,1},{13,5},{2,10},{6,14},... | collective-permute-start | bytes 786440 | tf_op jit(solution)/shard_map/ppermute | solution.py:123
  25.1 12.8 %collective-permute-start.5 = (bf16[1024,256]{1,0:T(8,128)(2,1)}, bf16[1024,256]{1,0:T(8,128)(2,1)}, u32[]{:S(2)}, u32[]{:S(2)}) collective-permute-start(bf16[1024,256]{1,0:T(8,128)(2,1)} %collective-permute-done.4.refs_6_), channel_id=1, source_target_pairs={{0,16},{16,0},{1,17},{17,1},{2,18},{18,2},{3,19},{19,3},{4,20},{20... | collective-permute-start | bytes 1572872 | tf_op jit(solution)/shard_map/ppermute | solution.py:118
  26.5 30.1 %copy-start = (bf16[1024,1024]{1,0:T(8,128)(2,1)S(1)}, bf16[1024,1024]{1,0:T(8,128)(2,1)}, u32[]{:S(2)}) copy-start(bf16[1024,1024]{1,0:T(8,128)(2,1)} %refs_5_.1) | copy-start | bytes 6291460
  27.3 12.4 %collective-permute-start.7 = (bf16[2,256,256]{2,1,0:T(8,128)(2,1)}, bf16[2,256,256]{2,1,0:T(8,128)(2,1)S(1)}, u32[]{:S(2)}, u32[]{:S(2)}) collective-permute-start(bf16[2,256,256]{2,1,0:T(8,128)(2,1)} %get-tuple-element.59), channel_id=1, source_target_pairs={{0,4},{4,0},{8,12},{12,8},{1,5},{5,1},{9,13},{13,9},{2,6},{6,2},{1... | collective-permute-start | bytes 786440 | tf_op jit(solution)/shard_map/ppermute | solution.py:123
  27.3 12.4 %collective-permute-start.9 = (bf16[2,256,256]{2,1,0:T(8,128)(2,1)}, bf16[2,256,256]{2,1,0:T(8,128)(2,1)S(1)}, u32[]{:S(2)}, u32[]{:S(2)}) collective-permute-start(bf16[2,256,256]{2,1,0:T(8,128)(2,1)} %get-tuple-element.58), channel_id=1, source_target_pairs={{0,12},{4,8},{8,4},{12,0},{1,13},{5,9},{9,5},{13,1},{2,14},{6,10},... | collective-permute-start | bytes 786440 | tf_op jit(solution)/shard_map/ppermute | solution.py:123
  41.3 8.6 %collective-permute-start.12 = (bf16[512,256]{1,0:T(8,128)(2,1)S(1)}, bf16[512,256]{1,0:T(8,128)(2,1)S(1)}, u32[]{:S(2)}, u32[]{:S(2)}) collective-permute-start(bf16[512,256]{1,0:T(8,128)(2,1)S(1)} %get-tuple-element.49.refs_0_), channel_id=1, source_target_pairs={{0,4},{4,0},{8,12},{12,8},{1,5},{5,1},{9,13},{13,9},{2,6},{6,2},{1... | collective-permute-start | bytes 786440 | tf_op jit(solution)/shard_map/ppermute | solution.py:118
  43.1 10.5 %collective-permute-start.13 = (bf16[512,256]{1,0:T(8,128)(2,1)S(1)}, bf16[512,256]{1,0:T(8,128)(2,1)S(1)}, u32[]{:S(2)}, u32[]{:S(2)}) collective-permute-start(bf16[512,256]{1,0:T(8,128)(2,1)S(1)} %get-tuple-element.49.refs_0_), channel_id=1, source_target_pairs={{0,2},{2,0},{1,3},{3,1},{4,6},{6,4},{5,7},{7,5},{8,10},{10,8},{9,1... | collective-permute-start | bytes 786440 | tf_op jit(solution)/shard_map/ppermute | solution.py:118
  43.1 10.5 %collective-permute-start.14 = (bf16[512,256]{1,0:T(8,128)(2,1)S(1)}, bf16[512,256]{1,0:T(8,128)(2,1)S(1)}, u32[]{:S(2)}, u32[]{:S(2)}) collective-permute-start(bf16[512,256]{1,0:T(8,128)(2,1)S(1)} %get-tuple-element.49.refs_0_), channel_id=1, source_target_pairs={{0,6},{2,4},{4,2},{6,0},{8,14},{10,12},{12,10},{14,8},{1,7},{3,5},... | collective-permute-start | bytes 786440 | tf_op jit(solution)/shard_map/ppermute | solution.py:118
  53.8 2.7 %collective-permute-start.15 = (bf16[4,512,256]{2,1,0:T(8,128)(2,1)S(1)}, bf16[4,512,256]{2,1,0:T(8,128)(2,1)S(1)}, u32[]{:S(2)}, u32[]{:S(2)}) collective-permute-start(bf16[4,512,256]{2,1,0:T(8,128)(2,1)S(1)} %pad_maximum_fusion.1), channel_id=1, source_target_pairs={{0,1},{1,0},{2,3},{3,2},{4,5},{5,4},{6,7},{7,6},{8,9},{9,8},{10,11... | collective-permute-start | bytes 3145736 | tf_op jit(solution)/shard_map/ppermute | solution.py:118
  53.9 9.8 %collective-permute-start.10 = (bf16[512,256]{1,0:T(8,128)(2,1)S(1)}, bf16[512,256]{1,0:T(8,128)(2,1)S(1)}, u32[]{:S(2)}, u32[]{:S(2)}) collective-permute-start(bf16[512,256]{1,0:T(8,128)(2,1)S(1)} %get-tuple-element.45), channel_id=1, source_target_pairs={{0,4},{4,0},{8,12},{12,8},{1,5},{5,1},{9,13},{13,9},{2,6},{6,2},{1... | collective-permute-start | bytes 786440 | tf_op jit(solution)/shard_map/ppermute | solution.py:118
  55.1 8.5 %collective-permute-start.11 = (bf16[512,256]{1,0:T(8,128)(2,1)S(1)}, bf16[512,256]{1,0:T(8,128)(2,1)S(1)}, u32[]{:S(2)}, u32[]{:S(2)}) collective-permute-start(bf16[512,256]{1,0:T(8,128)(2,1)S(1)} %get-tuple-element.45), channel_id=1, source_target_pairs={{0,2},{2,0},{1,3},{3,1},{4,6},{6,4},{5,7},{7,5},{8,10},{10,8},{9,1... | collective-permute-start | bytes 786440 | tf_op jit(solution)/shard_map/ppermute | solution.py:118
  59.0 26.6 %collective-permute-start.16 = (bf16[256,512]{1,0:T(8,128)(2,1)S(1)}, bf16[256,512]{1,0:T(8,128)(2,1)}, u32[]{:S(2)}, u32[]{:S(2)}) collective-permute-start(bf16[256,512]{1,0:T(8,128)(2,1)S(1)} %get-tuple-element.50), channel_id=1, source_target_pairs={{0,8},{4,12},{8,0},{12,4},{1,9},{5,13},{9,1},{13,5},{2,10},{6,14},... | collective-permute-start | bytes 786440 | tf_op jit(solution)/shard_map/ppermute | solution.py:123
  62.0 23.6 %collective-permute-start.17 = (bf16[256,512]{1,0:T(8,128)(2,1)S(1)}, bf16[256,512]{1,0:T(8,128)(2,1)}, u32[]{:S(2)}, u32[]{:S(2)}) collective-permute-start(bf16[256,512]{1,0:T(8,128)(2,1)S(1)} %get-tuple-element.52), channel_id=1, source_target_pairs={{0,12},{4,8},{8,4},{12,0},{1,13},{5,9},{9,5},{13,1},{2,14},{6,10},... | collective-permute-start | bytes 786440 | tf_op jit(solution)/shard_map/ppermute | solution.py:123
  63.7 8.1 %collective-permute-start = (bf16[512,256]{1,0:T(8,128)(2,1)S(1)}, bf16[512,256]{1,0:T(8,128)(2,1)S(1)}, u32[]{:S(2)}, u32[]{:S(2)}) collective-permute-start(bf16[512,256]{1,0:T(8,128)(2,1)S(1)} %get-tuple-element.20.refs_1_), channel_id=1, source_target_pairs={{0,2},{2,0},{1,3},{3,1},{4,6},{6,4},{5,7},{7,5},{8,10},{10,8},{9,1... | collective-permute-start | bytes 786440 | tf_op jit(solution)/shard_map/cond/branch_1_fun/ppermute | solution.py:118
  72.0 2.7 %collective-permute-start.1 = (bf16[4,512,256]{2,1,0:T(8,128)(2,1)S(1)}, bf16[4,512,256]{2,1,0:T(8,128)(2,1)S(1)}, u32[]{:S(2)}, u32[]{:S(2)}) collective-permute-start(bf16[4,512,256]{2,1,0:T(8,128)(2,1)S(1)} %pad_maximum_fusion), channel_id=1, source_target_pairs={{0,1},{1,0},{2,3},{3,2},{4,5},{5,4},{6,7},{7,6},{8,9},{9,8},{10,11... | collective-permute-start | bytes 3145736 | tf_op jit(solution)/shard_map/cond/branch_1_fun/ppermute | solution.py:118
  76.6 8.9 %collective-permute-start.2 = (bf16[256,512]{1,0:T(8,128)(2,1)S(1)}, bf16[256,512]{1,0:T(8,128)(2,1)S(1)}, u32[]{:S(2)}, u32[]{:S(2)}) collective-permute-start(bf16[256,512]{1,0:T(8,128)(2,1)S(1)} %branch_1_fun.3), channel_id=1, source_target_pairs={{0,4},{4,0},{8,12},{12,8},{1,5},{5,1},{9,13},{13,9},{2,6},{6,2},{1... | collective-permute-start | bytes 786440 | tf_op jit(solution)/shard_map/cond/branch_1_fun/ppermute | solution.py:123
